TPU v7x, 32 devices: a whole 2x2x4 slice. The times are simulated.
32 devices in a mesh: grp: 2 (over y), tp: 4 (over z), ffn: 4 (over x, core).
Axes of the slice: x: 2, y: 2, z: 4, core: 2. Of those that a mesh axis runs over, the one named last changes fastest.
Arguments:
- queries: bfloat16 [192, 8192], P('grp', 'tp'), may hold values from -320 to 320
- new_kv: bfloat16 [2, 192, 1024], P(None, 'grp', 'tp'), may hold values from -12 to 12
- kv_cache: bfloat16 [2, 2, 8192, 1024], P(None, 'grp', 'ffn', 'tp'), may hold values from -12 to 12
- lengths: int32 [2], P('grp'), may hold values from 1 to 96, as said below
- prefixes: int32 [2], P('grp'), may hold values from 0 to 8192, as said below
- resid: bfloat16 [192, 8192], P('grp', 'ffn'), may hold values from -0.29882812 to 0.29882812
- out_weight: bfloat16 [8192, 8192], P('tp', 'ffn'), may hold values from -0.0625 to 0.0625
- gain: bfloat16 [8192], P('ffn'), may hold values from 0.099609375 to 1.8984375
- gate_weight: bfloat16 [8192, 29568], P('ffn', ('grp', 'tp')), may hold values from -0.0625 to 0.0625
- up_weight: bfloat16 [8192, 29568], P('ffn', ('grp', 'tp')), may hold values from -0.0625 to 0.0625
- down_weight: bfloat16 [29568, 8192], P(('grp', 'tp'), 'ffn'), may hold values from -0.03125 to 0.03125
Outputs:
- layer_out: bfloat16 [192, 8192], P(('grp', 'tp'), 'ffn')
Inputs may be any that keep to these rules, and one draw needn't show every extreme that they name: `lengths`: some group has a full block of 96 live slots. `prefixes`: some group has all 8192 cached positions in use.
All inputs are finite; a program needn't handle non-finite values.
Results may differ from a plain program's by a relative error of at most 0.02.
Values may be sent and summed in bfloat16 or wider, within the bound.
No kernel may reach another device: no remote copies, remote signals or barrier semaphores. Data moves between devices by JAX's collectives and lax.ppermute only.
A program may use at most 128 MiB of HBM per device.

v0:
```python
import math

import jax
import jax.numpy as jnp
from jax import lax
from jax.sharding import PartitionSpec as P

D = 8192
DH = 128


negative = -1e30


def merged(x, axis, combine):
    everything = jax.tree.map(lambda part: lax.all_gather(part, axis), x)
    leading = jax.tree.map(lambda part: part[0], everything)

    def hop(k, so_far):
        return combine(so_far, jax.tree.map(lambda part: part[k], everything))

    return lax.fori_loop(1, lax.axis_size(axis), hop, leading)


def combine_parts(first, second):
    top = jnp.maximum(first[0], second[0])
    left = jnp.exp(first[0] - top)
    right = jnp.exp(second[0] - top)
    total = first[1] * left + second[1] * right
    values = first[2] * left[..., None] + second[2] * right[..., None]
    return (top, total, values)


def body(
    queries,
    new_kv,
    kv_cache,
    lengths,
    prefixes,
    resid,
    out_weight,
    gain,
    gate_weight,
    up_weight,
    down_weight,
):
    span, qcols = queries.shape
    kcols = new_kv.shape[2]
    local_kv = kcols // DH
    group = qcols // DH // local_kv
    cache_len = kv_cache.shape[2]
    length = lengths[0]
    prefix = prefixes[0]
    width_index = lax.axis_index("ffn")
    shard_start = width_index * cache_len
    query_heads = (
        queries.reshape(span, local_kv, group, DH)
        .transpose(1, 2, 0, 3)
        .reshape(local_kv, group * span, DH)
    )
    row_pos = jnp.tile(jnp.arange(span, dtype=jnp.int32), group)
    inv_scale = 1.0 / math.sqrt(DH)

    def update(state, keys, values, valid):
        top, total, acc = state
        scores = (
            jnp.einsum("hrd,hkd->hrk", query_heads, keys, preferred_element_type=jnp.float32)
            * inv_scale
        )
        scores = jnp.where(valid[None], scores, negative)
        new_top = jnp.maximum(top, jnp.max(scores, axis=-1))
        probs = jnp.where(valid[None], jnp.exp(scores - new_top[..., None]), 0.0)
        factor = jnp.exp(top - new_top)
        total = total * factor + jnp.sum(probs, axis=-1)
        acc = acc * factor[..., None] + jnp.einsum(
            "hrk,hkd->hrd", probs, values.astype(jnp.float32)
        )
        return (new_top, total, acc)

    block = math.gcd(512, cache_len)
    blocks = cache_len // block
    cache_keys = kv_cache[0, 0].reshape(blocks, block, local_kv, DH).transpose(0, 2, 1, 3)
    cache_values = kv_cache[1, 0].reshape(blocks, block, local_kv, DH).transpose(0, 2, 1, 3)
    rows = group * span
    start_state = (
        jnp.full((local_kv, rows), negative, jnp.float32),
        jnp.zeros((local_kv, rows), jnp.float32),
        jnp.zeros((local_kv, rows, DH), jnp.float32),
    )

    def cache_step(state, items):
        keys, values, index = items
        positions = shard_start + index * block + jnp.arange(block, dtype=jnp.int32)
        valid = jnp.broadcast_to((positions < prefix)[None, :], (rows, block))
        return (update(state, keys, values, valid), None)

    state, unused = lax.scan(
        cache_step, start_state, (cache_keys, cache_values, jnp.arange(blocks, dtype=jnp.int32))
    )
    block_keys = new_kv[0].reshape(span, local_kv, DH).transpose(1, 0, 2)
    block_values = new_kv[1].reshape(span, local_kv, DH).transpose(1, 0, 2)
    slots = jnp.arange(span, dtype=jnp.int32)[None, :]
    new_valid = (slots < length) & (slots <= row_pos[:, None]) & (width_index == 0)
    state = update(state, block_keys, block_values, new_valid)
    top, total, acc = merged(state, "ffn", combine_parts)
    heads = acc / total[..., None]
    attn = (
        heads.reshape(local_kv, group, span, DH)
        .transpose(2, 0, 1, 3)
        .reshape(span, qcols)
        .astype(jnp.bfloat16)
    )
    partial_value = jnp.dot(attn, out_weight, preferred_element_type=jnp.float32)
    summed = lax.psum(partial_value, "tp")
    h1 = (summed + resid.astype(jnp.float32)).astype(jnp.bfloat16)
    all_rows = lax.all_gather(h1, "grp", axis=0, tiled=True)
    rows_f = all_rows.astype(jnp.float32)
    squares = jnp.sum(rows_f * rows_f, axis=1)
    scaled = (rows_f * gain.astype(jnp.float32)[None, :]).astype(jnp.bfloat16)
    gate = jnp.dot(scaled, gate_weight, preferred_element_type=jnp.float32)
    upper = jnp.dot(scaled, up_weight, preferred_element_type=jnp.float32)
    rows_here = span // lax.axis_size("tp")
    gate, upper, squares = lax.psum((gate, upper, squares), "ffn")
    inv_rms = lax.rsqrt(squares / D + 1e-06)
    hidden = (jax.nn.silu(gate * inv_rms[:, None]) * (upper * inv_rms[:, None])).astype(
        jnp.bfloat16
    )
    down_rows = lax.psum_scatter(
        jnp.dot(hidden, down_weight, preferred_element_type=jnp.float32),
        ("grp", "tp"),
        scatter_dimension=0,
        tiled=True,
    )
    row_start = lax.axis_index("tp") * rows_here
    own = lax.dynamic_slice_in_dim(h1, row_start, rows_here, 0)
    live = row_start + jnp.arange(rows_here, dtype=jnp.int32) < length
    return jnp.where(live[:, None], own.astype(jnp.float32) + down_rows, 0.0).astype(jnp.bfloat16)


def solution(mesh):
    return jax.shard_map(
        body,
        mesh=mesh,
        in_specs=(
            P("grp", "tp"),
            P(None, "grp", "tp"),
            P(None, "grp", "ffn", "tp"),
            P("grp"),
            P("grp"),
            P("grp", "ffn"),
            P("tp", "ffn"),
            P("ffn"),
            P("ffn", ("grp", "tp")),
            P("ffn", ("grp", "tp")),
            P(("grp", "tp"), "ffn"),
        ),
        out_specs=P(("grp", "tp"), "ffn"),
        check_vma=False,
    )
```

profile of v0, /device:TPU:0, one launch (start us, length us, event | category | flops | bytes accessed | tf_op | source)
XLA Modules:
  0.0 361.4 jit_solution(1527593874091766841)
XLA Ops:
  7.2 0.6 iota_compare_fusion.1
  7.8 0.7 le.20
  8.4 0.8 fusion.50
  9.3 0.6 reshape_squeeze.15
  9.9 0.6 reshape_squeeze.14
  10.5 1.1 copy.31
  11.7 1.7 fusion.49
  14.0 24.6 %while.35 = (s32[]{:T(128)}, f32[2,768]{1,0:T(2,128)S(1)}, f32[2,768]{1,0:T(2,128)S(1)}, f32[2,768,128]{2,1,0:T(8,128)}, s32[4]{0:T(128)S(1)}, /*index=5*/s32[]{...) while((s32[]{:T(128)}, f32[2,768]{1,0:T(2,128)S(1)}, ...), condition=%wide.region_3.4_spmd.clone, body=%wide.region_0.3_spmd.clone.sunk | while | flops 412688896 | bytes 19368184 | solution.py:97
  15.2 0.7 add_compare_fusion.3
  16.2 0.6 bitcast_reduce_fusion.2
  16.9 0.9 fusion.71
  17.8 1.5 fusion.73
  19.3 0.9 copy-done.1
  21.3 0.7 add_compare_fusion.3
  22.4 0.6 bitcast_reduce_fusion.2
  23.0 0.9 fusion.71
  23.9 1.5 fusion.73
  25.5 0.9 copy-done.1
  27.4 0.7 add_compare_fusion.3
  28.5 0.6 bitcast_reduce_fusion.2
  29.1 0.9 fusion.71
  30.0 1.5 fusion.73
  31.6 0.9 copy-done.1
  33.6 0.7 add_compare_fusion.3
  34.6 0.6 bitcast_reduce_fusion.2
  35.3 0.9 fusion.71
  36.2 1.5 fusion.73
  37.7 0.9 copy-done.1
  39.2 2.5 convolution_add_fusion
  41.7 6.2 %all-gather.4 = f32[4,2,768]{2,1,0:T(2,128)S(1)} all-gather(f32[1,2,768]{2,1,0:T(2,128)S(1)} %get-tuple-element.336), channel_id=3, replica_groups=mesh['grp'=2,'tp'=4,'ffn'=4] {'ffn'}, dimensions={0}, use_global_device_ids=true | all-gather | bytes 30720 | tf_op jit(solution)/shard_map/all_gather | solution.py:16
  47.9 5.4 %all-gather.3 = f32[4,2,768]{2,1,0:T(2,128)S(1)} all-gather(f32[1,2,768]{2,1,0:T(2,128)S(1)} %bitcast.107), channel_id=2, replica_groups=mesh['grp'=2,'tp'=4,'ffn'=4] {'ffn'}, dimensions={0}, use_global_device_ids=true | all-gather | bytes 30720 | tf_op jit(solution)/shard_map/all_gather | solution.py:16
  53.3 19.7 %all-gather.7.cloned.1.call-done = f32[8,768,128]{2,1,0:T(8,128)} async-done(((f32[2,768,128]{2,1,0:T(8,128)}), f32[8,768,128]{2,1,0:T(8,128)}) %all-gather.7.cloned.1.call-update) | async-done | bytes 3145744 | tf_op jit(solution)/shard_map/all_gather | solution.py:16
  73.1 1.2 slice.35
  74.3 5.6 %while.34 = (s32[]{:T(128)}, f32[2,768]{1,0:T(2,128)S(1)}, f32[2,768]{1,0:T(2,128)S(1)}, f32[2,768,128]{2,1,0:T(8,128)S(1)}, f32[4,2,768]{2,1,0:T(2,128)S(1)}, /...) while((s32[]{:T(128)}, f32[2,768]{1,0:T(2,128)S(1)}, ...), condition=%wide.region_7.8_spmd, body=%wide.region_6.7_spmd.sunk | while | flops 599045 | bytes 2420879 | solution.py:22
  74.3 1.8 fusion.67
  76.2 1.8 fusion.67
  78.0 1.8 fusion.67
  80.3 5.8 %fusion.34 = f32[96,2048]{1,0:T(8,128)} fusion(bf16[2048,2048]{1,0:T(8,128)(2,1)} %param.21, bf16[12,8,16,128]{3,2,1,0:T(8,128)(2,1)S(1)} %bitcast.103), kind=kOutput, calls=%fused_computation.54 | convolution fusion | flops 805306368 | bytes 9568256 | tf_op jit(solution)/shard_map/dot_general | solution.py:113
  86.2 43.8 %all-reduce.4.cloned.1.call-done = f32[96,2048]{1,0:T(8,128)} async-done(((f32[96,2048]{1,0:T(8,128)}), f32[96,2048]{1,0:T(8,128)}) %all-reduce.4.cloned.1.call-update) | async-done | bytes 786448 | tf_op jit(solution)/shard_map/psum | solution.py:114
  130.0 1.2 add_convert_fusion
  131.2 11.6 %all_gather.27 = bf16[192,2048]{1,0:T(8,128)(2,1)S(1)} all-gather(bf16[96,2048]{1,0:T(8,128)(2,1)S(1)} %add_convert_fusion), channel_id=1, replica_groups=mesh['grp'=2,'tp'=4,'ffn'=4] {'grp'}, dimensions={0}, use_global_device_ids=true | all-gather | bytes 1179648 | tf_op jit(solution)/shard_map/all_gather | solution.py:116
  142.8 12.0 %fusion.29 = f32[192,3696]{1,0:T(8,128)} fusion(bf16[2048,3696]{0,1:T(8,128)(2,1)} %param.24, bf16[192,2048]{1,0:T(8,128)(2,1)S(1)} %all_gather.27, f32[2048]{0:T(1024)S(1)} %convert_element_type.46), kind=kOutput, calls=%fused_computation.50 | convolution fusion | flops 2907832320 | bytes 18771968 | tf_op jit(solution)/shard_map/dot_general | solution.py:121
  154.8 12.1 %fusion.31 = f32[192,3696]{1,0:T(8,128)} fusion(bf16[2048,3696]{0,1:T(8,128)(2,1)} %param.23, bf16[192,2048]{1,0:T(8,128)(2,1)S(1)} %all_gather.27, f32[2048]{0:T(1024)S(1)} %convert_element_type.46), kind=kOutput, calls=%fused_computation.51 | convolution fusion | flops 2907832320 | bytes 18771968 | tf_op jit(solution)/shard_map/dot_general | solution.py:120
  167.1 5.7 %psum.30 = f32[192]{0:T(256)S(1)} all-reduce(f32[192]{0:T(256)S(1)} %fusion.24), channel_id=1, replica_groups=mesh['grp'=2,'tp'=4,'ffn'=4] {'ffn'}, use_global_device_ids=true, to_apply=%region_11.12 | all-reduce | flops 192 | bytes 1536 | tf_op jit(solution)/shard_map/psum | solution.py:123
  172.8 103.5 %all-reduce.6.cloned.1.call-done = (f32[192,3696]{1,0:T(8,128)}, f32[192,3696]{1,0:T(8,128)}) async-done(((f32[192,3696]{1,0:T(8,128)}, f32[192,3696]{1,0:T(8,128)}), (f32[192,3696]{1,0:T(8,128)}, f32[192,3696]{1,0:T(8,128)})) %all-reduce.6.cloned.1.call-update) | async-done | bytes 5677072 | tf_op jit(solution)/shard_map/psum | solution.py:123
  276.3 11.7 %fusion.25 = f32[192,2048]{1,0:T(8,128)} fusion(bf16[3696,2048]{1,0:T(8,128)(2,1)} %param.25, f32[192,3696]{1,0:T(8,128)} %get-tuple-element.328, f32[192,3696]{1,0:T(8,128)} %get-tuple-element.329, f32[192]{0:T(256)S(1)} %add_rsqrt_fusion), kind=kOutput, calls=%fused_computation.42 | convolution fusion | flops 2912329728 | bytes 22389504 | tf_op jit(solution)/shard_map/dot_general | solution.py:129
  288.0 65.2 %reduce-scatter.2.cloned.1.call-done = f32[24,2048]{1,0:T(8,128)} async-done(((f32[192,2048]{1,0:T(8,128)}), f32[24,2048]{1,0:T(8,128)}) %reduce-scatter.2.cloned.1.call-update) | async-done | bytes 196624 | tf_op jit(solution)/shard_map/reduce_scatter | solution.py:128
  353.2 1.6 select_convert_fusion
  (76 shorter events, 6.1 us)
Async XLA Ops:
  6.5 66.5 %all-gather.7.cloned.1.call-start = ((), (), s32[]{:S(2)}) async-start(), calls=%async_computation.3 | async-start | bytes 3932160 | tf_op jit(solution)/shard_map/all_gather | solution.py:16
  14.0 24.6 %copy-start.5 = (s32[768]{0:T(1024)S(1)}, s32[768]{0:T(1024)}, u32[]{:S(2)}) copy-start(s32[768]{0:T(1024)} %le.20) | copy-start | bytes 9220
  14.0 24.6 %copy-start.7 = (pred[96]{0:T(512)(128)(4,1)S(1)}, pred[96]{0:T(512)(128)(4,1)}, u32[]{:S(2)}) copy-start(pred[96]{0:T(512)(128)(4,1)} %iota_compare_fusion.1) | copy-start | bytes 292
  14.0 24.7 %copy-start.3 = (bf16[96,2,128]{2,1,0:T(2,128)(2,1)S(1)}, bf16[96,2,128]{2,1,0:T(2,128)(2,1)}, u32[]{:S(2)}) copy-start(bf16[96,2,128]{2,1,0:T(2,128)(2,1)} %reshape_squeeze.14) | copy-start | bytes 147460
  14.0 25.2 %copy-start.4 = (bf16[96,2,128]{2,1,0:T(2,128)(2,1)S(1)}, bf16[96,2,128]{2,1,0:T(2,128)(2,1)}, u32[]{:S(2)}) copy-start(bf16[96,2,128]{2,1,0:T(2,128)(2,1)} %reshape_squeeze.15) | copy-start | bytes 147460
  16.2 1.6 copy-start
  19.3 0.9 copy-start.1
  22.3 1.6 copy-start
  25.4 0.9 copy-start.1
  28.5 1.6 copy-start
  31.6 0.9 copy-start.1
  34.6 1.6 copy-start
  37.7 0.9 copy-start.1
  41.7 88.3 %all-reduce.4.cloned.1.call-start = ((), (), s32[]{:S(2)}) async-start(), calls=%async_computation.1 | async-start | bytes 1572864 | tf_op jit(solution)/shard_map/psum | solution.py:114
  80.3 5.9 %copy-start.6 = (bf16[2048]{0:T(1024)(128)(2,1)S(1)}, bf16[2048]{0:T(1024)(128)(2,1)}, u32[]{:S(2)}) copy-start(bf16[2048]{0:T(1024)(128)(2,1)} %param.22) | copy-start | bytes 12292
  80.3 49.6 %copy-start.2 = (bf16[96,2048]{1,0:T(8,128)(2,1)S(1)}, bf16[96,2048]{1,0:T(8,128)(2,1)}, u32[]{:S(2)}) copy-start(bf16[96,2048]{1,0:T(8,128)(2,1)} %param.20) | copy-start | bytes 1179652
  86.1 190.2 %all-reduce.6.cloned.1.call-start = ((), (), s32[]{:S(2)}) async-start(), calls=%async_computation.4 | async-start | bytes 11403264 | tf_op jit(solution)/shard_map/psum | solution.py:123
  166.9 186.4 %reduce-scatter.2.cloned.1.call-start = ((), (), s32[]{:S(2)}) async-start(), calls=%async_computation.2 | async-start | bytes 1769472 | tf_op jit(solution)/shard_map/reduce_scatter | solution.py:128
Sparse Core Ops, SparseCore 0:
  41.8 31.2 all-gather.6
  86.2 43.6 all-reduce.3
  167.0 109.3 all-reduce.5
  288.1 65.0 reduce-scatter.1
where the time goes:
time: 362 us; the launch traced here: 361 us
  waiting for transfers between devices  232 us (64%)
  matrix products  52.8 us (15%)
  blocking collectives  28.9 us (8%)
  other arithmetic  16 us (4%)
  local copies, waits for them, and re-layouts  14.8 us (4%)
  between operations  14 us (4%)
    psum x1, waiting for transfers between devices, body(): gate, upper, squares = lax.psum((gate, upper, squares), 'ffn')  104 us
    reduce_scatter x1, waiting for transfers between devices, body(): lax.psum_scatter(jnp.dot(hidden, down_weight, preferred_element_type=jnp....  65.2 us
    psum x1, waiting for transfers between devices, body(): summed = lax.psum(partial_value, 'tp')  43.8 us
    all_gather x1, waiting for transfers between devices, merged(): everything = jax.tree.map(lambda part: lax.all_gather(part, axis), x)  19.7 us
    dot_general x1, matrix products, body(): gate = jnp.dot(scaled, gate_weight, preferred_element_type=jnp.float32)  12.1 us
    dot_general x1, matrix products, body(): upper = jnp.dot(scaled, up_weight, preferred_element_type=jnp.float32)  12 us
    dot_general x1, matrix products, body(): jnp.dot(hidden, down_weight, preferred_element_type=jnp.float32)  11.7 us
    all_gather x1, blocking collectives, body(): all_rows = lax.all_gather(h1, 'grp', axis=0, tiled=True)  11.6 us
  transfers between devices with their start and end apart: 4, of which 4 were waited for; matrix products, arithmetic and copies ran while one was open for 0% of the time, Pallas kernels for 0%

commit v1 on v0

--- a/solution.py
+++ b/solution.py
@@ -1,15 +1,500 @@
+import functools
 import math
 
 import jax
 import jax.numpy as jnp
 from jax import lax
+from jax.experimental import pallas as pl
+from jax.experimental.pallas import tpu as pltpu
 from jax.sharding import PartitionSpec as P
 
-D = 8192
 DH = 128
-
-
-negative = -1e30
+TILE = 256
+NEGATIVE = -1e30
+BF16 = jnp.bfloat16
+F32 = jnp.float32
+LIMIT = 50 * 1024 * 1024
+ORDER = (0, 2, 1, 3)
+
+
+def swapped_bits(index):
+    return (index & 1) * 2 + (index >> 1)
+
+
+def params(limit=LIMIT):
+    return pltpu.CompilerParams(vmem_limit_bytes=limit)
+
+
+def cost(flops, moved, exps=0):
+    return pl.CostEstimate(flops=int(flops), bytes_accessed=int(moved), transcendentals=int(exps))
+
+
+def whole(shape):
+    return pl.BlockSpec(shape, lambda *unused: (0,) * len(shape))
+
+
+def attention_kernel(heads, scalars, q_ref, key_ref, value_ref, new_key_ref, new_value_ref, out_ref, lse_ref, columns):
+    step = pl.program_id(0)
+    span = q_ref.shape[0]
+    cache_len = key_ref.shape[2]
+    usable, length, first = scalars[1], scalars[2], scalars[3]
+    scale = 1.0 / math.sqrt(DH)
+    q = jnp.concatenate([q_ref[:, h * DH : (h + 1) * DH] for h in range(heads)], axis=0)
+    contract = (((1,), (1,)), ((), ()))
+    scores = lax.dot_general(q, key_ref[0, 0], contract, preferred_element_type=F32)
+    position = lax.broadcasted_iota(jnp.int32, (1, cache_len), 1)
+    bias = jnp.where(position < usable, 0.0, NEGATIVE)
+    scores = scores * scale + bias
+    fresh = lax.dot_general(q, new_key_ref[0], contract, preferred_element_type=F32)
+    row = lax.broadcasted_iota(jnp.int32, (span, span), 0)
+    col = lax.broadcasted_iota(jnp.int32, (span, span), 1)
+    allowed = (col <= row) & (col < length) & (first > 0)
+    fresh_bias = jnp.where(allowed, 0.0, NEGATIVE)
+    fresh = fresh * scale + jnp.concatenate([fresh_bias] * heads, axis=0)
+    top = jnp.maximum(
+        jnp.max(scores, axis=1, keepdims=True), jnp.max(fresh, axis=1, keepdims=True)
+    )
+    probs = jnp.exp(scores - top)
+    fresh_probs = jnp.exp(fresh - top)
+    total = jnp.sum(probs, axis=1, keepdims=True) + jnp.sum(fresh_probs, axis=1, keepdims=True)
+    values = jnp.dot(probs.astype(BF16), value_ref[0, 0], preferred_element_type=F32)
+    values += jnp.dot(fresh_probs.astype(BF16), new_value_ref[0], preferred_element_type=F32)
+    values = (values / total).astype(BF16)
+    lse = top + jnp.log(total)
+    for h in range(heads):
+        out_ref[:, h * DH : (h + 1) * DH] = values[h * span : (h + 1) * span]
+
+    @pl.when(step == 0)
+    def first_step():
+        columns[...] = jnp.zeros_like(columns)
+
+    lane = lax.broadcasted_iota(jnp.int32, (span, 128), 1)
+    kept = columns[0:span, :]
+    for h in range(heads):
+        kept = jnp.where(lane == step * heads + h, lse[h * span : (h + 1) * span], kept)
+    columns[0:span, :] = kept
+
+    @pl.when(step == pl.num_programs(0) - 1)
+    def last_step():
+        lse_ref[...] = jnp.transpose(columns[...])[0 : lse_ref.shape[0], :]
+
+
+def attention(scalars, queries, kv_cache, new_kv, local_kv):
+    span, qcols = queries.shape
+    per_kv = qcols // DH // local_kv
+    heads = 4
+    steps = per_kv // heads
+    cache_len = kv_cache.shape[2]
+    width = heads * DH
+    call = pl.pallas_call(
+        functools.partial(attention_kernel, heads),
+        grid_spec=pltpu.PrefetchScalarGridSpec(
+            num_scalar_prefetch=1,
+            grid=(steps,),
+            in_specs=[
+                pl.BlockSpec((span, width), lambda i, s: (0, s[0] * steps + i)),
+                pl.BlockSpec((1, 1, cache_len, DH), lambda i, s: (0, 0, 0, s[0])),
+                pl.BlockSpec((1, 1, cache_len, DH), lambda i, s: (1, 0, 0, s[0])),
+                pl.BlockSpec((1, span, DH), lambda i, s: (0, 0, s[0])),
+                pl.BlockSpec((1, span, DH), lambda i, s: (1, 0, s[0])),
+            ],
+            out_specs=[
+                pl.BlockSpec((span, width), lambda i, s: (0, i)),
+                pl.BlockSpec((per_kv, 128), lambda i, s: (0, 0)),
+            ],
+            scratch_shapes=[pltpu.VMEM((128, 128), F32)],
+        ),
+        out_shape=[
+            jax.ShapeDtypeStruct((span, per_kv * DH), BF16),
+            jax.ShapeDtypeStruct((per_kv, 128), F32),
+        ],
+        compiler_params=params(60 * 1024 * 1024),
+        cost_estimate=cost(
+            4 * span * per_kv * cache_len * DH, 4 * cache_len * DH, span * per_kv * cache_len
+        ),
+    )
+    return call(scalars, queries, kv_cache, kv_cache, new_kv, new_kv)
+
+
+def combine_kernel(a_ref, b_ref, lse_a_ref, lse_b_ref, out_ref, lse_ref):
+    span = a_ref.shape[0]
+    heads = lse_a_ref.shape[0]
+    lse_a, lse_b = lse_a_ref[...], lse_b_ref[...]
+    top = jnp.maximum(lse_a, lse_b)
+    left, right = jnp.exp(lse_a - top), jnp.exp(lse_b - top)
+    total = left + right
+    lse_ref[...] = top + jnp.log(total)
+    rest = jnp.zeros((128 - 2 * heads, 128), F32)
+    table = jnp.transpose(jnp.concatenate([left / total, right / total, rest], axis=0))
+    for h in range(heads):
+        cols = slice(h * DH, (h + 1) * DH)
+        mixed = a_ref[:, cols].astype(F32) * table[0:span, h : h + 1]
+        mixed += b_ref[:, cols].astype(F32) * table[0:span, heads + h : heads + h + 1]
+        out_ref[:, cols] = mixed.astype(BF16)
+
+
+def combine(a, b, lse_a, lse_b):
+    return pl.pallas_call(
+        combine_kernel,
+        out_shape=[
+            jax.ShapeDtypeStruct(a.shape, BF16),
+            jax.ShapeDtypeStruct(lse_a.shape, F32),
+        ],
+        compiler_params=params(),
+        cost_estimate=cost(4 * a.size, 6 * a.size),
+    )(a, b, lse_a, lse_b)
+
+
+def project_kernel(scalars, keep_ref, other_ref, weight_ref, *rest):
+    outs, acc = rest[:-1], rest[-1]
+    step = pl.program_id(0)
+    depth = weight_ref.shape[0]
+    half = pl.num_programs(0) // 2
+    rows = outs[0].shape[0]
+
+    @pl.when(step < half)
+    def from_keep():
+        start = pl.multiple_of(step * depth, depth)
+        term = jnp.dot(keep_ref[:, pl.ds(start, depth)], weight_ref[...], preferred_element_type=F32)
+
+        @pl.when(step == 0)
+        def begin():
+            acc[...] = term
+
+        @pl.when(step > 0)
+        def go_on():
+            acc[...] += term
+
+    @pl.when(step >= half)
+    def from_other():
+        start = pl.multiple_of((step - half) * depth, depth)
+        acc[...] += jnp.dot(
+            other_ref[:, pl.ds(start, depth)], weight_ref[...], preferred_element_type=F32
+        )
+
+    @pl.when(step == pl.num_programs(0) - 1)
+    def finish():
+        for k, out in enumerate(outs):
+            start = pl.multiple_of((scalars[1] ^ k) * rows, 8)
+            out[...] = acc[pl.ds(start, rows), :].astype(out.dtype)
+
+
+def project(scalars, keep, other, out_weight, tp_size):
+    span, width = keep.shape
+    depth = 512
+    half = width // depth
+    cols = out_weight.shape[1]
+    rows = span // tp_size
+    return pl.pallas_call(
+        project_kernel,
+        grid_spec=pltpu.PrefetchScalarGridSpec(
+            num_scalar_prefetch=1,
+            grid=(2 * half,),
+            in_specs=[
+                whole((span, width)),
+                whole((span, width)),
+                pl.BlockSpec(
+                    (depth, cols),
+                    lambda i, s: (jnp.where(i < half, s[0], 1 - s[0]) * half + i % half, 0),
+                ),
+            ],
+            out_specs=[whole((rows, cols))] * tp_size,
+            scratch_shapes=[pltpu.VMEM((span, cols), F32)],
+        ),
+        out_shape=[
+            jax.ShapeDtypeStruct((rows, cols), F32 if k == 0 else BF16) for k in range(tp_size)
+        ],
+        compiler_params=params(),
+        cost_estimate=cost(4 * span * width * cols, 4 * width * cols),
+    )(scalars, keep, other, out_weight)
+
+
+def scale_kernel(slots, scalars, *refs):
+    count = 4 * slots
+    sources, gain_ref, scaled_ref, square_ref = refs[:count], refs[count], refs[count + 1], refs[count + 2]
+    gain = gain_ref[...].astype(F32)
+    cols = gain.shape[1]
+    for k in range(4):
+        place = swapped_bits(scalars[0] ^ k)
+        rows = jnp.concatenate(
+            [sources[k * slots + s][...].astype(F32) for s in range(slots)], axis=0
+        )
+        scaled_ref[place] = (rows * gain).astype(BF16)
+        squares = rows * rows
+        part = squares[:, 0:128]
+        for c in range(128, cols, 128):
+            part += squares[:, c : c + 128]
+        square_ref[place] = part
+
+
+def scale_rows(scalars, sources, gain):
+    slots = len(sources) // 4
+    rows, cols = sources[0].shape
+    high = rows * slots
+    return pl.pallas_call(
+        functools.partial(scale_kernel, slots),
+        grid_spec=pltpu.PrefetchScalarGridSpec(
+            num_scalar_prefetch=1,
+            grid=(1,),
+            in_specs=[whole((rows, cols))] * len(sources) + [whole((1, cols))],
+            out_specs=[whole((4, high, cols)), whole((4, high, 128))],
+        ),
+        out_shape=[
+            jax.ShapeDtypeStruct((4, high, cols), BF16),
+            jax.ShapeDtypeStruct((4, high, 128), F32),
+        ],
+        compiler_params=params(),
+        cost_estimate=cost(4 * 4 * high * cols, 4 * 4 * high * cols),
+    )(scalars, *sources, gain)
+
+
+def gate_up_kernel(scaled_ref, gate_ref, up_ref, keep_ref, cross_ref, send_ref):
+    places, high, depth = scaled_ref.shape
+    rows = scaled_ref[...].reshape(places * high, depth)
+    for which, weight in enumerate((gate_ref, up_ref)):
+        term = lax.dot_general(
+            rows, weight[...], (((1,), (1,)), ((), ())), preferred_element_type=F32
+        ).astype(BF16)
+        keep_ref[which] = term[0:high]
+        cross_ref[which] = term[high : 2 * high]
+        send_ref[0, which] = term[2 * high : 3 * high]
+        send_ref[1, which] = term[3 * high :]
+
+
+def gate_up(scaled, gate_weight, up_weight, begin, width):
+    places, high, depth = scaled.shape
+    tiles = pl.cdiv(width, TILE)
+    first = begin // TILE
+    weight = pl.BlockSpec((TILE, depth), lambda j: (first + j, 0))
+    piece = pl.BlockSpec((2, high, TILE), lambda j: (0, 0, j))
+    return pl.pallas_call(
+        gate_up_kernel,
+        grid=(tiles,),
+        in_specs=[whole(scaled.shape), weight, weight],
+        out_specs=[piece, piece, pl.BlockSpec((2, 2, high, TILE), lambda j: (0, 0, 0, j))],
+        out_shape=[
+            jax.ShapeDtypeStruct((2, high, width), BF16),
+            jax.ShapeDtypeStruct((2, high, width), BF16),
+            jax.ShapeDtypeStruct((2, 2, high, width), BF16),
+        ],
+        compiler_params=params(),
+        cost_estimate=cost(4 * places * high * depth * width, 4 * depth * width),
+    )(scaled, gate_weight, up_weight)
+
+
+def down_kernel(width, slots, has_start, last, scalars, *refs):
+    hidden = refs[0:4]
+    weight_ref = refs[4]
+    rest = list(refs[5:])
+    start_ref = rest.pop(0) if has_start else None
+    acc, packed = rest[-2], rest[-1]
+    outs = rest[:-2]
+    step = pl.program_id(0)
+    depth = weight_ref.shape[0]
+    high = hidden[0].shape[0]
+    steps = pl.num_programs(0)
+
+    @pl.when(step == 0)
+    def begin():
+        if width % depth:
+            packed[...] = jnp.zeros_like(packed)
+        for place in range(4):
+            packed[place * high : (place + 1) * high, 0:width] = hidden[place][...]
+        if has_start:
+            acc[...] = start_ref[...]
+        else:
+            acc[...] = jnp.zeros_like(acc)
+
+    start = pl.multiple_of(step * depth, depth)
+
+    def add(weight):
+        term = jnp.dot(packed[:, pl.ds(start, depth)], weight, preferred_element_type=F32)
+        acc[...] += term.reshape(acc.shape)
+
+    if width % depth:
+
+        @pl.when(step < steps - 1)
+        def inner():
+            add(weight_ref[...])
+
+        @pl.when(step == steps - 1)
+        def edge():
+            row = lax.broadcasted_iota(jnp.int32, weight_ref.shape, 0)
+            add(jnp.where(row < width % depth, weight_ref[...], jnp.zeros_like(weight_ref)))
+    else:
+        add(weight_ref[...])
+
+    @pl.when(step == steps - 1)
+    def finish():
+        if not last:
+            outs[0][...] = acc[...]
+            return
+        rows = high // slots
+        for k in range(4):
+            place = swapped_bits(scalars[0] ^ k)
+            block = acc[place]
+            for s in range(slots):
+                out = outs[k * slots + s]
+                out[...] = block[s * rows : (s + 1) * rows].astype(out.dtype)
+
+
+def down(scalars, hidden, down_weight, begin, start, slots, last):
+    high, width = hidden[0].shape
+    cols = down_weight.shape[1]
+    steps = pl.cdiv(width, TILE)
+    first = begin // TILE
+    rows = high // slots
+    ins = [whole((high, width))] * 4 + [pl.BlockSpec((TILE, cols), lambda i, s: (first + i, 0))]
+    args = list(hidden) + [down_weight]
+    if start is not None:
+        ins.append(whole((4, high, cols)))
+        args.append(start)
+    if last:
+        shapes = [
+            jax.ShapeDtypeStruct((rows, cols), F32 if s == 0 else BF16)
+            for k in range(4)
+            for s in range(slots)
+        ]
+    else:
+        shapes = [jax.ShapeDtypeStruct((4, high, cols), F32)]
+    return pl.pallas_call(
+        functools.partial(down_kernel, width, slots, start is not None, last),
+        grid_spec=pltpu.PrefetchScalarGridSpec(
+            num_scalar_prefetch=1,
+            grid=(steps,),
+            in_specs=ins,
+            out_specs=[whole(shape.shape) for shape in shapes],
+            scratch_shapes=[
+                pltpu.VMEM((4, high, cols), F32),
+                pltpu.VMEM((4 * high, steps * TILE), BF16),
+            ],
+        ),
+        out_shape=shapes,
+        compiler_params=params(),
+        cost_estimate=cost(8 * high * width * cols, 2 * width * cols),
+    )(scalars, *args)
+
+
+def to_core(x):
+    return lax.ppermute(x, "ffn", [(i, i ^ 1) for i in range(4)])
+
+
+def to_x(x):
+    return lax.ppermute(x, "ffn", [(i, i ^ 2) for i in range(4)])
+
+
+def to_z(x, k):
+    return lax.ppermute(x, "tp", [(i, i ^ k) for i in range(4)])
+
+
+def to_y(x):
+    return lax.ppermute(x, "grp", [(0, 1), (1, 0)])
+
+
+def cut(total):
+    tiles = -(-total // TILE)
+    head = (tiles + 1) // 2 * TILE
+    return [(0, head), (head, total - head)]
+
+
+def body(
+    queries,
+    new_kv,
+    kv_cache,
+    lengths,
+    prefixes,
+    resid,
+    out_weight,
+    gain,
+    gate_weight,
+    up_weight,
+    down_weight,
+):
+    span = queries.shape[0]
+    local_kv = new_kv.shape[2] // DH
+    cache_len = kv_cache.shape[2]
+    groups = lax.axis_size("grp")
+    tp_size = lax.axis_size("tp")
+    g, t, f = lax.axis_index("grp"), lax.axis_index("tp"), lax.axis_index("ffn")
+    core = f & 1
+    length = lengths[0]
+    rows = span // tp_size
+    model = gain.shape[0] * lax.axis_size("ffn")
+    usable = jnp.clip(prefixes[0] - f * cache_len, 0, cache_len)
+    first = (f == 0).astype(jnp.int32)
+
+    def attend(which):
+        scalars = jnp.stack([which, usable, length, first]).astype(jnp.int32)
+        return attention(scalars, queries, kv_cache, new_kv, local_kv)
+
+    sent, sent_lse = attend(1 - core)
+    got, got_lse = to_core(sent), to_core(sent_lse)
+    kept, kept_lse = attend(core)
+    kept, kept_lse = combine(kept, got, kept_lse, got_lse)
+    got, got_lse = to_x(kept), to_x(kept_lse)
+    mine, unused = combine(kept, got, kept_lse, got_lse)
+    other = to_core(mine)
+
+    order = jnp.stack([core, t]).astype(jnp.int32)
+    terms = project(order, mine, other, out_weight, tp_size)
+    own_resid = lax.dynamic_slice_in_dim(resid, t * rows, rows, 0).astype(F32)
+    summed = terms[0] + own_resid
+    for k in (1, 3, 2):
+        summed += to_z(terms[k], k).astype(F32)
+    h1 = summed.astype(BF16)
+
+    turn = jnp.stack([t ^ f]).astype(jnp.int32)
+    natural = g ^ jnp.arange(groups, dtype=jnp.int32)
+    by_z = [h1, to_z(h1, 1), to_z(h1, 2), to_z(h1, 3)]
+    sources = []
+    for part in by_z:
+        if groups == 2:
+            sources += [part, to_y(part)]
+        else:
+            everyone = jnp.take(lax.all_gather(part, "grp"), natural, axis=0)
+            sources += [everyone[s] for s in range(groups)]
+    scaled, squares = scale_rows(turn, sources, gain[None, :])
+
+    pair = squares[0:2] + to_core(squares[2:4])
+    own_squares = pair[0] + to_x(pair[1])
+    inv_rms = lax.rsqrt(jnp.sum(own_squares, axis=1, keepdims=True) / model + 1e-06)
+
+    chunks = cut(gate_weight.shape[1])
+    total = None
+    parts = [gate_up(scaled, gate_weight.T, up_weight.T, begin, width) for begin, width in chunks]
+    for index, (begin, width) in enumerate(chunks):
+        keep, cross, send = parts[index]
+        got = to_core(send)
+        crossed = to_x((cross.astype(F32) + got[1].astype(F32)).astype(BF16))
+        both = (keep.astype(F32) + got[0].astype(F32) + crossed.astype(F32)) * inv_rms
+        hidden = (jax.nn.silu(both[0]) * both[1]).astype(BF16)
+        over = to_x(hidden)
+        pieces = [hidden, over, to_core(hidden), to_core(over)]
+        is_last = index == len(chunks) - 1
+        result = down(turn, pieces, down_weight, begin, total, groups, is_last)
+        total = None if is_last else result[0]
+
+    chunk_sums = []
+    for k in range(4):
+        own = result[k * groups]
+        others = result[k * groups + 1 : (k + 1) * groups]
+        if groups == 2:
+            chunk_sums.append((own, others[0]))
+        else:
+            stacked = jnp.stack([own.astype(BF16)] + list(others))
+            stacked = jnp.take(stacked, natural, axis=0)
+            moved = lax.all_to_all(stacked, "grp", split_axis=0, concat_axis=0, tiled=True)
+            chunk_sums.append(jnp.sum(moved.astype(F32), axis=0))
+    out = h1.astype(F32)
+    for k in (3, 2, 1, 0):
+        if groups == 2:
+            own, away = chunk_sums[k]
+            value = own + to_y(away).astype(F32)
+        else:
+            value = chunk_sums[k]
+        out += value if k == 0 else to_z(value.astype(BF16), k).astype(F32)
+    live = t * rows + jnp.arange(rows, dtype=jnp.int32) < length
+    return jnp.where(live[:, None], out, 0.0).astype(BF16)
 
 
 def merged(x, axis, combine):
@@ -31,7 +516,7 @@
     return (top, total, values)
 
 
-def body(
+def general_body(
     queries,
     new_kv,
     kv_cache,
@@ -50,6 +535,7 @@
     group = qcols // DH // local_kv
     cache_len = kv_cache.shape[2]
     length = lengths[0]
+    model = gain.shape[0] * lax.axis_size("ffn")
     prefix = prefixes[0]
     width_index = lax.axis_index("ffn")
     shard_start = width_index * cache_len
@@ -67,7 +553,7 @@
             jnp.einsum("hrd,hkd->hrk", query_heads, keys, preferred_element_type=jnp.float32)
             * inv_scale
         )
-        scores = jnp.where(valid[None], scores, negative)
+        scores = jnp.where(valid[None], scores, NEGATIVE)
         new_top = jnp.maximum(top, jnp.max(scores, axis=-1))
         probs = jnp.where(valid[None], jnp.exp(scores - new_top[..., None]), 0.0)
         factor = jnp.exp(top - new_top)
@@ -83,7 +569,7 @@
     cache_values = kv_cache[1, 0].reshape(blocks, block, local_kv, DH).transpose(0, 2, 1, 3)
     rows = group * span
     start_state = (
-        jnp.full((local_kv, rows), negative, jnp.float32),
+        jnp.full((local_kv, rows), NEGATIVE, jnp.float32),
         jnp.zeros((local_kv, rows), jnp.float32),
         jnp.zeros((local_kv, rows, DH), jnp.float32),
     )
@@ -121,7 +607,7 @@
     upper = jnp.dot(scaled, up_weight, preferred_element_type=jnp.float32)
     rows_here = span // lax.axis_size("tp")
     gate, upper, squares = lax.psum((gate, upper, squares), "ffn")
-    inv_rms = lax.rsqrt(squares / D + 1e-06)
+    inv_rms = lax.rsqrt(squares / model + 1e-06)
     hidden = (jax.nn.silu(gate * inv_rms[:, None]) * (upper * inv_rms[:, None])).astype(
         jnp.bfloat16
     )
@@ -138,8 +624,9 @@
 
 
 def solution(mesh):
+    sizes = tuple(mesh.shape[axis] for axis in ("grp", "tp", "ffn"))
     return jax.shard_map(
-        body,
+        body if sizes == (2, 4, 4) else general_body,
         mesh=mesh,
         in_specs=(
             P("grp", "tp"),

time: 362 us -> 153 us (0.42)
  waiting for transfers between devices: 232 us -> 59 us
  Pallas kernels: 0 us -> 56.6 us
  matrix products: 52.8 us -> 0 us
  starting transfers between devices: 0.13 us -> 29.6 us
  blocking collectives: 28.9 us -> 0 us
  local copies, waits for them, and re-layouts: 14.8 us -> 1.63 us
  between operations: 14 us -> 1.56 us
  other arithmetic: 16 us -> 3.93 us
    psum x2 -> x0, waiting for transfers between devices: 147 us -> none  [the longest x1 104 us: body(): gate, upper, squares = lax.psum((gate, upper, squares), 'ffn')]
    reduce_scatter x1 -> x0, waiting for transfers between devices: 65.2 us -> none  [body(): lax.psum_scatter(jnp.dot(hidden, down_weight, preferred_element_type=jnp....]
    ppermute x0 -> x34, waiting for transfers between devices: none -> 59 us  [the longest x7 29.9 us: to_x(): return lax.ppermute(x, 'ffn', [(i, i ^ 2) for i in range(4)])]
    pallas_call x0 -> x10, Pallas kernels: none -> 56.6 us  [the longest x2 20.6 us: gate_up(): pl.pallas_call(gate_up_kernel, grid=(tiles,), in_specs=[whole(scaled.shap...]
    dot_general x14 -> x0, matrix products: 52.8 us -> none  [the longest x1 12.1 us: body(): gate = jnp.dot(scaled, gate_weight, preferred_element_type=jnp.float32)]
    ppermute x0 -> x34, starting transfers between devices: none -> 29.6 us  [the longest x9 11.9 us: to_z(): return lax.ppermute(x, 'tp', [(i, i ^ k) for i in range(4)])]
    all_gather x3 -> x0, blocking collectives: 23.2 us -> none  [the longest x1 11.6 us: body(): all_rows = lax.all_gather(h1, 'grp', axis=0, tiled=True)]
    all_gather x1 -> x0, waiting for transfers between devices: 19.7 us -> none  [merged(): everything = jax.tree.map(lambda part: lax.all_gather(part, axis), x)]
  transfers between devices with their start and end apart: 4 -> 34, of which waited for: 4 -> 20; matrix products, arithmetic and copies ran while one was open for 0% -> 1% of each run, Pallas kernels for 0% -> 23%
where the time goes in v1:
time: 153 us; the launch traced here: 152 us
  waiting for transfers between devices  59 us (39%)
  Pallas kernels  56.6 us (37%)
  starting transfers between devices  29.6 us (19%)
  other arithmetic  3.93 us (3%)
  local copies, waits for them, and re-layouts  1.63 us (1%)
  between operations  1.56 us (1%)
    ppermute x7, waiting for transfers between devices, to_x(): return lax.ppermute(x, 'ffn', [(i, i ^ 2) for i in range(4)])  29.9 us
    pallas_call x2, Pallas kernels, gate_up(): pl.pallas_call(gate_up_kernel, grid=(tiles,), in_specs=[whole(scaled.shap...  20.6 us
    ppermute x9, waiting for transfers between devices, to_z(): return lax.ppermute(x, 'tp', [(i, i ^ k) for i in range(4)])  17.4 us
    pallas_call x2, Pallas kernels, attention(): return call(scalars, queries, kv_cache, kv_cache, new_kv, new_kv)  14.7 us
    pallas_call x2, Pallas kernels, down(): pl.pallas_call(functools.partial(down_kernel, width, slots, start is not...  14 us
    ppermute x9, starting transfers between devices, to_z(): return lax.ppermute(x, 'tp', [(i, i ^ k) for i in range(4)])  11.9 us
    ppermute x8, waiting for transfers between devices, to_y(): return lax.ppermute(x, 'grp', [(0, 1), (1, 0)])  9.22 us
    ppermute x8, starting transfers between devices, to_y(): return lax.ppermute(x, 'grp', [(0, 1), (1, 0)])  9.18 us
  transfers between devices with their start and end apart: 34, of which 20 were waited for; matrix products, arithmetic and copies ran while one was open for 1% of the time, Pallas kernels for 23%

profile of v1, /device:TPU:0, one launch (start us, length us, event | category | flops | bytes accessed | tf_op | source)
XLA Modules:
  0.0 152.4 jit_solution(14719361181644629881)
XLA Ops:
  1.3 0.7 add_add_fusion.1.scalars
  2.0 7.3 %shard_map.110 = (bf16[96,1024]{1,0:T(8,128)(2,1)}, f32[8,128]{1,0:T(8,128)}) custom-call(s32[4]{0:T(128)} %add_add_fusion.1.scalars, bf16[96,2048]{1,0:T(8,128)(2,1)} %q_ref.3, bf16[2,1,2048,256]{3,2,1,0:T(8,128)(2,1)} %value_ref.3, bf16[2,1,2048,256]{3,2,1,0:T(8,128)(2,1)} %value_ref.3, bf16[2,96,256]{2,1,0:T(8,128)(2,1)} %new_value_ref.3, ...), custom_call_target="tpu_custom_call" | custom-call | flops 805306368 | bytes 1048576 | tf_op jit(solution)/shard_map/pallas_call | solution.py:116
  9.8 0.6 add_add_fusion.scalars
  10.4 7.3 %shard_map.109 = (bf16[96,1024]{1,0:T(8,128)(2,1)}, f32[8,128]{1,0:T(8,128)}) custom-call(s32[4]{0:T(128)} %add_add_fusion.scalars, bf16[96,2048]{1,0:T(8,128)(2,1)} %q_ref.3, bf16[2,1,2048,256]{3,2,1,0:T(8,128)(2,1)} %value_ref.3, bf16[2,1,2048,256]{3,2,1,0:T(8,128)(2,1)} %value_ref.3, bf16[2,96,256]{2,1,0:T(8,128)(2,1)} %new_value_ref.3, ...), custom_call_target="tpu_custom_call" | custom-call | flops 805306368 | bytes 1048576 | tf_op jit(solution)/shard_map/pallas_call | solution.py:116
  17.8 0.9 copy-done
  18.7 0.7 copy-done.1
  19.8 3.0 %collective-permute-start.2 = (bf16[96,1024]{1,0:T(8,128)(2,1)S(1)}, bf16[96,1024]{1,0:T(8,128)(2,1)S(1)}, u32[]{:S(2)}, u32[]{:S(2)}) collective-permute-start(bf16[96,1024]{1,0:T(8,128)(2,1)S(1)} %get-tuple-element.36.a_ref), channel_id=1, source_target_pairs={{0,2},{1,3},{2,0},{3,1},{4,6},{5,7},{6,4},{7,5},{8,10},{9,11},{10,... | collective-permute-start | bytes 589832 | tf_op jit(solution)/shard_map/ppermute | solution.py:383
  22.9 5.1 %collective-permute-done.3.lse_b_ref = f32[8,128]{1,0:T(8,128)S(1)} collective-permute-done((f32[8,128]{1,0:T(8,128)S(1)}, f32[8,128]{1,0:T(8,128)S(1)}, u32[]{:S(2)}, u32[]{:S(2)}) %collective-permute-start.3) | collective-permute-done | bytes 4128 | tf_op jit(solution)/shard_map/ppermute | solution.py:383
  28.0 0.9 shard_map.112
  29.1 1.4 collective-permute-done.4.other_ref
  30.4 5.6 %shard_map.113 = (f32[24,2048]{1,0:T(8,128)S(1)}, bf16[24,2048]{1,0:T(8,128)(2,1)S(1)}, bf16[24,2048]{1,0:T(8,128)(2,1)S(1)}, bf16[24,2048]{1,0:T(8,128)(2,1)S(1)}) custom-call(s32[2]{0:T(128)S(1)} %pad_add_fusion.scalars, bf16[96,1024]{1,0:T(8,128)(2,1)S(1)} %get-tuple-element.38.keep_ref, bf16[96,1024]{1,0:T(8,128)(2,1)S(1)} %collective-permute-done.4.other_ref, ...), custom_call_target="tpu_custom_call" | custom-call | flops 805306368 | bytes 8388608 | tf_op jit(solution)/shard_map/pallas_call | solution.py:188
  36.1 1.9 %collective-permute-start.5 = (bf16[24,2048]{1,0:T(8,128)(2,1)S(1)}, bf16[24,2048]{1,0:T(8,128)(2,1)S(1)}, u32[]{:S(2)}, u32[]{:S(2)}) collective-permute-start(bf16[24,2048]{1,0:T(8,128)(2,1)S(1)} %get-tuple-element.40), channel_id=1, source_target_pairs={{0,4},{4,0},{8,12},{12,8},{1,5},{5,1},{9,13},{13,9},{2,6},{6,2},{1... | collective-permute-start | bytes 294920 | tf_op jit(solution)/shard_map/ppermute | solution.py:387
  38.0 2.5 %collective-permute-start.6 = (bf16[24,2048]{1,0:T(8,128)(2,1)S(1)}, bf16[24,2048]{1,0:T(8,128)(2,1)S(1)}, u32[]{:S(2)}, u32[]{:S(2)}) collective-permute-start(bf16[24,2048]{1,0:T(8,128)(2,1)S(1)} %get-tuple-element.41), channel_id=1, source_target_pairs={{0,12},{4,8},{8,4},{12,0},{1,13},{5,9},{9,5},{13,1},{2,14},{6,10},... | collective-permute-start | bytes 294920 | tf_op jit(solution)/shard_map/ppermute | solution.py:387
  41.1 5.2 %collective-permute-done.6 = bf16[24,2048]{1,0:T(8,128)(2,1)S(1)} collective-permute-done((bf16[24,2048]{1,0:T(8,128)(2,1)S(1)}, bf16[24,2048]{1,0:T(8,128)(2,1)S(1)}, u32[]{:S(2)}, u32[]{:S(2)}) %collective-permute-start.6) | collective-permute-done | bytes 98336 | tf_op jit(solution)/shard_map/ppermute | solution.py:387
  46.3 3.4 %collective-permute-done.7 = bf16[24,2048]{1,0:T(8,128)(2,1)S(1)} collective-permute-done((bf16[24,2048]{1,0:T(8,128)(2,1)S(1)}, bf16[24,2048]{1,0:T(8,128)(2,1)S(1)}, u32[]{:S(2)}, u32[]{:S(2)}) %collective-permute-start.7) | collective-permute-done | bytes 98336 | tf_op jit(solution)/shard_map/ppermute | solution.py:387
  49.7 1.0 add_convert_fusion.3.refs_0_
  50.6 2.7 %collective-permute-start.13 = (bf16[24,2048]{1,0:T(8,128)(2,1)S(1)}, bf16[24,2048]{1,0:T(8,128)(2,1)S(1)}, u32[]{:S(2)}, u32[]{:S(2)}) collective-permute-start(bf16[24,2048]{1,0:T(8,128)(2,1)S(1)} %add_convert_fusion.3.refs_0_), channel_id=1, source_target_pairs={{0,12},{4,8},{8,4},{12,0},{1,13},{5,9},{9,5},{13,1},{2,14},{6,10},... | collective-permute-start | bytes 294920 | tf_op jit(solution)/shard_map/ppermute | solution.py:387
  53.4 1.7 %collective-permute-start.9 = (bf16[24,2048]{1,0:T(8,128)(2,1)S(1)}, bf16[24,2048]{1,0:T(8,128)(2,1)S(1)}, u32[]{:S(2)}, u32[]{:S(2)}) collective-permute-start(bf16[24,2048]{1,0:T(8,128)(2,1)S(1)} %add_convert_fusion.3.refs_0_), channel_id=1, source_target_pairs={{0,4},{4,0},{8,12},{12,8},{1,5},{5,1},{9,13},{13,9},{2,6},{6,2},{1... | collective-permute-start | bytes 294920 | tf_op jit(solution)/shard_map/ppermute | solution.py:387
  55.1 1.5 collective-permute-start.8
  56.6 1.6 %collective-permute-done.13.refs_6_ = bf16[24,2048]{1,0:T(8,128)(2,1)S(1)} collective-permute-done((bf16[24,2048]{1,0:T(8,128)(2,1)S(1)}, bf16[24,2048]{1,0:T(8,128)(2,1)S(1)}, u32[]{:S(2)}, u32[]{:S(2)}) %collective-permute-start.13) | collective-permute-done | bytes 98336 | tf_op jit(solution)/shard_map/ppermute | solution.py:387
  58.3 1.5 collective-permute-start.14
  59.8 1.4 collective-permute-done.11.refs_4_
  61.2 1.5 collective-permute-start.12
  63.3 3.5 %collective-permute-done.12.refs_5_ = bf16[24,2048]{1,0:T(8,128)(2,1)S(1)} collective-permute-done((bf16[24,2048]{1,0:T(8,128)(2,1)S(1)}, bf16[24,2048]{1,0:T(8,128)(2,1)S(1)}, u32[]{:S(2)}, u32[]{:S(2)}) %collective-permute-start.12) | collective-permute-done | bytes 98336 | tf_op jit(solution)/shard_map/ppermute | solution.py:391
  66.8 1.2 collective-permute-done.10.refs_3_
  68.5 11.0 %shard_map.116 = (bf16[2,48,2048]{2,1,0:T(8,128)(2,1)S(1)}, bf16[2,48,2048]{2,1,0:T(8,128)(2,1)S(1)}, bf16[2,2,48,2048]{3,2,1,0:T(8,128)(2,1)S(1)}) custom-call(bf16[4,48,2048]{2,1,0:T(8,128)(2,1)S(1)} %get-tuple-element.43.scaled_ref, bf16[3696,2048]{1,0:T(8,128)(2,1)} %bitcast.60, bf16[3696,2048]{1,0:T(8,128)(2,1)} %bitcast.62), custom_call_target="tpu_custom_call" | custom-call | flops 3221225472 | bytes 16777216 | tf_op jit(solution)/shard_map/pallas_call | solution.py:270
  80.0 1.6 %collective-permute-start.18 = (f32[48,128]{1,0:T(8,128)S(1)}, f32[48,128]{1,0:T(8,128)S(1)}, u32[]{:S(2)}, u32[]{:S(2)}) collective-permute-start(f32[48,128]{1,0:T(8,128)S(1)} %slice_bitcast_fusion.8), channel_id=1, source_target_pairs={{0,2},{1,3},{2,0},{3,1},{4,6},{5,7},{6,4},{7,5},{8,10},{9,11},{10,... | collective-permute-start | bytes 73736 | tf_op jit(solution)/shard_map/ppermute | solution.py:383
  81.5 9.7 %shard_map.115 = (bf16[2,48,1648]{2,1,0:T(8,128)(2,1)S(1)}, bf16[2,48,1648]{2,1,0:T(8,128)(2,1)S(1)}, bf16[2,2,48,1648]{3,2,1,0:T(8,128)(2,1)S(1)}) custom-call(bf16[4,48,2048]{2,1,0:T(8,128)(2,1)S(1)} %get-tuple-element.43.scaled_ref, bf16[3696,2048]{1,0:T(8,128)(2,1)} %bitcast.61, bf16[3696,2048]{1,0:T(8,128)(2,1)} %bitcast.63), custom_call_target="tpu_custom_call" | custom-call | flops 2592079872 | bytes 13500416 | tf_op jit(solution)/shard_map/pallas_call | solution.py:270
  91.6 0.6 collective-permute-start.23
  92.2 1.2 collective-permute-done.15
  93.5 0.6 collective-permute-start.16
  94.1 9.5 %collective-permute-done.23 = bf16[2,48,2048]{2,1,0:T(8,128)(2,1)S(1)} collective-permute-done((bf16[2,48,2048]{2,1,0:T(8,128)(2,1)S(1)}, bf16[2,48,2048]{2,1,0:T(8,128)(2,1)S(1)}, u32[]{:S(2)}, u32[]{:S(2)}) %collective-permute-start.23) | collective-permute-done | bytes 393248 | tf_op jit(solution)/shard_map/ppermute | solution.py:383
  104.5 5.9 %collective-permute-done.16 = bf16[2,48,1648]{2,1,0:T(8,128)(2,1)S(1)} collective-permute-done((bf16[2,48,1648]{2,1,0:T(8,128)(2,1)S(1)}, bf16[2,48,1648]{2,1,0:T(8,128)(2,1)S(1)}, u32[]{:S(2)}, u32[]{:S(2)}) %collective-permute-start.16) | collective-permute-done | bytes 316448 | tf_op jit(solution)/shard_map/ppermute | solution.py:383
  110.6 3.6 %collective-permute-done.24.refs_1_ = bf16[48,2048]{1,0:T(8,128)(2,1)S(1)} collective-permute-done((bf16[48,2048]{1,0:T(8,128)(2,1)S(1)}, bf16[48,2048]{1,0:T(8,128)(2,1)S(1)}, u32[]{:S(2)}, u32[]{:S(2)}) %collective-permute-start.24) | collective-permute-done | bytes 196640 | tf_op jit(solution)/shard_map/ppermute | solution.py:383
  115.1 5.8 %collective-permute-done.19.refs_1_ = bf16[48,1648]{1,0:T(8,128)(2,1)S(1)} collective-permute-done((bf16[48,1648]{1,0:T(8,128)(2,1)S(1)}, bf16[48,1648]{1,0:T(8,128)(2,1)S(1)}, u32[]{:S(2)}, u32[]{:S(2)}) %collective-permute-start.19) | collective-permute-done | bytes 158240 | tf_op jit(solution)/shard_map/ppermute | solution.py:383
  120.9 7.4 %shard_map.117.refs_5_ = f32[4,48,2048]{2,1,0:T(8,128)S(1)} custom-call(s32[1]{0:T(128)} %bitcast.7.scalars, bf16[48,2048]{1,0:T(8,128)(2,1)S(1)} %fusion.7.refs_0_, bf16[48,2048]{1,0:T(8,128)(2,1)S(1)} %collective-permute-done.24.refs_1_, bf16[48,2048]{1,0:T(8,128)(2,1)S(1)} %collective-permute-done.25.refs_2_, ...), custom_call_target="tpu_custom_call" | custom-call | flops 1610612736 | bytes 8388608 | tf_op jit(solution)/shard_map/pallas_call | solution.py:360
  128.3 6.6 %shard_map.118 = (f32[24,2048]{1,0:T(8,128)S(1)}, bf16[24,2048]{1,0:T(8,128)(2,1)S(1)}, f32[24,2048]{1,0:T(8,128)S(1)}, bf16[24,2048]{1,0:T(8,128)(2,1)S(1)}, f3...) custom-call(s32[1]{0:T(128)} %bitcast.7.scalars, ...), custom_call_target="tpu_custom_call" | custom-call | flops 1296039936 | bytes 6750208 | tf_op jit(solution)/shard_map/pallas_call | solution.py:360
  135.0 1.6 %collective-permute-start.27 = (bf16[24,2048]{1,0:T(8,128)(2,1)S(1)}, bf16[24,2048]{1,0:T(8,128)(2,1)S(1)}, u32[]{:S(2)}, u32[]{:S(2)}) collective-permute-start(bf16[24,2048]{1,0:T(8,128)(2,1)S(1)} %get-tuple-element.52), channel_id=1, source_target_pairs={{0,16},{16,0},{1,17},{17,1},{2,18},{18,2},{3,19},{19,3},{4,20},{20... | collective-permute-start | bytes 294920 | tf_op jit(solution)/shard_map/ppermute | solution.py:391
  137.0 1.5 collective-permute-start.31
  139.1 1.5 %collective-permute-done.27 = bf16[24,2048]{1,0:T(8,128)(2,1)S(1)} collective-permute-done((bf16[24,2048]{1,0:T(8,128)(2,1)S(1)}, bf16[24,2048]{1,0:T(8,128)(2,1)S(1)}, u32[]{:S(2)}, u32[]{:S(2)}) %collective-permute-start.27) | collective-permute-done | bytes 98336 | tf_op jit(solution)/shard_map/ppermute | solution.py:391
  140.6 2.1 %collective-permute-start.28 = (bf16[24,2048]{1,0:T(8,128)(2,1)S(1)}, bf16[24,2048]{1,0:T(8,128)(2,1)S(1)}, u32[]{:S(2)}, u32[]{:S(2)}) collective-permute-start(bf16[24,2048]{1,0:T(8,128)(2,1)S(1)} %add_convert_fusion.2), channel_id=1, source_target_pairs={{0,12},{4,8},{8,4},{12,0},{1,13},{5,9},{9,5},{13,1},{2,14},{6,10},... | collective-permute-start | bytes 294920 | tf_op jit(solution)/shard_map/ppermute | solution.py:387
  142.9 1.9 %collective-permute-done.31 = bf16[24,2048]{1,0:T(8,128)(2,1)S(1)} collective-permute-done((bf16[24,2048]{1,0:T(8,128)(2,1)S(1)}, bf16[24,2048]{1,0:T(8,128)(2,1)S(1)}, u32[]{:S(2)}, u32[]{:S(2)}) %collective-permute-start.31) | collective-permute-done | bytes 98336 | tf_op jit(solution)/shard_map/ppermute | solution.py:391
  144.8 0.7 collective-permute-start.32
  145.5 1.0 collective-permute-done.33
  146.5 1.5 collective-permute-done.28
  148.0 2.8 %collective-permute-done.30 = bf16[24,2048]{1,0:T(8,128)(2,1)S(1)} collective-permute-done((bf16[24,2048]{1,0:T(8,128)(2,1)S(1)}, bf16[24,2048]{1,0:T(8,128)(2,1)S(1)}, u32[]{:S(2)}, u32[]{:S(2)}) %collective-permute-start.30) | collective-permute-done | bytes 98336 | tf_op jit(solution)/shard_map/ppermute | solution.py:387
  150.8 0.9 collective-permute-done.32
  151.7 0.7 select_convert_fusion
  (57 shorter events, 6.8 us)
Async XLA Ops:
  0.0 63.2 %copy-start.2 = (bf16[2048]{0:T(1024)(128)(2,1)S(1)}, bf16[2048]{0:T(1024)(128)(2,1)}, u32[]{:S(2)}) copy-start(bf16[2048]{0:T(1024)(128)(2,1)} %param.18) | copy-start | bytes 12292
  9.3 8.5 %collective-permute-start = (bf16[96,1024]{1,0:T(8,128)(2,1)}, bf16[96,1024]{1,0:T(8,128)(2,1)S(1)}, u32[]{:S(2)}, u32[]{:S(2)}) collective-permute-start(bf16[96,1024]{1,0:T(8,128)(2,1)} %get-tuple-element.33), channel_id=1, source_target_pairs={{0,1},{1,0},{2,3},{3,2},{4,5},{5,4},{6,7},{7,6},{8,9},{9,8},{10,11... | collective-permute-start | bytes 589832 | tf_op jit(solution)/shard_map/ppermute | solution.py:379
  9.8 8.0 %collective-permute-start.1 = (f32[8,128]{1,0:T(8,128)}, f32[8,128]{1,0:T(8,128)S(1)}, u32[]{:S(2)}, u32[]{:S(2)}) collective-permute-start(f32[8,128]{1,0:T(8,128)} %get-tuple-element.35), channel_id=1, source_target_pairs={{0,1},{1,0},{2,3},{3,2},{4,5},{5,4},{6,7},{7,6},{8,9},{9,8},{10,11... | collective-permute-start | bytes 12296 | tf_op jit(solution)/shard_map/ppermute | solution.py:379
  17.8 0.9 copy-start
  18.7 0.7 copy-start.1
  19.8 8.2 %collective-permute-start.2 = (bf16[96,1024]{1,0:T(8,128)(2,1)S(1)}, bf16[96,1024]{1,0:T(8,128)(2,1)S(1)}, u32[]{:S(2)}, u32[]{:S(2)}) collective-permute-start(bf16[96,1024]{1,0:T(8,128)(2,1)S(1)} %get-tuple-element.36.a_ref), channel_id=1, source_target_pairs={{0,2},{1,3},{2,0},{3,1},{4,6},{5,7},{6,4},{7,5},{8,10},{9,11},{10,... | collective-permute-start | bytes 589832 | tf_op jit(solution)/shard_map/ppermute | solution.py:383
  22.8 5.2 %collective-permute-start.3 = (f32[8,128]{1,0:T(8,128)S(1)}, f32[8,128]{1,0:T(8,128)S(1)}, u32[]{:S(2)}, u32[]{:S(2)}) collective-permute-start(f32[8,128]{1,0:T(8,128)S(1)} %get-tuple-element.37.lse_a_ref), channel_id=1, source_target_pairs={{0,2},{1,3},{2,0},{3,1},{4,6},{5,7},{6,4},{7,5},{8,10},{9,11},{10,... | collective-permute-start | bytes 12296 | tf_op jit(solution)/shard_map/ppermute | solution.py:383
  29.0 1.4 collective-permute-start.4
  36.1 5.0 %collective-permute-start.5 = (bf16[24,2048]{1,0:T(8,128)(2,1)S(1)}, bf16[24,2048]{1,0:T(8,128)(2,1)S(1)}, u32[]{:S(2)}, u32[]{:S(2)}) collective-permute-start(bf16[24,2048]{1,0:T(8,128)(2,1)S(1)} %get-tuple-element.40), channel_id=1, source_target_pairs={{0,4},{4,0},{8,12},{12,8},{1,5},{5,1},{9,13},{13,9},{2,6},{6,2},{1... | collective-permute-start | bytes 294920 | tf_op jit(solution)/shard_map/ppermute | solution.py:387
  38.0 8.3 %collective-permute-start.6 = (bf16[24,2048]{1,0:T(8,128)(2,1)S(1)}, bf16[24,2048]{1,0:T(8,128)(2,1)S(1)}, u32[]{:S(2)}, u32[]{:S(2)}) collective-permute-start(bf16[24,2048]{1,0:T(8,128)(2,1)S(1)} %get-tuple-element.41), channel_id=1, source_target_pairs={{0,12},{4,8},{8,4},{12,0},{1,13},{5,9},{9,5},{13,1},{2,14},{6,10},... | collective-permute-start | bytes 294920 | tf_op jit(solution)/shard_map/ppermute | solution.py:387
  40.4 9.3 %collective-permute-start.7 = (bf16[24,2048]{1,0:T(8,128)(2,1)S(1)}, bf16[24,2048]{1,0:T(8,128)(2,1)S(1)}, u32[]{:S(2)}, u32[]{:S(2)}) collective-permute-start(bf16[24,2048]{1,0:T(8,128)(2,1)S(1)} %get-tuple-element.42), channel_id=1, source_target_pairs={{0,8},{4,12},{8,0},{12,4},{1,9},{5,13},{9,1},{13,5},{2,10},{6,14},... | collective-permute-start | bytes 294920 | tf_op jit(solution)/shard_map/ppermute | solution.py:387
  50.6 7.6 %collective-permute-start.13 = (bf16[24,2048]{1,0:T(8,128)(2,1)S(1)}, bf16[24,2048]{1,0:T(8,128)(2,1)S(1)}, u32[]{:S(2)}, u32[]{:S(2)}) collective-permute-start(bf16[24,2048]{1,0:T(8,128)(2,1)S(1)} %add_convert_fusion.3.refs_0_), channel_id=1, source_target_pairs={{0,12},{4,8},{8,4},{12,0},{1,13},{5,9},{9,5},{13,1},{2,14},{6,10},... | collective-permute-start | bytes 294920 | tf_op jit(solution)/shard_map/ppermute | solution.py:387
  53.4 7.8 %collective-permute-start.11 = (bf16[24,2048]{1,0:T(8,128)(2,1)S(1)}, bf16[24,2048]{1,0:T(8,128)(2,1)S(1)}, u32[]{:S(2)}, u32[]{:S(2)}) collective-permute-start(bf16[24,2048]{1,0:T(8,128)(2,1)S(1)} %add_convert_fusion.3.refs_0_), channel_id=1, source_target_pairs={{0,8},{4,12},{8,0},{12,4},{1,9},{5,13},{9,1},{13,5},{2,10},{6,14},... | collective-permute-start | bytes 294920 | tf_op jit(solution)/shard_map/ppermute | solution.py:387
  53.4 9.4 %collective-permute-start.9 = (bf16[24,2048]{1,0:T(8,128)(2,1)S(1)}, bf16[24,2048]{1,0:T(8,128)(2,1)S(1)}, u32[]{:S(2)}, u32[]{:S(2)}) collective-permute-start(bf16[24,2048]{1,0:T(8,128)(2,1)S(1)} %add_convert_fusion.3.refs_0_), channel_id=1, source_target_pairs={{0,4},{4,0},{8,12},{12,8},{1,5},{5,1},{9,13},{13,9},{2,6},{6,2},{1... | collective-permute-start | bytes 294920 | tf_op jit(solution)/shard_map/ppermute | solution.py:387
  55.1 8.1 %collective-permute-start.8 = (bf16[24,2048]{1,0:T(8,128)(2,1)S(1)}, bf16[24,2048]{1,0:T(8,128)(2,1)S(1)}, u32[]{:S(2)}, u32[]{:S(2)}) collective-permute-start(bf16[24,2048]{1,0:T(8,128)(2,1)S(1)} %add_convert_fusion.3.refs_0_), channel_id=1, source_target_pairs={{0,16},{16,0},{1,17},{17,1},{2,18},{18,2},{3,19},{19,3},{4,20},{20... | collective-permute-start | bytes 294920 | tf_op jit(solution)/shard_map/ppermute | solution.py:391
  58.3 5.0 %collective-permute-start.14 = (bf16[24,2048]{1,0:T(8,128)(2,1)S(1)}, bf16[24,2048]{1,0:T(8,128)(2,1)S(1)}, u32[]{:S(2)}, u32[]{:S(2)}) collective-permute-start(bf16[24,2048]{1,0:T(8,128)(2,1)S(1)} %collective-permute-done.13.refs_6_), channel_id=1, source_target_pairs={{0,16},{16,0},{1,17},{17,1},{2,18},{18,2},{3,19},{19,3},{4,20},{20... | collective-permute-start | bytes 294920 | tf_op jit(solution)/shard_map/ppermute | solution.py:391
  61.2 5.6 %collective-permute-start.12 = (bf16[24,2048]{1,0:T(8,128)(2,1)S(1)}, bf16[24,2048]{1,0:T(8,128)(2,1)S(1)}, u32[]{:S(2)}, u32[]{:S(2)}) collective-permute-start(bf16[24,2048]{1,0:T(8,128)(2,1)S(1)} %collective-permute-done.11.refs_4_), channel_id=1, source_target_pairs={{0,16},{16,0},{1,17},{17,1},{2,18},{18,2},{3,19},{19,3},{4,20},{20... | collective-permute-start | bytes 294920 | tf_op jit(solution)/shard_map/ppermute | solution.py:391
  62.7 5.3 %collective-permute-start.10 = (bf16[24,2048]{1,0:T(8,128)(2,1)S(1)}, bf16[24,2048]{1,0:T(8,128)(2,1)S(1)}, u32[]{:S(2)}, u32[]{:S(2)}) collective-permute-start(bf16[24,2048]{1,0:T(8,128)(2,1)S(1)} %collective-permute-done.9.refs_2_), channel_id=1, source_target_pairs={{0,16},{16,0},{1,17},{17,1},{2,18},{18,2},{3,19},{19,3},{4,20},{20... | collective-permute-start | bytes 294920 | tf_op jit(solution)/shard_map/ppermute | solution.py:391
  68.4 11.6 %collective-permute-start.17 = (f32[2,48,128]{2,1,0:T(8,128)S(1)}, f32[2,48,128]{2,1,0:T(8,128)S(1)}, u32[]{:S(2)}, u32[]{:S(2)}) collective-permute-start(f32[2,48,128]{2,1,0:T(8,128)S(1)} %slice.39), channel_id=1, source_target_pairs={{0,1},{1,0},{2,3},{3,2},{4,5},{5,4},{6,7},{7,6},{8,9},{9,8},{10,11... | collective-permute-start | bytes 147464 | tf_op jit(solution)/shard_map/ppermute | solution.py:379
  79.4 12.0 %collective-permute-start.22 = (bf16[2,2,48,2048]{3,2,1,0:T(8,128)(2,1)S(1)}, bf16[2,2,48,2048]{3,2,1,0:T(8,128)(2,1)S(1)}, u32[]{:S(2)}, u32[]{:S(2)}) collective-permute-start(bf16[2,2,48,2048]{3,2,1,0:T(8,128)(2,1)S(1)} %get-tuple-element.49), channel_id=1, source_target_pairs={{0,1},{1,0},{2,3},{3,2},{4,5},{5,4},{6,7},{7,6},{8,9},{9,8},{10,11... | collective-permute-start | bytes 2359304 | tf_op jit(solution)/shard_map/ppermute | solution.py:379
  80.0 11.3 %collective-permute-start.18 = (f32[48,128]{1,0:T(8,128)S(1)}, f32[48,128]{1,0:T(8,128)S(1)}, u32[]{:S(2)}, u32[]{:S(2)}) collective-permute-start(f32[48,128]{1,0:T(8,128)S(1)} %slice_bitcast_fusion.8), channel_id=1, source_target_pairs={{0,2},{1,3},{2,0},{3,1},{4,6},{5,7},{6,4},{7,5},{8,10},{9,11},{10,... | collective-permute-start | bytes 73736 | tf_op jit(solution)/shard_map/ppermute | solution.py:383
  91.2 2.1 %collective-permute-start.15 = (bf16[2,2,48,1648]{3,2,1,0:T(8,128)(2,1)S(1)}, bf16[2,2,48,1648]{3,2,1,0:T(8,128)(2,1)S(1)}, u32[]{:S(2)}, u32[]{:S(2)}) collective-permute-start(bf16[2,2,48,1648]{3,2,1,0:T(8,128)(2,1)S(1)} %get-tuple-element.45), channel_id=1, source_target_pairs={{0,1},{1,0},{2,3},{3,2},{4,5},{5,4},{6,7},{7,6},{8,9},{9,8},{10,11... | collective-permute-start | bytes 1898504 | tf_op jit(solution)/shard_map/ppermute | solution.py:379
  91.6 12.0 %collective-permute-start.23 = (bf16[2,48,2048]{2,1,0:T(8,128)(2,1)S(1)}, bf16[2,48,2048]{2,1,0:T(8,128)(2,1)S(1)}, u32[]{:S(2)}, u32[]{:S(2)}) collective-permute-start(bf16[2,48,2048]{2,1,0:T(8,128)(2,1)S(1)} %fusion), channel_id=1, source_target_pairs={{0,2},{1,3},{2,0},{3,1},{4,6},{5,7},{6,4},{7,5},{8,10},{9,11},{10,... | collective-permute-start | bytes 1179656 | tf_op jit(solution)/shard_map/ppermute | solution.py:383
  93.5 16.9 %collective-permute-start.16 = (bf16[2,48,1648]{2,1,0:T(8,128)(2,1)S(1)}, bf16[2,48,1648]{2,1,0:T(8,128)(2,1)S(1)}, u32[]{:S(2)}, u32[]{:S(2)}) collective-permute-start(bf16[2,48,1648]{2,1,0:T(8,128)(2,1)S(1)} %fusion.3), channel_id=1, source_target_pairs={{0,2},{1,3},{2,0},{3,1},{4,6},{5,7},{6,4},{7,5},{8,10},{9,11},{10,... | collective-permute-start | bytes 949256 | tf_op jit(solution)/shard_map/ppermute | solution.py:383
  103.9 10.3 %collective-permute-start.24 = (bf16[48,2048]{1,0:T(8,128)(2,1)S(1)}, bf16[48,2048]{1,0:T(8,128)(2,1)S(1)}, u32[]{:S(2)}, u32[]{:S(2)}) collective-permute-start(bf16[48,2048]{1,0:T(8,128)(2,1)S(1)} %fusion.7.refs_0_), channel_id=1, source_target_pairs={{0,2},{1,3},{2,0},{3,1},{4,6},{5,7},{6,4},{7,5},{8,10},{9,11},{10,... | collective-permute-start | bytes 589832 | tf_op jit(solution)/shard_map/ppermute | solution.py:383
  110.5 10.4 %collective-permute-start.25 = (bf16[48,2048]{1,0:T(8,128)(2,1)S(1)}, bf16[48,2048]{1,0:T(8,128)(2,1)S(1)}, u32[]{:S(2)}, u32[]{:S(2)}) collective-permute-start(bf16[48,2048]{1,0:T(8,128)(2,1)S(1)} %fusion.7.refs_0_), channel_id=1, source_target_pairs={{0,1},{1,0},{2,3},{3,2},{4,5},{5,4},{6,7},{7,6},{8,9},{9,8},{10,11... | collective-permute-start | bytes 589832 | tf_op jit(solution)/shard_map/ppermute | solution.py:379
  114.2 6.7 %collective-permute-start.26 = (bf16[48,2048]{1,0:T(8,128)(2,1)S(1)}, bf16[48,2048]{1,0:T(8,128)(2,1)S(1)}, u32[]{:S(2)}, u32[]{:S(2)}) collective-permute-start(bf16[48,2048]{1,0:T(8,128)(2,1)S(1)} %collective-permute-done.24.refs_1_), channel_id=1, source_target_pairs={{0,1},{1,0},{2,3},{3,2},{4,5},{5,4},{6,7},{7,6},{8,9},{9,8},{10,11... | collective-permute-start | bytes 589832 | tf_op jit(solution)/shard_map/ppermute | solution.py:379
  114.3 6.6 %collective-permute-start.19 = (bf16[48,1648]{1,0:T(8,128)(2,1)S(1)}, bf16[48,1648]{1,0:T(8,128)(2,1)S(1)}, u32[]{:S(2)}, u32[]{:S(2)}) collective-permute-start(bf16[48,1648]{1,0:T(8,128)(2,1)S(1)} %fusion.9.refs_0_), channel_id=1, source_target_pairs={{0,2},{1,3},{2,0},{3,1},{4,6},{5,7},{6,4},{7,5},{8,10},{9,11},{10,... | collective-permute-start | bytes 474632 | tf_op jit(solution)/shard_map/ppermute | solution.py:383
  114.9 13.4 %collective-permute-start.20 = (bf16[48,1648]{1,0:T(8,128)(2,1)S(1)}, bf16[48,1648]{1,0:T(8,128)(2,1)S(1)}, u32[]{:S(2)}, u32[]{:S(2)}) collective-permute-start(bf16[48,1648]{1,0:T(8,128)(2,1)S(1)} %fusion.9.refs_0_), channel_id=1, source_target_pairs={{0,1},{1,0},{2,3},{3,2},{4,5},{5,4},{6,7},{7,6},{8,9},{9,8},{10,11... | collective-permute-start | bytes 474632 | tf_op jit(solution)/shard_map/ppermute | solution.py:379
  120.9 7.4 %collective-permute-start.21 = (bf16[48,1648]{1,0:T(8,128)(2,1)S(1)}, bf16[48,1648]{1,0:T(8,128)(2,1)S(1)}, u32[]{:S(2)}, u32[]{:S(2)}) collective-permute-start(bf16[48,1648]{1,0:T(8,128)(2,1)S(1)} %collective-permute-done.19.refs_1_), channel_id=1, source_target_pairs={{0,1},{1,0},{2,3},{3,2},{4,5},{5,4},{6,7},{7,6},{8,9},{9,8},{10,11... | collective-permute-start | bytes 474632 | tf_op jit(solution)/shard_map/ppermute | solution.py:379
  135.0 5.7 %collective-permute-start.27 = (bf16[24,2048]{1,0:T(8,128)(2,1)S(1)}, bf16[24,2048]{1,0:T(8,128)(2,1)S(1)}, u32[]{:S(2)}, u32[]{:S(2)}) collective-permute-start(bf16[24,2048]{1,0:T(8,128)(2,1)S(1)} %get-tuple-element.52), channel_id=1, source_target_pairs={{0,16},{16,0},{1,17},{17,1},{2,18},{18,2},{3,19},{19,3},{4,20},{20... | collective-permute-start | bytes 294920 | tf_op jit(solution)/shard_map/ppermute | solution.py:391
  136.5 6.2 %collective-permute-start.29 = (bf16[24,2048]{1,0:T(8,128)(2,1)S(1)}, bf16[24,2048]{1,0:T(8,128)(2,1)S(1)}, u32[]{:S(2)}, u32[]{:S(2)}) collective-permute-start(bf16[24,2048]{1,0:T(8,128)(2,1)S(1)} %get-tuple-element.54), channel_id=1, source_target_pairs={{0,16},{16,0},{1,17},{17,1},{2,18},{18,2},{3,19},{19,3},{4,20},{20... | collective-permute-start | bytes 294920 | tf_op jit(solution)/shard_map/ppermute | solution.py:391
  137.0 7.8 %collective-permute-start.31 = (bf16[24,2048]{1,0:T(8,128)(2,1)S(1)}, bf16[24,2048]{1,0:T(8,128)(2,1)S(1)}, u32[]{:S(2)}, u32[]{:S(2)}) collective-permute-start(bf16[24,2048]{1,0:T(8,128)(2,1)S(1)} %get-tuple-element.56), channel_id=1, source_target_pairs={{0,16},{16,0},{1,17},{17,1},{2,18},{18,2},{3,19},{19,3},{4,20},{20... | collective-permute-start | bytes 294920 | tf_op jit(solution)/shard_map/ppermute | solution.py:391
  138.6 8.0 %collective-permute-start.33 = (bf16[24,2048]{1,0:T(8,128)(2,1)S(1)}, bf16[24,2048]{1,0:T(8,128)(2,1)S(1)}, u32[]{:S(2)}, u32[]{:S(2)}) collective-permute-start(bf16[24,2048]{1,0:T(8,128)(2,1)S(1)} %get-tuple-element.58), channel_id=1, source_target_pairs={{0,16},{16,0},{1,17},{17,1},{2,18},{18,2},{3,19},{19,3},{4,20},{20... | collective-permute-start | bytes 294920 | tf_op jit(solution)/shard_map/ppermute | solution.py:391
  140.6 7.4 %collective-permute-start.28 = (bf16[24,2048]{1,0:T(8,128)(2,1)S(1)}, bf16[24,2048]{1,0:T(8,128)(2,1)S(1)}, u32[]{:S(2)}, u32[]{:S(2)}) collective-permute-start(bf16[24,2048]{1,0:T(8,128)(2,1)S(1)} %add_convert_fusion.2), channel_id=1, source_target_pairs={{0,12},{4,8},{8,4},{12,0},{1,13},{5,9},{9,5},{13,1},{2,14},{6,10},... | collective-permute-start | bytes 294920 | tf_op jit(solution)/shard_map/ppermute | solution.py:387
  142.8 8.0 %collective-permute-start.30 = (bf16[24,2048]{1,0:T(8,128)(2,1)S(1)}, bf16[24,2048]{1,0:T(8,128)(2,1)S(1)}, u32[]{:S(2)}, u32[]{:S(2)}) collective-permute-start(bf16[24,2048]{1,0:T(8,128)(2,1)S(1)} %add_convert_fusion.1), channel_id=1, source_target_pairs={{0,8},{4,12},{8,0},{12,4},{1,9},{5,13},{9,1},{13,5},{2,10},{6,14},... | collective-permute-start | bytes 294920 | tf_op jit(solution)/shard_map/ppermute | solution.py:387
  144.8 6.8 %collective-permute-start.32 = (bf16[24,2048]{1,0:T(8,128)(2,1)S(1)}, bf16[24,2048]{1,0:T(8,128)(2,1)S(1)}, u32[]{:S(2)}, u32[]{:S(2)}) collective-permute-start(bf16[24,2048]{1,0:T(8,128)(2,1)S(1)} %add_convert_fusion), channel_id=1, source_target_pairs={{0,4},{4,0},{8,12},{12,8},{1,5},{5,1},{9,13},{13,9},{2,6},{6,2},{1... | collective-permute-start | bytes 294920 | tf_op jit(solution)/shard_map/ppermute | solution.py:387

commit v2 on v1

--- a/solution.py
+++ b/solution.py
@@ -9,11 +9,13 @@
 from jax.sharding import PartitionSpec as P
 
 DH = 128
-TILE = 256
+TILE = 640
+CHUNKS = (3, 3)
+HEADS = 4
 NEGATIVE = -1e30
 BF16 = jnp.bfloat16
 F32 = jnp.float32
-LIMIT = 50 * 1024 * 1024
+LIMIT = 16 * 1024 * 1024
 ORDER = (0, 2, 1, 3)
 
 
@@ -33,86 +35,124 @@
     return pl.BlockSpec(shape, lambda *unused: (0,) * len(shape))
 
 
-def attention_kernel(heads, scalars, q_ref, key_ref, value_ref, new_key_ref, new_value_ref, out_ref, lse_ref, columns):
+def fetch_kernel(source, target, zero, done):
+    copy = pltpu.make_async_copy(source, target, done)
+    copy.start()
+    zero[...] = jnp.zeros_like(zero)
+    copy.wait()
+
+
+def fetch(weight, after):
+    weight, after = lax.optimization_barrier((weight, after))
+    weight = pltpu.with_memory_space_constraint(weight, pltpu.HBM)
+    held, zero = pl.pallas_call(
+        fetch_kernel,
+        in_specs=[pl.BlockSpec(memory_space=pltpu.HBM)],
+        out_specs=[pl.BlockSpec(memory_space=pltpu.VMEM)] * 2,
+        out_shape=[
+            jax.ShapeDtypeStruct(weight.shape, weight.dtype),
+            jax.ShapeDtypeStruct((8, 128), F32),
+        ],
+        scratch_shapes=[pltpu.SemaphoreType.DMA],
+        compiler_params=params(),
+        cost_estimate=cost(0, 2 * weight.size * 2),
+    )(weight)
+    return held, zero, after
+
+
+def attention_kernel(
+    scalars, q_ref, key_ref, value_ref, new_key_ref, new_value_ref, sent_ref, kept_ref, sent_lse_ref, kept_lse_ref, columns
+):
     step = pl.program_id(0)
     span = q_ref.shape[0]
     cache_len = key_ref.shape[2]
+    per_kv = sent_lse_ref.shape[0]
     usable, length, first = scalars[1], scalars[2], scalars[3]
     scale = 1.0 / math.sqrt(DH)
-    q = jnp.concatenate([q_ref[:, h * DH : (h + 1) * DH] for h in range(heads)], axis=0)
-    contract = (((1,), (1,)), ((), ()))
-    scores = lax.dot_general(q, key_ref[0, 0], contract, preferred_element_type=F32)
     position = lax.broadcasted_iota(jnp.int32, (1, cache_len), 1)
     bias = jnp.where(position < usable, 0.0, NEGATIVE)
-    scores = scores * scale + bias
-    fresh = lax.dot_general(q, new_key_ref[0], contract, preferred_element_type=F32)
     row = lax.broadcasted_iota(jnp.int32, (span, span), 0)
     col = lax.broadcasted_iota(jnp.int32, (span, span), 1)
     allowed = (col <= row) & (col < length) & (first > 0)
-    fresh_bias = jnp.where(allowed, 0.0, NEGATIVE)
-    fresh = fresh * scale + jnp.concatenate([fresh_bias] * heads, axis=0)
-    top = jnp.maximum(
-        jnp.max(scores, axis=1, keepdims=True), jnp.max(fresh, axis=1, keepdims=True)
-    )
-    probs = jnp.exp(scores - top)
-    fresh_probs = jnp.exp(fresh - top)
-    total = jnp.sum(probs, axis=1, keepdims=True) + jnp.sum(fresh_probs, axis=1, keepdims=True)
-    values = jnp.dot(probs.astype(BF16), value_ref[0, 0], preferred_element_type=F32)
-    values += jnp.dot(fresh_probs.astype(BF16), new_value_ref[0], preferred_element_type=F32)
-    values = (values / total).astype(BF16)
-    lse = top + jnp.log(total)
-    for h in range(heads):
-        out_ref[:, h * DH : (h + 1) * DH] = values[h * span : (h + 1) * span]
+    fresh_bias = jnp.concatenate([jnp.where(allowed, 0.0, NEGATIVE)] * HEADS, axis=0)
+    contract = (((1,), (1,)), ((), ()))
+    keys, values = key_ref[0, 0], value_ref[0, 0]
+    new_keys, new_values = new_key_ref[0], new_value_ref[0]
+    columns[...] = jnp.zeros_like(columns)
+    for low in range(0, per_kv, HEADS):
+        heads = range(low, low + HEADS)
+        q = jnp.concatenate([q_ref[:, h * DH : (h + 1) * DH] for h in heads], axis=0)
+        scores = lax.dot_general(q, keys, contract, preferred_element_type=F32) * scale + bias
+        fresh = lax.dot_general(q, new_keys, contract, preferred_element_type=F32)
+        fresh = fresh * scale + fresh_bias
+        top = jnp.maximum(
+            jnp.max(scores, axis=1, keepdims=True), jnp.max(fresh, axis=1, keepdims=True)
+        )
+        probs = jnp.exp(scores - top)
+        fresh_probs = jnp.exp(fresh - top)
+        total = jnp.sum(probs, axis=1, keepdims=True) + jnp.sum(fresh_probs, axis=1, keepdims=True)
+        mixed = jnp.dot(probs.astype(BF16), values, preferred_element_type=F32)
+        mixed += jnp.dot(fresh_probs.astype(BF16), new_values, preferred_element_type=F32)
+        mixed = (mixed / total).astype(BF16)
+        lse = top + jnp.log(total)
+        for i, h in enumerate(heads):
+            columns[0:span, h : h + 1] = lse[i * span : (i + 1) * span]
+            piece = mixed[i * span : (i + 1) * span]
+
+            @pl.when(step == 0)
+            def to_sent():
+                sent_ref[:, h * DH : (h + 1) * DH] = piece
+
+            @pl.when(step == 1)
+            def to_kept():
+                kept_ref[:, h * DH : (h + 1) * DH] = piece
+
+    rows = jnp.transpose(columns[...])[0:per_kv, :]
 
     @pl.when(step == 0)
-    def first_step():
-        columns[...] = jnp.zeros_like(columns)
-
-    lane = lax.broadcasted_iota(jnp.int32, (span, 128), 1)
-    kept = columns[0:span, :]
-    for h in range(heads):
-        kept = jnp.where(lane == step * heads + h, lse[h * span : (h + 1) * span], kept)
-    columns[0:span, :] = kept
-
-    @pl.when(step == pl.num_programs(0) - 1)
-    def last_step():
-        lse_ref[...] = jnp.transpose(columns[...])[0 : lse_ref.shape[0], :]
-
-
-def attention(scalars, queries, kv_cache, new_kv, local_kv):
+    def lse_sent():
+        sent_lse_ref[...] = rows
+
+    @pl.when(step == 1)
+    def lse_kept():
+        kept_lse_ref[...] = rows
+
+
+def attention(scalars, queries, kv_cache, new_kv):
     span, qcols = queries.shape
-    per_kv = qcols // DH // local_kv
-    heads = 4
-    steps = per_kv // heads
+    per_kv = qcols // DH // 2
     cache_len = kv_cache.shape[2]
-    width = heads * DH
+    width = per_kv * DH
+
+    def which(i, s):
+        return s[0] ^ 1 ^ i
+
+    def at_home(array):
+        return pltpu.with_memory_space_constraint(array, pltpu.HBM)
+
     call = pl.pallas_call(
-        functools.partial(attention_kernel, heads),
+        attention_kernel,
         grid_spec=pltpu.PrefetchScalarGridSpec(
             num_scalar_prefetch=1,
-            grid=(steps,),
+            grid=(2,),
             in_specs=[
-                pl.BlockSpec((span, width), lambda i, s: (0, s[0] * steps + i)),
-                pl.BlockSpec((1, 1, cache_len, DH), lambda i, s: (0, 0, 0, s[0])),
-                pl.BlockSpec((1, 1, cache_len, DH), lambda i, s: (1, 0, 0, s[0])),
-                pl.BlockSpec((1, span, DH), lambda i, s: (0, 0, s[0])),
-                pl.BlockSpec((1, span, DH), lambda i, s: (1, 0, s[0])),
+                pl.BlockSpec((span, width), lambda i, s: (0, which(i, s))),
+                pl.BlockSpec((1, 1, cache_len, DH), lambda i, s: (0, 0, 0, which(i, s))),
+                pl.BlockSpec((1, 1, cache_len, DH), lambda i, s: (1, 0, 0, which(i, s))),
+                pl.BlockSpec((1, span, DH), lambda i, s: (0, 0, which(i, s))),
+                pl.BlockSpec((1, span, DH), lambda i, s: (1, 0, which(i, s))),
             ],
-            out_specs=[
-                pl.BlockSpec((span, width), lambda i, s: (0, i)),
-                pl.BlockSpec((per_kv, 128), lambda i, s: (0, 0)),
-            ],
+            out_specs=[whole((span, width))] * 2 + [whole((per_kv, 128))] * 2,
             scratch_shapes=[pltpu.VMEM((128, 128), F32)],
         ),
-        out_shape=[
-            jax.ShapeDtypeStruct((span, per_kv * DH), BF16),
-            jax.ShapeDtypeStruct((per_kv, 128), F32),
-        ],
-        compiler_params=params(60 * 1024 * 1024),
+        out_shape=[jax.ShapeDtypeStruct((span, width), BF16)] * 2
+        + [jax.ShapeDtypeStruct((per_kv, 128), F32)] * 2,
+        compiler_params=params(40 * 1024 * 1024),
         cost_estimate=cost(
-            4 * span * per_kv * cache_len * DH, 4 * cache_len * DH, span * per_kv * cache_len
+            8 * span * per_kv * cache_len * DH, 8 * cache_len * DH, 2 * span * per_kv * cache_len
         ),
     )
+    queries, kv_cache, new_kv = at_home(queries), at_home(kv_cache), at_home(new_kv)
     return call(scalars, queries, kv_cache, kv_cache, new_kv, new_kv)
 
 
@@ -175,7 +215,7 @@
     @pl.when(step == pl.num_programs(0) - 1)
     def finish():
         for k, out in enumerate(outs):
-            start = pl.multiple_of((scalars[1] ^ k) * rows, 8)
+            start = pl.multiple_of((scalars[4] ^ k) * rows, 8)
             out[...] = acc[pl.ds(start, rows), :].astype(out.dtype)
 
 
@@ -211,20 +251,22 @@
 
 def scale_kernel(slots, scalars, *refs):
     count = 4 * slots
-    sources, gain_ref, scaled_ref, square_ref = refs[:count], refs[count], refs[count + 1], refs[count + 2]
+    sources, gain_ref, scaled_ref, square_ref, ordered = refs[:count], *refs[count:]
     gain = gain_ref[...].astype(F32)
     cols = gain.shape[1]
     for k in range(4):
-        place = swapped_bits(scalars[0] ^ k)
+        place = swapped_bits(scalars[5] ^ k)
         rows = jnp.concatenate(
             [sources[k * slots + s][...].astype(F32) for s in range(slots)], axis=0
         )
-        scaled_ref[place] = (rows * gain).astype(BF16)
+        ordered[place] = rows * gain
         squares = rows * rows
         part = squares[:, 0:128]
         for c in range(128, cols, 128):
             part += squares[:, c : c + 128]
         square_ref[place] = part
+    tall = ordered[...].reshape(scaled_ref.shape[1], cols)
+    scaled_ref[...] = jnp.transpose(tall).astype(BF16)
 
 
 def scale_rows(scalars, sources, gain):
@@ -237,10 +279,11 @@
             num_scalar_prefetch=1,
             grid=(1,),
             in_specs=[whole((rows, cols))] * len(sources) + [whole((1, cols))],
-            out_specs=[whole((4, high, cols)), whole((4, high, 128))],
+            out_specs=[whole((cols, 4 * high)), whole((4, high, 128))],
+            scratch_shapes=[pltpu.VMEM((4, high, cols), F32)],
         ),
         out_shape=[
-            jax.ShapeDtypeStruct((4, high, cols), BF16),
+            jax.ShapeDtypeStruct((cols, 4 * high), BF16),
             jax.ShapeDtypeStruct((4, high, 128), F32),
         ],
         compiler_params=params(),
@@ -249,12 +292,10 @@
 
 
 def gate_up_kernel(scaled_ref, gate_ref, up_ref, keep_ref, cross_ref, send_ref):
-    places, high, depth = scaled_ref.shape
-    rows = scaled_ref[...].reshape(places * high, depth)
+    high = keep_ref.shape[1]
     for which, weight in enumerate((gate_ref, up_ref)):
-        term = lax.dot_general(
-            rows, weight[...], (((1,), (1,)), ((), ())), preferred_element_type=F32
-        ).astype(BF16)
+        term = jnp.dot(weight[...], scaled_ref[...], preferred_element_type=F32)
+        term = jnp.transpose(term).astype(BF16)
         keep_ref[which] = term[0:high]
         cross_ref[which] = term[high : 2 * high]
         send_ref[0, which] = term[2 * high : 3 * high]
@@ -262,7 +303,8 @@
 
 
 def gate_up(scaled, gate_weight, up_weight, begin, width):
-    places, high, depth = scaled.shape
+    depth, rows = scaled.shape
+    high = rows // 4
     tiles = pl.cdiv(width, TILE)
     first = begin // TILE
     weight = pl.BlockSpec((TILE, depth), lambda j: (first + j, 0))
@@ -278,7 +320,7 @@
             jax.ShapeDtypeStruct((2, 2, high, width), BF16),
         ],
         compiler_params=params(),
-        cost_estimate=cost(4 * places * high * depth * width, 4 * depth * width),
+        cost_estimate=cost(4 * rows * depth * width, 4 * depth * width),
     )(scaled, gate_weight, up_weight)
 
 
@@ -331,7 +373,7 @@
             return
         rows = high // slots
         for k in range(4):
-            place = swapped_bits(scalars[0] ^ k)
+            place = swapped_bits(scalars[5] ^ k)
             block = acc[place]
             for s in range(slots):
                 out = outs[k * slots + s]
@@ -392,9 +434,10 @@
 
 
 def cut(total):
-    tiles = -(-total // TILE)
-    head = (tiles + 1) // 2 * TILE
-    return [(0, head), (head, total - head)]
+    edges = [0]
+    for tiles in CHUNKS:
+        edges.append(min(edges[-1] + tiles * TILE, total))
+    return [(low, high - low) for low, high in zip(edges, edges[1:])]
 
 
 def body(
@@ -422,30 +465,30 @@
     model = gain.shape[0] * lax.axis_size("ffn")
     usable = jnp.clip(prefixes[0] - f * cache_len, 0, cache_len)
     first = (f == 0).astype(jnp.int32)
-
-    def attend(which):
-        scalars = jnp.stack([which, usable, length, first]).astype(jnp.int32)
-        return attention(scalars, queries, kv_cache, new_kv, local_kv)
-
-    sent, sent_lse = attend(1 - core)
+    scalars = jnp.stack([core, usable, length, first, t, t ^ f]).astype(jnp.int32)
+    own_resid = lax.dynamic_slice_in_dim(resid, t * rows, rows, 0).astype(F32)
+    live = (t * rows + jnp.arange(rows, dtype=jnp.int32) < length)[:, None]
+    live = jnp.broadcast_to(live, (rows, 128)).astype(F32)
+    scalars, own_resid, live = lax.optimization_barrier((scalars, own_resid, live))
+    sent, kept, sent_lse, kept_lse = attention(scalars, queries, kv_cache, new_kv)
     got, got_lse = to_core(sent), to_core(sent_lse)
-    kept, kept_lse = attend(core)
     kept, kept_lse = combine(kept, got, kept_lse, got_lse)
-    got, got_lse = to_x(kept), to_x(kept_lse)
+    out_held, zero, kept = fetch(out_weight, kept)
+    got, got_lse = to_x(kept), to_x(kept_lse) + zero
     mine, unused = combine(kept, got, kept_lse, got_lse)
     other = to_core(mine)
 
-    order = jnp.stack([core, t]).astype(jnp.int32)
-    terms = project(order, mine, other, out_weight, tp_size)
-    own_resid = lax.dynamic_slice_in_dim(resid, t * rows, rows, 0).astype(F32)
-    summed = terms[0] + own_resid
-    for k in (1, 3, 2):
-        summed += to_z(terms[k], k).astype(F32)
+    terms = list(project(scalars, mine, other, out_held, tp_size))
+    gate_held, zero, terms[1] = fetch(gate_weight.T, terms[1])
+    passed = [to_z(terms[k], k) for k in (1, 3, 2)]
+    summed = terms[0] + own_resid + zero[0:1, 0:1]
+    for term in passed:
+        summed += term.astype(F32)
     h1 = summed.astype(BF16)
 
-    turn = jnp.stack([t ^ f]).astype(jnp.int32)
     natural = g ^ jnp.arange(groups, dtype=jnp.int32)
     by_z = [h1, to_z(h1, 1), to_z(h1, 2), to_z(h1, 3)]
+    up_held, unused, by_z[1] = fetch(up_weight.T, by_z[1])
     sources = []
     for part in by_z:
         if groups == 2:
@@ -453,25 +496,35 @@
         else:
             everyone = jnp.take(lax.all_gather(part, "grp"), natural, axis=0)
             sources += [everyone[s] for s in range(groups)]
-    scaled, squares = scale_rows(turn, sources, gain[None, :])
-
-    pair = squares[0:2] + to_core(squares[2:4])
-    own_squares = pair[0] + to_x(pair[1])
+    scaled, squares = scale_rows(scalars, sources, gain[None, :])
+
+    chunks = cut(gate_weight.shape[1])
+    reduced = []
+    for begin, width in chunks:
+        keep, cross, send = gate_up(scaled, gate_held, up_held, begin, width)
+        got = to_core(send)
+        cross = (cross.astype(F32) + got[1].astype(F32)).astype(BF16)
+        scaled, cross = lax.optimization_barrier((scaled, cross))
+        reduced.append((keep, got, to_x(cross)))
+        if begin == 0:
+            squares, scaled = lax.optimization_barrier((squares, scaled))
+            pair = squares[0:2] + to_core(squares[2:4])
+            own_squares = pair[0] + to_x(pair[1])
     inv_rms = lax.rsqrt(jnp.sum(own_squares, axis=1, keepdims=True) / model + 1e-06)
-
-    chunks = cut(gate_weight.shape[1])
     total = None
-    parts = [gate_up(scaled, gate_weight.T, up_weight.T, begin, width) for begin, width in chunks]
     for index, (begin, width) in enumerate(chunks):
-        keep, cross, send = parts[index]
-        got = to_core(send)
-        crossed = to_x((cross.astype(F32) + got[1].astype(F32)).astype(BF16))
+        keep, got, crossed = reduced[index]
         both = (keep.astype(F32) + got[0].astype(F32) + crossed.astype(F32)) * inv_rms
         hidden = (jax.nn.silu(both[0]) * both[1]).astype(BF16)
+        if index == 0:
+            down_held, zero, hidden = fetch(down_weight, hidden)
+            inv_rms += zero[0:1, 0:1]
         over = to_x(hidden)
+        if index > 0:
+            over, total = lax.optimization_barrier((over, total))
         pieces = [hidden, over, to_core(hidden), to_core(over)]
         is_last = index == len(chunks) - 1
-        result = down(turn, pieces, down_weight, begin, total, groups, is_last)
+        result = down(scalars, pieces, down_held, begin, total, groups, is_last)
         total = None if is_last else result[0]
 
     chunk_sums = []
@@ -493,8 +546,7 @@
         else:
             value = chunk_sums[k]
         out += value if k == 0 else to_z(value.astype(BF16), k).astype(F32)
-    live = t * rows + jnp.arange(rows, dtype=jnp.int32) < length
-    return jnp.where(live[:, None], out, 0.0).astype(BF16)
+    return jnp.where(live[:, 0:1] > 0, out, 0.0).astype(BF16)
 
 
 def merged(x, axis, combine):

time: 153 us -> 127 us (0.83)
  waiting for transfers between devices: 59 us -> 33.6 us
  Pallas kernels: 56.6 us -> 53.5 us
  starting transfers between devices: 29.6 us -> 32.5 us
    pallas_call x0 -> x4, Pallas kernels: none -> 19.9 us  [fetch(): pl.pallas_call(fetch_kernel, in_specs=[pl.BlockSpec(memory_space=pltpu.HB...]
    ppermute x7, waiting for transfers between devices: 29.9 us -> 11.5 us  [to_x(): return lax.ppermute(x, 'ffn', [(i, i ^ 2) for i in range(4)])]
    pallas_call x2, Pallas kernels: 20.6 us -> 10.3 us  [gate_up(): pl.pallas_call(gate_up_kernel, grid=(tiles,), in_specs=[whole(scaled.shap...]
    pallas_call x2, Pallas kernels: 14 us -> 6.72 us  [down(): pl.pallas_call(functools.partial(down_kernel, width, slots, start is not...]
    ppermute x8, waiting for transfers between devices: 9.22 us -> 2.28 us  [to_y(): return lax.ppermute(x, 'grp', [(0, 1), (1, 0)])]
    ppermute x9, waiting for transfers between devices: 17.4 us -> 13.7 us  [to_z(): return lax.ppermute(x, 'tp', [(i, i ^ k) for i in range(4)])]
    ppermute x10, waiting for transfers between devices: 2.59 us -> 6.14 us  [to_core(): return lax.ppermute(x, 'ffn', [(i, i ^ 1) for i in range(4)])]
    pallas_call x2 -> x1, Pallas kernels: 14.7 us -> 11.3 us  [attention(): return call(scalars, queries, kv_cache, kv_cache, new_kv, new_kv)]
  transfers between devices with their start and end apart: 34 -> 34, of which waited for: 20 -> 16; matrix products, arithmetic and copies ran while one was open for 1% -> 2% of each run, Pallas kernels for 23% -> 23%
where the time goes in v2:
time: 127 us; the launch traced here: 126 us
  Pallas kernels  53.5 us (42%)
  waiting for transfers between devices  33.6 us (26%)
  starting transfers between devices  32.5 us (26%)
  other arithmetic  3.9 us (3%)
  between operations  1.6 us (1%)
    pallas_call x4, Pallas kernels, fetch(): pl.pallas_call(fetch_kernel, in_specs=[pl.BlockSpec(memory_space=pltpu.HB...  19.9 us
    ppermute x9, waiting for transfers between devices, to_z(): return lax.ppermute(x, 'tp', [(i, i ^ k) for i in range(4)])  13.7 us
    ppermute x9, starting transfers between devices, to_z(): return lax.ppermute(x, 'tp', [(i, i ^ k) for i in range(4)])  12.8 us
    ppermute x7, waiting for transfers between devices, to_x(): return lax.ppermute(x, 'ffn', [(i, i ^ 2) for i in range(4)])  11.5 us
    pallas_call x1, Pallas kernels, attention(): return call(scalars, queries, kv_cache, kv_cache, new_kv, new_kv)  11.3 us
    pallas_call x2, Pallas kernels, gate_up(): pl.pallas_call(gate_up_kernel, grid=(tiles,), in_specs=[whole(scaled.shap...  10.3 us
    ppermute x7, starting transfers between devices, to_x(): return lax.ppermute(x, 'ffn', [(i, i ^ 2) for i in range(4)])  9.27 us
    ppermute x8, starting transfers between devices, to_y(): return lax.ppermute(x, 'grp', [(0, 1), (1, 0)])  9.19 us
  transfers between devices with their start and end apart: 34, of which 16 were waited for; matrix products, arithmetic and copies ran while one was open for 2% of the time, Pallas kernels for 23%

profile of v2, /device:TPU:0, one launch (start us, length us, event | category | flops | bytes accessed | tf_op | source)
XLA Modules:
  0.0 126.3 jit_solution(15962791339298492420)
XLA Ops:
  1.3 0.9 dynamic-slice_convert_fusion
  2.3 11.3 %shard_map.109 = (bf16[96,1024]{1,0:T(8,128)(2,1)S(1)}, bf16[96,1024]{1,0:T(8,128)(2,1)S(1)}, f32[8,128]{1,0:T(8,128)S(1)}, f32[8,128]{1,0:T(8,128)S(1)}) custom-call(s32[6]{0:T(128)S(1)} %stack.27.scalars, bf16[96,2048]{1,0:T(8,128)(2,1)} %q_ref.1, bf16[2,1,2048,256]{3,2,1,0:T(8,128)(2,1)} %value_ref.1, bf16[2,1,2048,256]{3,2,1,0:T(8,128)(2,1)} %value_ref.1, ...), custom_call_target="tpu_custom_call" | custom-call | flops 1610612736 | bytes 2097152 | tf_op jit(solution)/shard_map/pallas_call | solution.py:156
  14.2 1.1 collective-permute-done.1.lse_b_ref
  15.8 2.8 %collective-permute-start.2 = (bf16[96,1024]{1,0:T(8,128)(2,1)S(1)}, bf16[96,1024]{1,0:T(8,128)(2,1)S(1)}, u32[]{:S(2)}, u32[]{:S(2)}) collective-permute-start(bf16[96,1024]{1,0:T(8,128)(2,1)S(1)} %get-tuple-element.64.a_ref), channel_id=1, source_target_pairs={{0,2},{1,3},{2,0},{3,1},{4,6},{5,7},{6,4},{7,5},{8,10},{9,11},{10,... | collective-permute-start | bytes 589832 | tf_op jit(solution)/shard_map/ppermute | solution.py:425
  18.7 3.4 %shard_map.111 = (bf16[2048,2048]{1,0:T(8,128)(2,1)S(1)}, f32[8,128]{1,0:T(8,128)S(1)}) custom-call(bf16[2048,2048]{1,0:T(8,128)(2,1)} %source), custom_call_target="tpu_custom_call" | custom-call | bytes 16777216 | tf_op jit(solution)/shard_map/pallas_call | solution.py:48
  22.1 1.9 %collective-permute-done.3 = f32[8,128]{1,0:T(8,128)S(1)} collective-permute-done((f32[8,128]{1,0:T(8,128)S(1)}, f32[8,128]{1,0:T(8,128)S(1)}, u32[]{:S(2)}, u32[]{:S(2)}) %collective-permute-start.3) | collective-permute-done | bytes 4128 | tf_op jit(solution)/shard_map/ppermute | solution.py:425
  24.0 0.9 shard_map.112
  24.9 1.4 %collective-permute-done.4.other_ref = bf16[96,1024]{1,0:T(8,128)(2,1)S(1)} collective-permute-done((bf16[96,1024]{1,0:T(8,128)(2,1)S(1)}, bf16[96,1024]{1,0:T(8,128)(2,1)S(1)}, u32[]{:S(2)}, u32[]{:S(2)}) %collective-permute-start.4) | collective-permute-done | bytes 196640 | tf_op jit(solution)/shard_map/ppermute | solution.py:421
  26.4 2.7 %shard_map.113 = (f32[24,2048]{1,0:T(8,128)S(1)}, bf16[24,2048]{1,0:T(8,128)(2,1)S(1)}, bf16[24,2048]{1,0:T(8,128)(2,1)S(1)}, bf16[24,2048]{1,0:T(8,128)(2,1)S(1)}) custom-call(s32[6]{0:T(128)S(1)} %stack.27.scalars, bf16[96,1024]{1,0:T(8,128)(2,1)S(1)} %get-tuple-element.68.keep_ref, bf16[96,1024]{1,0:T(8,128)(2,1)S(1)} %collective-permute-done.4.other_ref, ...), custom_call_target="tpu_custom_call" | custom-call | flops 805306368 | bytes 8388608 | tf_op jit(solution)/shard_map/pallas_call | solution.py:228
  29.0 1.9 %collective-permute-start.5 = (bf16[24,2048]{1,0:T(8,128)(2,1)S(1)}, bf16[24,2048]{1,0:T(8,128)(2,1)S(1)}, u32[]{:S(2)}, u32[]{:S(2)}) collective-permute-start(bf16[24,2048]{1,0:T(8,128)(2,1)S(1)} %get-tuple-element.75), channel_id=1, source_target_pairs={{0,4},{4,0},{8,12},{12,8},{1,5},{5,1},{9,13},{13,9},{2,6},{6,2},{1... | collective-permute-start | bytes 294920 | tf_op jit(solution)/shard_map/ppermute | solution.py:429
  30.9 2.5 %collective-permute-start.6 = (bf16[24,2048]{1,0:T(8,128)(2,1)S(1)}, bf16[24,2048]{1,0:T(8,128)(2,1)S(1)}, u32[]{:S(2)}, u32[]{:S(2)}) collective-permute-start(bf16[24,2048]{1,0:T(8,128)(2,1)S(1)} %get-tuple-element.76), channel_id=1, source_target_pairs={{0,12},{4,8},{8,4},{12,0},{1,13},{5,9},{9,5},{13,1},{2,14},{6,10},... | collective-permute-start | bytes 294920 | tf_op jit(solution)/shard_map/ppermute | solution.py:429
  33.5 5.3 %shard_map.114 = (bf16[3696,2048]{1,0:T(8,128)(2,1)S(1)}, f32[8,128]{1,0:T(8,128)S(1)}) custom-call(bf16[3696,2048]{1,0:T(8,128)(2,1)} %bitcast.63), custom_call_target="tpu_custom_call" | custom-call | bytes 30277632 | tf_op jit(solution)/shard_map/pallas_call | solution.py:48
  39.4 3.3 %collective-permute-done.7 = bf16[24,2048]{1,0:T(8,128)(2,1)S(1)} collective-permute-done((bf16[24,2048]{1,0:T(8,128)(2,1)S(1)}, bf16[24,2048]{1,0:T(8,128)(2,1)S(1)}, u32[]{:S(2)}, u32[]{:S(2)}) %collective-permute-start.7) | collective-permute-done | bytes 98336 | tf_op jit(solution)/shard_map/ppermute | solution.py:429
  42.7 0.7 add_convert_fusion.3.refs_0_
  43.5 2.7 %collective-permute-start.13 = (bf16[24,2048]{1,0:T(8,128)(2,1)S(1)}, bf16[24,2048]{1,0:T(8,128)(2,1)S(1)}, u32[]{:S(2)}, u32[]{:S(2)}) collective-permute-start(bf16[24,2048]{1,0:T(8,128)(2,1)S(1)} %add_convert_fusion.3.refs_0_), channel_id=1, source_target_pairs={{0,12},{4,8},{8,4},{12,0},{1,13},{5,9},{9,5},{13,1},{2,14},{6,10},... | collective-permute-start | bytes 294920 | tf_op jit(solution)/shard_map/ppermute | solution.py:429
  46.2 0.8 collective-permute-start.11
  46.9 1.5 %collective-permute-start.8 = (bf16[24,2048]{1,0:T(8,128)(2,1)S(1)}, bf16[24,2048]{1,0:T(8,128)(2,1)S(1)}, u32[]{:S(2)}, u32[]{:S(2)}) collective-permute-start(bf16[24,2048]{1,0:T(8,128)(2,1)S(1)} %add_convert_fusion.3.refs_0_), channel_id=1, source_target_pairs={{0,16},{16,0},{1,17},{17,1},{2,18},{18,2},{3,19},{19,3},{4,20},{20... | collective-permute-start | bytes 294920 | tf_op jit(solution)/shard_map/ppermute | solution.py:433
  48.5 3.4 %collective-permute-done.13.refs_6_ = bf16[24,2048]{1,0:T(8,128)(2,1)S(1)} collective-permute-done((bf16[24,2048]{1,0:T(8,128)(2,1)S(1)}, bf16[24,2048]{1,0:T(8,128)(2,1)S(1)}, u32[]{:S(2)}, u32[]{:S(2)}) %collective-permute-start.13) | collective-permute-done | bytes 98336 | tf_op jit(solution)/shard_map/ppermute | solution.py:429
  51.9 1.5 %collective-permute-start.14 = (bf16[24,2048]{1,0:T(8,128)(2,1)S(1)}, bf16[24,2048]{1,0:T(8,128)(2,1)S(1)}, u32[]{:S(2)}, u32[]{:S(2)}) collective-permute-start(bf16[24,2048]{1,0:T(8,128)(2,1)S(1)} %collective-permute-done.13.refs_6_), channel_id=1, source_target_pairs={{0,16},{16,0},{1,17},{17,1},{2,18},{18,2},{3,19},{19,3},{4,20},{20... | collective-permute-start | bytes 294920 | tf_op jit(solution)/shard_map/ppermute | solution.py:433
  53.4 2.1 %collective-permute-done.11.refs_4_ = bf16[24,2048]{1,0:T(8,128)(2,1)S(1)} collective-permute-done((bf16[24,2048]{1,0:T(8,128)(2,1)S(1)}, bf16[24,2048]{1,0:T(8,128)(2,1)S(1)}, u32[]{:S(2)}, u32[]{:S(2)}) %collective-permute-start.11) | collective-permute-done | bytes 98336 | tf_op jit(solution)/shard_map/ppermute | solution.py:429
  55.5 1.5 %collective-permute-start.12 = (bf16[24,2048]{1,0:T(8,128)(2,1)S(1)}, bf16[24,2048]{1,0:T(8,128)(2,1)S(1)}, u32[]{:S(2)}, u32[]{:S(2)}) collective-permute-start(bf16[24,2048]{1,0:T(8,128)(2,1)S(1)} %collective-permute-done.11.refs_4_), channel_id=1, source_target_pairs={{0,16},{16,0},{1,17},{17,1},{2,18},{18,2},{3,19},{19,3},{4,20},{20... | collective-permute-start | bytes 294920 | tf_op jit(solution)/shard_map/ppermute | solution.py:433
  57.5 5.9 %shard_map.116 = (bf16[3696,2048]{1,0:T(8,128)(2,1)S(1)}, f32[8,128]{1,0:T(8,128)}) custom-call(bf16[3696,2048]{1,0:T(8,128)(2,1)} %bitcast.64), custom_call_target="tpu_custom_call" | custom-call | bytes 30277632 | tf_op jit(solution)/shard_map/pallas_call | solution.py:48
  63.5 1.2 shard_map.115
  64.7 5.0 %shard_map.117 = (bf16[2,48,1920]{2,1,0:T(8,128)(2,1)S(1)}, bf16[2,48,1920]{2,1,0:T(8,128)(2,1)S(1)}, bf16[2,2,48,1920]{3,2,1,0:T(8,128)(2,1)S(1)}) custom-call(bf16[2048,192]{1,0:T(8,128)(2,1)S(1)} %get-tuple-element.87.scaled_ref, bf16[3696,2048]{1,0:T(8,128)(2,1)S(1)} %get-tuple-element.81.gate_ref, bf16[3696,2048]{1,0:T(8,128)(2,1)S(1)} %get-tuple-element.83.up_ref), custom_call_target="tpu_custom_call" | custom-call | flops 3019898880 | bytes 15728640 | tf_op jit(solution)/shard_map/pallas_call | solution.py:312
  69.7 2.2 %collective-permute-done.15 = bf16[2,2,48,1920]{3,2,1,0:T(8,128)(2,1)S(1)} collective-permute-done((bf16[2,2,48,1920]{3,2,1,0:T(8,128)(2,1)S(1)}, bf16[2,2,48,1920]{3,2,1,0:T(8,128)(2,1)S(1)}, u32[]{:S(2)}, u32[]{:S(2)}) %collective-permute-start.15) | collective-permute-done | bytes 737312 | tf_op jit(solution)/shard_map/ppermute | solution.py:421
  72.3 1.5 %collective-permute-start.20 = (bf16[2,48,1920]{2,1,0:T(8,128)(2,1)S(1)}, bf16[2,48,1920]{2,1,0:T(8,128)(2,1)S(1)}, u32[]{:S(2)}, u32[]{:S(2)}) collective-permute-start(bf16[2,48,1920]{2,1,0:T(8,128)(2,1)S(1)} %fusion.2), channel_id=1, source_target_pairs={{0,2},{1,3},{2,0},{3,1},{4,6},{5,7},{6,4},{7,5},{8,10},{9,11},{10,... | collective-permute-start | bytes 1105928 | tf_op jit(solution)/shard_map/ppermute | solution.py:425
  73.8 1.1 collective-permute-start.19
  74.9 5.3 %shard_map.118 = (bf16[2,48,1776]{2,1,0:T(8,128)(2,1)S(1)}, bf16[2,48,1776]{2,1,0:T(8,128)(2,1)S(1)}, bf16[2,2,48,1776]{3,2,1,0:T(8,128)(2,1)S(1)}) custom-call(bf16[2048,192]{1,0:T(8,128)(2,1)S(1)} %get-tuple-element.87.scaled_ref, bf16[3696,2048]{1,0:T(8,128)(2,1)S(1)} %get-tuple-element.81.gate_ref, bf16[3696,2048]{1,0:T(8,128)(2,1)S(1)} %get-tuple-element.83.up_ref), custom_call_target="tpu_custom_call" | custom-call | flops 2793406464 | bytes 14548992 | tf_op jit(solution)/shard_map/pallas_call | solution.py:312
  80.3 3.3 %collective-permute-done.19 = f32[48,128]{1,0:T(8,128)S(1)} collective-permute-done((f32[48,128]{1,0:T(8,128)S(1)}, f32[48,128]{1,0:T(8,128)S(1)}, u32[]{:S(2)}, u32[]{:S(2)}) %collective-permute-start.19) | collective-permute-done | bytes 24608 | tf_op jit(solution)/shard_map/ppermute | solution.py:425
  84.1 1.6 %collective-permute-start.17 = (bf16[2,48,1776]{2,1,0:T(8,128)(2,1)S(1)}, bf16[2,48,1776]{2,1,0:T(8,128)(2,1)S(1)}, u32[]{:S(2)}, u32[]{:S(2)}) collective-permute-start(bf16[2,48,1776]{2,1,0:T(8,128)(2,1)S(1)} %fusion.3), channel_id=1, source_target_pairs={{0,2},{1,3},{2,0},{3,1},{4,6},{5,7},{6,4},{7,5},{8,10},{9,11},{10,... | collective-permute-start | bytes 1022984 | tf_op jit(solution)/shard_map/ppermute | solution.py:425
  85.8 0.6 collective-permute-start.22
  86.4 5.3 %shard_map.119 = (bf16[3696,2048]{1,0:T(8,128)(2,1)S(1)}, f32[8,128]{1,0:T(8,128)S(1)}) custom-call(bf16[3696,2048]{1,0:T(8,128)(2,1)} %source.1), custom_call_target="tpu_custom_call" | custom-call | bytes 30277632 | tf_op jit(solution)/shard_map/pallas_call | solution.py:48
  92.2 0.7 broadcast_add_fusion
  92.9 4.7 %collective-permute-done.22.refs_1_ = bf16[48,1920]{1,0:T(8,128)(2,1)S(1)} collective-permute-done((bf16[48,1920]{1,0:T(8,128)(2,1)S(1)}, bf16[48,1920]{1,0:T(8,128)(2,1)S(1)}, u32[]{:S(2)}, u32[]{:S(2)}) %collective-permute-start.22) | collective-permute-done | bytes 184352 | tf_op jit(solution)/shard_map/ppermute | solution.py:425
  97.9 1.6 %collective-permute-start.21 = (bf16[48,1776]{1,0:T(8,128)(2,1)S(1)}, bf16[48,1776]{1,0:T(8,128)(2,1)S(1)}, u32[]{:S(2)}, u32[]{:S(2)}) collective-permute-start(bf16[48,1776]{1,0:T(8,128)(2,1)S(1)} %fusion.9.refs_0_), channel_id=1, source_target_pairs={{0,2},{1,3},{2,0},{3,1},{4,6},{5,7},{6,4},{7,5},{8,10},{9,11},{10,... | collective-permute-start | bytes 511496 | tf_op jit(solution)/shard_map/ppermute | solution.py:425
  99.4 3.4 %shard_map.120.refs_5_ = f32[4,48,2048]{2,1,0:T(8,128)S(1)} custom-call(s32[6]{0:T(128)S(1)} %stack.27.scalars, bf16[48,1920]{1,0:T(8,128)(2,1)S(1)} %fusion.7.refs_0_, bf16[48,1920]{1,0:T(8,128)(2,1)S(1)} %collective-permute-done.22.refs_1_, bf16[48,1920]{1,0:T(8,128)(2,1)S(1)} %collective-permute-done.23.refs_2_, ...), custom_call_target="tpu_custom_call" | custom-call | flops 1509949440 | bytes 7864320 | tf_op jit(solution)/shard_map/pallas_call | solution.py:402
  103.2 1.5 %collective-permute-done.21.refs_1_ = bf16[48,1776]{1,0:T(8,128)(2,1)S(1)} collective-permute-done((bf16[48,1776]{1,0:T(8,128)(2,1)S(1)}, bf16[48,1776]{1,0:T(8,128)(2,1)S(1)}, u32[]{:S(2)}, u32[]{:S(2)}) %collective-permute-start.21) | collective-permute-done | bytes 170528 | tf_op jit(solution)/shard_map/ppermute | solution.py:425
  104.7 1.4 %collective-permute-done.26.refs_3_ = bf16[48,1776]{1,0:T(8,128)(2,1)S(1)} collective-permute-done((bf16[48,1776]{1,0:T(8,128)(2,1)S(1)}, bf16[48,1776]{1,0:T(8,128)(2,1)S(1)}, u32[]{:S(2)}, u32[]{:S(2)}) %collective-permute-start.26) | collective-permute-done | bytes 170528 | tf_op jit(solution)/shard_map/ppermute | solution.py:421
  106.1 3.3 %shard_map.121 = (f32[24,2048]{1,0:T(8,128)S(1)}, bf16[24,2048]{1,0:T(8,128)(2,1)S(1)}, f32[24,2048]{1,0:T(8,128)S(1)}, bf16[24,2048]{1,0:T(8,128)(2,1)S(1)}, f3...) custom-call(s32[6]{0:T(128)S(1)} %stack.27.scalars, ...), custom_call_target="tpu_custom_call" | custom-call | flops 1396703232 | bytes 7274496 | tf_op jit(solution)/shard_map/pallas_call | solution.py:402
  109.4 1.6 %collective-permute-start.27 = (bf16[24,2048]{1,0:T(8,128)(2,1)S(1)}, bf16[24,2048]{1,0:T(8,128)(2,1)S(1)}, u32[]{:S(2)}, u32[]{:S(2)}) collective-permute-start(bf16[24,2048]{1,0:T(8,128)(2,1)S(1)} %get-tuple-element.102), channel_id=1, source_target_pairs={{0,16},{16,0},{1,17},{17,1},{2,18},{18,2},{3,19},{19,3},{4,20},{20... | collective-permute-start | bytes 294920 | tf_op jit(solution)/shard_map/ppermute | solution.py:433
  111.5 1.5 %collective-permute-start.31 = (bf16[24,2048]{1,0:T(8,128)(2,1)S(1)}, bf16[24,2048]{1,0:T(8,128)(2,1)S(1)}, u32[]{:S(2)}, u32[]{:S(2)}) collective-permute-start(bf16[24,2048]{1,0:T(8,128)(2,1)S(1)} %get-tuple-element.106), channel_id=1, source_target_pairs={{0,16},{16,0},{1,17},{17,1},{2,18},{18,2},{3,19},{19,3},{4,20},{20... | collective-permute-start | bytes 294920 | tf_op jit(solution)/shard_map/ppermute | solution.py:433
  113.5 1.6 %collective-permute-done.27 = bf16[24,2048]{1,0:T(8,128)(2,1)S(1)} collective-permute-done((bf16[24,2048]{1,0:T(8,128)(2,1)S(1)}, bf16[24,2048]{1,0:T(8,128)(2,1)S(1)}, u32[]{:S(2)}, u32[]{:S(2)}) %collective-permute-start.27) | collective-permute-done | bytes 98336 | tf_op jit(solution)/shard_map/ppermute | solution.py:433
  115.1 2.1 %collective-permute-start.28 = (bf16[24,2048]{1,0:T(8,128)(2,1)S(1)}, bf16[24,2048]{1,0:T(8,128)(2,1)S(1)}, u32[]{:S(2)}, u32[]{:S(2)}) collective-permute-start(bf16[24,2048]{1,0:T(8,128)(2,1)S(1)} %add_convert_fusion.2), channel_id=1, source_target_pairs={{0,12},{4,8},{8,4},{12,0},{1,13},{5,9},{9,5},{13,1},{2,14},{6,10},... | collective-permute-start | bytes 294920 | tf_op jit(solution)/shard_map/ppermute | solution.py:429
  117.3 1.7 %collective-permute-start.30 = (bf16[24,2048]{1,0:T(8,128)(2,1)S(1)}, bf16[24,2048]{1,0:T(8,128)(2,1)S(1)}, u32[]{:S(2)}, u32[]{:S(2)}) collective-permute-start(bf16[24,2048]{1,0:T(8,128)(2,1)S(1)} %add_convert_fusion.1), channel_id=1, source_target_pairs={{0,8},{4,12},{8,0},{12,4},{1,9},{5,13},{9,1},{13,5},{2,10},{6,14},... | collective-permute-start | bytes 294920 | tf_op jit(solution)/shard_map/ppermute | solution.py:429
  119.4 1.0 collective-permute-start.32
  120.6 1.5 %collective-permute-done.28 = bf16[24,2048]{1,0:T(8,128)(2,1)S(1)} collective-permute-done((bf16[24,2048]{1,0:T(8,128)(2,1)S(1)}, bf16[24,2048]{1,0:T(8,128)(2,1)S(1)}, u32[]{:S(2)}, u32[]{:S(2)}) %collective-permute-start.28) | collective-permute-done | bytes 98336 | tf_op jit(solution)/shard_map/ppermute | solution.py:429
  122.2 3.4 %collective-permute-done.30 = bf16[24,2048]{1,0:T(8,128)(2,1)S(1)} collective-permute-done((bf16[24,2048]{1,0:T(8,128)(2,1)S(1)}, bf16[24,2048]{1,0:T(8,128)(2,1)S(1)}, u32[]{:S(2)}, u32[]{:S(2)}) %collective-permute-start.30) | collective-permute-done | bytes 98336 | tf_op jit(solution)/shard_map/ppermute | solution.py:429
  125.6 0.7 select_convert_fusion
  (61 shorter events, 6.3 us)
Async XLA Ops:
  13.6 1.7 %collective-permute-start = (bf16[96,1024]{1,0:T(8,128)(2,1)S(1)}, bf16[96,1024]{1,0:T(8,128)(2,1)S(1)}, u32[]{:S(2)}, u32[]{:S(2)}) collective-permute-start(bf16[96,1024]{1,0:T(8,128)(2,1)S(1)} %get-tuple-element.60), channel_id=1, source_target_pairs={{0,1},{1,0},{2,3},{3,2},{4,5},{5,4},{6,7},{7,6},{8,9},{9,8},{10,11... | collective-permute-start | bytes 589832 | tf_op jit(solution)/shard_map/ppermute | solution.py:421
  14.2 1.2 collective-permute-start.1
  15.8 8.2 %collective-permute-start.2 = (bf16[96,1024]{1,0:T(8,128)(2,1)S(1)}, bf16[96,1024]{1,0:T(8,128)(2,1)S(1)}, u32[]{:S(2)}, u32[]{:S(2)}) collective-permute-start(bf16[96,1024]{1,0:T(8,128)(2,1)S(1)} %get-tuple-element.64.a_ref), channel_id=1, source_target_pairs={{0,2},{1,3},{2,0},{3,1},{4,6},{5,7},{6,4},{7,5},{8,10},{9,11},{10,... | collective-permute-start | bytes 589832 | tf_op jit(solution)/shard_map/ppermute | solution.py:425
  18.6 38.9 %copy-start = (bf16[2048]{0:T(1024)(128)(2,1)S(1)}, bf16[2048]{0:T(1024)(128)(2,1)}, u32[]{:S(2)}) copy-start(bf16[2048]{0:T(1024)(128)(2,1)} %param.18) | copy-start | bytes 12292
  18.6 5.4 %collective-permute-start.3 = (f32[8,128]{1,0:T(8,128)S(1)}, f32[8,128]{1,0:T(8,128)S(1)}, u32[]{:S(2)}, u32[]{:S(2)}) collective-permute-start(f32[8,128]{1,0:T(8,128)S(1)} %get-tuple-element.65.lse_a_ref), channel_id=1, source_target_pairs={{0,2},{1,3},{2,0},{3,1},{4,6},{5,7},{6,4},{7,5},{8,10},{9,11},{10,... | collective-permute-start | bytes 12296 | tf_op jit(solution)/shard_map/ppermute | solution.py:425
  24.9 1.4 %collective-permute-start.4 = (bf16[96,1024]{1,0:T(8,128)(2,1)S(1)}, bf16[96,1024]{1,0:T(8,128)(2,1)S(1)}, u32[]{:S(2)}, u32[]{:S(2)}) collective-permute-start(bf16[96,1024]{1,0:T(8,128)(2,1)S(1)} %get-tuple-element.68.keep_ref), channel_id=1, source_target_pairs={{0,1},{1,0},{2,3},{3,2},{4,5},{5,4},{6,7},{7,6},{8,9},{9,8},{10,11... | collective-permute-start | bytes 589832 | tf_op jit(solution)/shard_map/ppermute | solution.py:421
  29.0 10.3 %collective-permute-start.5 = (bf16[24,2048]{1,0:T(8,128)(2,1)S(1)}, bf16[24,2048]{1,0:T(8,128)(2,1)S(1)}, u32[]{:S(2)}, u32[]{:S(2)}) collective-permute-start(bf16[24,2048]{1,0:T(8,128)(2,1)S(1)} %get-tuple-element.75), channel_id=1, source_target_pairs={{0,4},{4,0},{8,12},{12,8},{1,5},{5,1},{9,13},{13,9},{2,6},{6,2},{1... | collective-permute-start | bytes 294920 | tf_op jit(solution)/shard_map/ppermute | solution.py:429
  30.9 8.4 %collective-permute-start.6 = (bf16[24,2048]{1,0:T(8,128)(2,1)S(1)}, bf16[24,2048]{1,0:T(8,128)(2,1)S(1)}, u32[]{:S(2)}, u32[]{:S(2)}) collective-permute-start(bf16[24,2048]{1,0:T(8,128)(2,1)S(1)} %get-tuple-element.76), channel_id=1, source_target_pairs={{0,12},{4,8},{8,4},{12,0},{1,13},{5,9},{9,5},{13,1},{2,14},{6,10},... | collective-permute-start | bytes 294920 | tf_op jit(solution)/shard_map/ppermute | solution.py:429
  33.4 9.3 %collective-permute-start.7 = (bf16[24,2048]{1,0:T(8,128)(2,1)S(1)}, bf16[24,2048]{1,0:T(8,128)(2,1)S(1)}, u32[]{:S(2)}, u32[]{:S(2)}) collective-permute-start(bf16[24,2048]{1,0:T(8,128)(2,1)S(1)} %get-tuple-element.77), channel_id=1, source_target_pairs={{0,8},{4,12},{8,0},{12,4},{1,9},{5,13},{9,1},{13,5},{2,10},{6,14},... | collective-permute-start | bytes 294920 | tf_op jit(solution)/shard_map/ppermute | solution.py:429
  43.4 5.1 %collective-permute-start.9 = (bf16[24,2048]{1,0:T(8,128)(2,1)S(1)}, bf16[24,2048]{1,0:T(8,128)(2,1)S(1)}, u32[]{:S(2)}, u32[]{:S(2)}) collective-permute-start(bf16[24,2048]{1,0:T(8,128)(2,1)S(1)} %add_convert_fusion.3.refs_0_), channel_id=1, source_target_pairs={{0,4},{4,0},{8,12},{12,8},{1,5},{5,1},{9,13},{13,9},{2,6},{6,2},{1... | collective-permute-start | bytes 294920 | tf_op jit(solution)/shard_map/ppermute | solution.py:429
  43.5 8.4 %collective-permute-start.13 = (bf16[24,2048]{1,0:T(8,128)(2,1)S(1)}, bf16[24,2048]{1,0:T(8,128)(2,1)S(1)}, u32[]{:S(2)}, u32[]{:S(2)}) collective-permute-start(bf16[24,2048]{1,0:T(8,128)(2,1)S(1)} %add_convert_fusion.3.refs_0_), channel_id=1, source_target_pairs={{0,12},{4,8},{8,4},{12,0},{1,13},{5,9},{9,5},{13,1},{2,14},{6,10},... | collective-permute-start | bytes 294920 | tf_op jit(solution)/shard_map/ppermute | solution.py:429
  46.2 9.3 %collective-permute-start.11 = (bf16[24,2048]{1,0:T(8,128)(2,1)S(1)}, bf16[24,2048]{1,0:T(8,128)(2,1)S(1)}, u32[]{:S(2)}, u32[]{:S(2)}) collective-permute-start(bf16[24,2048]{1,0:T(8,128)(2,1)S(1)} %add_convert_fusion.3.refs_0_), channel_id=1, source_target_pairs={{0,8},{4,12},{8,0},{12,4},{1,9},{5,13},{9,1},{13,5},{2,10},{6,14},... | collective-permute-start | bytes 294920 | tf_op jit(solution)/shard_map/ppermute | solution.py:429
  46.9 16.5 %collective-permute-start.8 = (bf16[24,2048]{1,0:T(8,128)(2,1)S(1)}, bf16[24,2048]{1,0:T(8,128)(2,1)S(1)}, u32[]{:S(2)}, u32[]{:S(2)}) collective-permute-start(bf16[24,2048]{1,0:T(8,128)(2,1)S(1)} %add_convert_fusion.3.refs_0_), channel_id=1, source_target_pairs={{0,16},{16,0},{1,17},{17,1},{2,18},{18,2},{3,19},{19,3},{4,20},{20... | collective-permute-start | bytes 294920 | tf_op jit(solution)/shard_map/ppermute | solution.py:433
  51.9 11.6 %collective-permute-start.14 = (bf16[24,2048]{1,0:T(8,128)(2,1)S(1)}, bf16[24,2048]{1,0:T(8,128)(2,1)S(1)}, u32[]{:S(2)}, u32[]{:S(2)}) collective-permute-start(bf16[24,2048]{1,0:T(8,128)(2,1)S(1)} %collective-permute-done.13.refs_6_), channel_id=1, source_target_pairs={{0,16},{16,0},{1,17},{17,1},{2,18},{18,2},{3,19},{19,3},{4,20},{20... | collective-permute-start | bytes 294920 | tf_op jit(solution)/shard_map/ppermute | solution.py:433
  55.5 8.0 %collective-permute-start.12 = (bf16[24,2048]{1,0:T(8,128)(2,1)S(1)}, bf16[24,2048]{1,0:T(8,128)(2,1)S(1)}, u32[]{:S(2)}, u32[]{:S(2)}) collective-permute-start(bf16[24,2048]{1,0:T(8,128)(2,1)S(1)} %collective-permute-done.11.refs_4_), channel_id=1, source_target_pairs={{0,16},{16,0},{1,17},{17,1},{2,18},{18,2},{3,19},{19,3},{4,20},{20... | collective-permute-start | bytes 294920 | tf_op jit(solution)/shard_map/ppermute | solution.py:433
  57.0 6.5 %collective-permute-start.10 = (bf16[24,2048]{1,0:T(8,128)(2,1)S(1)}, bf16[24,2048]{1,0:T(8,128)(2,1)S(1)}, u32[]{:S(2)}, u32[]{:S(2)}) collective-permute-start(bf16[24,2048]{1,0:T(8,128)(2,1)S(1)} %collective-permute-done.9.refs_2_), channel_id=1, source_target_pairs={{0,16},{16,0},{1,17},{17,1},{2,18},{18,2},{3,19},{19,3},{4,20},{20... | collective-permute-start | bytes 294920 | tf_op jit(solution)/shard_map/ppermute | solution.py:433
  69.7 2.3 %collective-permute-start.15 = (bf16[2,2,48,1920]{3,2,1,0:T(8,128)(2,1)S(1)}, bf16[2,2,48,1920]{3,2,1,0:T(8,128)(2,1)S(1)}, u32[]{:S(2)}, u32[]{:S(2)}) collective-permute-start(bf16[2,2,48,1920]{3,2,1,0:T(8,128)(2,1)S(1)} %get-tuple-element.85), channel_id=1, source_target_pairs={{0,1},{1,0},{2,3},{3,2},{4,5},{5,4},{6,7},{7,6},{8,9},{9,8},{10,11... | collective-permute-start | bytes 2211848 | tf_op jit(solution)/shard_map/ppermute | solution.py:421
  72.1 1.7 %collective-permute-start.18 = (f32[2,48,128]{2,1,0:T(8,128)S(1)}, f32[2,48,128]{2,1,0:T(8,128)S(1)}, u32[]{:S(2)}, u32[]{:S(2)}) collective-permute-start(f32[2,48,128]{2,1,0:T(8,128)S(1)} %slice.51), channel_id=1, source_target_pairs={{0,1},{1,0},{2,3},{3,2},{4,5},{5,4},{6,7},{7,6},{8,9},{9,8},{10,11... | collective-permute-start | bytes 147464 | tf_op jit(solution)/shard_map/ppermute | solution.py:421
  72.3 11.5 %collective-permute-start.20 = (bf16[2,48,1920]{2,1,0:T(8,128)(2,1)S(1)}, bf16[2,48,1920]{2,1,0:T(8,128)(2,1)S(1)}, u32[]{:S(2)}, u32[]{:S(2)}) collective-permute-start(bf16[2,48,1920]{2,1,0:T(8,128)(2,1)S(1)} %fusion.2), channel_id=1, source_target_pairs={{0,2},{1,3},{2,0},{3,1},{4,6},{5,7},{6,4},{7,5},{8,10},{9,11},{10,... | collective-permute-start | bytes 1105928 | tf_op jit(solution)/shard_map/ppermute | solution.py:425
  73.8 9.9 %collective-permute-start.19 = (f32[48,128]{1,0:T(8,128)S(1)}, f32[48,128]{1,0:T(8,128)S(1)}, u32[]{:S(2)}, u32[]{:S(2)}) collective-permute-start(f32[48,128]{1,0:T(8,128)S(1)} %slice_bitcast_fusion.8), channel_id=1, source_target_pairs={{0,2},{1,3},{2,0},{3,1},{4,6},{5,7},{6,4},{7,5},{8,10},{9,11},{10,... | collective-permute-start | bytes 73736 | tf_op jit(solution)/shard_map/ppermute | solution.py:425
  80.2 3.7 %collective-permute-start.16 = (bf16[2,2,48,1776]{3,2,1,0:T(8,128)(2,1)S(1)}, bf16[2,2,48,1776]{3,2,1,0:T(8,128)(2,1)S(1)}, u32[]{:S(2)}, u32[]{:S(2)}) collective-permute-start(bf16[2,2,48,1776]{3,2,1,0:T(8,128)(2,1)S(1)} %get-tuple-element.89), channel_id=1, source_target_pairs={{0,1},{1,0},{2,3},{3,2},{4,5},{5,4},{6,7},{7,6},{8,9},{9,8},{10,11... | collective-permute-start | bytes 2045960 | tf_op jit(solution)/shard_map/ppermute | solution.py:421
  84.1 13.5 %collective-permute-start.17 = (bf16[2,48,1776]{2,1,0:T(8,128)(2,1)S(1)}, bf16[2,48,1776]{2,1,0:T(8,128)(2,1)S(1)}, u32[]{:S(2)}, u32[]{:S(2)}) collective-permute-start(bf16[2,48,1776]{2,1,0:T(8,128)(2,1)S(1)} %fusion.3), channel_id=1, source_target_pairs={{0,2},{1,3},{2,0},{3,1},{4,6},{5,7},{6,4},{7,5},{8,10},{9,11},{10,... | collective-permute-start | bytes 1022984 | tf_op jit(solution)/shard_map/ppermute | solution.py:425
  85.7 13.7 %collective-permute-start.23 = (bf16[48,1920]{1,0:T(8,128)(2,1)S(1)}, bf16[48,1920]{1,0:T(8,128)(2,1)S(1)}, u32[]{:S(2)}, u32[]{:S(2)}) collective-permute-start(bf16[48,1920]{1,0:T(8,128)(2,1)S(1)} %fusion.7.refs_0_), channel_id=1, source_target_pairs={{0,1},{1,0},{2,3},{3,2},{4,5},{5,4},{6,7},{7,6},{8,9},{9,8},{10,11... | collective-permute-start | bytes 552968 | tf_op jit(solution)/shard_map/ppermute | solution.py:421
  85.8 11.8 %collective-permute-start.22 = (bf16[48,1920]{1,0:T(8,128)(2,1)S(1)}, bf16[48,1920]{1,0:T(8,128)(2,1)S(1)}, u32[]{:S(2)}, u32[]{:S(2)}) collective-permute-start(bf16[48,1920]{1,0:T(8,128)(2,1)S(1)} %fusion.7.refs_0_), channel_id=1, source_target_pairs={{0,2},{1,3},{2,0},{3,1},{4,6},{5,7},{6,4},{7,5},{8,10},{9,11},{10,... | collective-permute-start | bytes 552968 | tf_op jit(solution)/shard_map/ppermute | solution.py:425
  97.6 1.8 %collective-permute-start.24 = (bf16[48,1920]{1,0:T(8,128)(2,1)S(1)}, bf16[48,1920]{1,0:T(8,128)(2,1)S(1)}, u32[]{:S(2)}, u32[]{:S(2)}) collective-permute-start(bf16[48,1920]{1,0:T(8,128)(2,1)S(1)} %collective-permute-done.22.refs_1_), channel_id=1, source_target_pairs={{0,1},{1,0},{2,3},{3,2},{4,5},{5,4},{6,7},{7,6},{8,9},{9,8},{10,11... | collective-permute-start | bytes 552968 | tf_op jit(solution)/shard_map/ppermute | solution.py:421
  97.9 6.9 %collective-permute-start.21 = (bf16[48,1776]{1,0:T(8,128)(2,1)S(1)}, bf16[48,1776]{1,0:T(8,128)(2,1)S(1)}, u32[]{:S(2)}, u32[]{:S(2)}) collective-permute-start(bf16[48,1776]{1,0:T(8,128)(2,1)S(1)} %fusion.9.refs_0_), channel_id=1, source_target_pairs={{0,2},{1,3},{2,0},{3,1},{4,6},{5,7},{6,4},{7,5},{8,10},{9,11},{10,... | collective-permute-start | bytes 511496 | tf_op jit(solution)/shard_map/ppermute | solution.py:425
  102.9 1.8 %collective-permute-start.25 = (bf16[48,1776]{1,0:T(8,128)(2,1)S(1)}, bf16[48,1776]{1,0:T(8,128)(2,1)S(1)}, u32[]{:S(2)}, u32[]{:S(2)}) collective-permute-start(bf16[48,1776]{1,0:T(8,128)(2,1)S(1)} %fusion.9.refs_0_), channel_id=1, source_target_pairs={{0,1},{1,0},{2,3},{3,2},{4,5},{5,4},{6,7},{7,6},{8,9},{9,8},{10,11... | collective-permute-start | bytes 511496 | tf_op jit(solution)/shard_map/ppermute | solution.py:421
  104.7 1.4 %collective-permute-start.26 = (bf16[48,1776]{1,0:T(8,128)(2,1)S(1)}, bf16[48,1776]{1,0:T(8,128)(2,1)S(1)}, u32[]{:S(2)}, u32[]{:S(2)}) collective-permute-start(bf16[48,1776]{1,0:T(8,128)(2,1)S(1)} %collective-permute-done.21.refs_1_), channel_id=1, source_target_pairs={{0,1},{1,0},{2,3},{3,2},{4,5},{5,4},{6,7},{7,6},{8,9},{9,8},{10,11... | collective-permute-start | bytes 511496 | tf_op jit(solution)/shard_map/ppermute | solution.py:421
  109.4 5.7 %collective-permute-start.27 = (bf16[24,2048]{1,0:T(8,128)(2,1)S(1)}, bf16[24,2048]{1,0:T(8,128)(2,1)S(1)}, u32[]{:S(2)}, u32[]{:S(2)}) collective-permute-start(bf16[24,2048]{1,0:T(8,128)(2,1)S(1)} %get-tuple-element.102), channel_id=1, source_target_pairs={{0,16},{16,0},{1,17},{17,1},{2,18},{18,2},{3,19},{19,3},{4,20},{20... | collective-permute-start | bytes 294920 | tf_op jit(solution)/shard_map/ppermute | solution.py:433
  111.0 6.2 %collective-permute-start.29 = (bf16[24,2048]{1,0:T(8,128)(2,1)S(1)}, bf16[24,2048]{1,0:T(8,128)(2,1)S(1)}, u32[]{:S(2)}, u32[]{:S(2)}) collective-permute-start(bf16[24,2048]{1,0:T(8,128)(2,1)S(1)} %get-tuple-element.104), channel_id=1, source_target_pairs={{0,16},{16,0},{1,17},{17,1},{2,18},{18,2},{3,19},{19,3},{4,20},{20... | collective-permute-start | bytes 294920 | tf_op jit(solution)/shard_map/ppermute | solution.py:433
  111.5 7.8 %collective-permute-start.31 = (bf16[24,2048]{1,0:T(8,128)(2,1)S(1)}, bf16[24,2048]{1,0:T(8,128)(2,1)S(1)}, u32[]{:S(2)}, u32[]{:S(2)}) collective-permute-start(bf16[24,2048]{1,0:T(8,128)(2,1)S(1)} %get-tuple-element.106), channel_id=1, source_target_pairs={{0,16},{16,0},{1,17},{17,1},{2,18},{18,2},{3,19},{19,3},{4,20},{20... | collective-permute-start | bytes 294920 | tf_op jit(solution)/shard_map/ppermute | solution.py:433
  113.0 7.6 %collective-permute-start.33 = (bf16[24,2048]{1,0:T(8,128)(2,1)S(1)}, bf16[24,2048]{1,0:T(8,128)(2,1)S(1)}, u32[]{:S(2)}, u32[]{:S(2)}) collective-permute-start(bf16[24,2048]{1,0:T(8,128)(2,1)S(1)} %get-tuple-element.108), channel_id=1, source_target_pairs={{0,16},{16,0},{1,17},{17,1},{2,18},{18,2},{3,19},{19,3},{4,20},{20... | collective-permute-start | bytes 294920 | tf_op jit(solution)/shard_map/ppermute | solution.py:433
  115.1 7.0 %collective-permute-start.28 = (bf16[24,2048]{1,0:T(8,128)(2,1)S(1)}, bf16[24,2048]{1,0:T(8,128)(2,1)S(1)}, u32[]{:S(2)}, u32[]{:S(2)}) collective-permute-start(bf16[24,2048]{1,0:T(8,128)(2,1)S(1)} %add_convert_fusion.2), channel_id=1, source_target_pairs={{0,12},{4,8},{8,4},{12,0},{1,13},{5,9},{9,5},{13,1},{2,14},{6,10},... | collective-permute-start | bytes 294920 | tf_op jit(solution)/shard_map/ppermute | solution.py:429
  117.3 8.3 %collective-permute-start.30 = (bf16[24,2048]{1,0:T(8,128)(2,1)S(1)}, bf16[24,2048]{1,0:T(8,128)(2,1)S(1)}, u32[]{:S(2)}, u32[]{:S(2)}) collective-permute-start(bf16[24,2048]{1,0:T(8,128)(2,1)S(1)} %add_convert_fusion.1), channel_id=1, source_target_pairs={{0,8},{4,12},{8,0},{12,4},{1,9},{5,13},{9,1},{13,5},{2,10},{6,14},... | collective-permute-start | bytes 294920 | tf_op jit(solution)/shard_map/ppermute | solution.py:429
  119.4 6.2 %collective-permute-start.32 = (bf16[24,2048]{1,0:T(8,128)(2,1)S(1)}, bf16[24,2048]{1,0:T(8,128)(2,1)S(1)}, u32[]{:S(2)}, u32[]{:S(2)}) collective-permute-start(bf16[24,2048]{1,0:T(8,128)(2,1)S(1)} %add_convert_fusion), channel_id=1, source_target_pairs={{0,4},{4,0},{8,12},{12,8},{1,5},{5,1},{9,13},{13,9},{2,6},{6,2},{1... | collective-permute-start | bytes 294920 | tf_op jit(solution)/shard_map/ppermute | solution.py:429

commit v3 on v2

--- a/solution.py
+++ b/solution.py
@@ -12,10 +12,11 @@
 TILE = 640
 CHUNKS = (3, 3)
 HEADS = 4
+THIN = 1
 NEGATIVE = -1e30
 BF16 = jnp.bfloat16
 F32 = jnp.float32
-LIMIT = 16 * 1024 * 1024
+LIMIT = 8 * 1024 * 1024
 ORDER = (0, 2, 1, 3)
 
 
@@ -28,36 +29,46 @@
 
 
 def cost(flops, moved, exps=0):
-    return pl.CostEstimate(flops=int(flops), bytes_accessed=int(moved), transcendentals=int(exps))
+    return pl.CostEstimate(
+        flops=int(flops) // THIN, bytes_accessed=int(moved) // THIN, transcendentals=int(exps) // THIN
+    )
 
 
 def whole(shape):
     return pl.BlockSpec(shape, lambda *unused: (0,) * len(shape))
 
 
-def fetch_kernel(source, target, zero, done):
-    copy = pltpu.make_async_copy(source, target, done)
-    copy.start()
-    zero[...] = jnp.zeros_like(zero)
-    copy.wait()
-
-
-def fetch(weight, after):
-    weight, after = lax.optimization_barrier((weight, after))
-    weight = pltpu.with_memory_space_constraint(weight, pltpu.HBM)
-    held, zero = pl.pallas_call(
-        fetch_kernel,
-        in_specs=[pl.BlockSpec(memory_space=pltpu.HBM)],
-        out_specs=[pl.BlockSpec(memory_space=pltpu.VMEM)] * 2,
-        out_shape=[
-            jax.ShapeDtypeStruct(weight.shape, weight.dtype),
-            jax.ShapeDtypeStruct((8, 128), F32),
-        ],
-        scratch_shapes=[pltpu.SemaphoreType.DMA],
+def fetch_kernel(pieces, *refs):
+    count = len(pieces)
+    sources, targets, mark, done = refs[:count], refs[count : 2 * count], refs[-2], refs[-1]
+    copies = []
+    for i, (begin, width) in enumerate(pieces):
+        source = sources[i].at[pl.ds(begin, width)]
+        copies.append(pltpu.make_async_copy(source, targets[i], done.at[i]))
+    for copy in copies:
+        copy.start()
+    mark[...] = jnp.zeros_like(mark)
+    for copy in copies:
+        copy.wait()
+
+
+def fetch(weights, pieces, after):
+    *weights, after = lax.optimization_barrier((*weights, after))
+    weights = [pltpu.with_memory_space_constraint(weight, pltpu.HBM) for weight in weights]
+    shapes = [
+        jax.ShapeDtypeStruct((width, weight.shape[1]), weight.dtype)
+        for weight, (begin, width) in zip(weights, pieces)
+    ]
+    *held, mark = pl.pallas_call(
+        functools.partial(fetch_kernel, pieces),
+        in_specs=[pl.BlockSpec(memory_space=pltpu.HBM)] * len(weights),
+        out_specs=[pl.BlockSpec(memory_space=pltpu.VMEM)] * (len(weights) + 1),
+        out_shape=shapes + [jax.ShapeDtypeStruct((8, 128), F32)],
+        scratch_shapes=[pltpu.SemaphoreType.DMA((len(weights),))],
         compiler_params=params(),
-        cost_estimate=cost(0, 2 * weight.size * 2),
-    )(weight)
-    return held, zero, after
+        cost_estimate=cost(0, 4 * sum(shape.size for shape in shapes)),
+    )(*weights)
+    return held, mark, after
 
 
 def attention_kernel(
@@ -156,7 +167,8 @@
     return call(scalars, queries, kv_cache, kv_cache, new_kv, new_kv)
 
 
-def combine_kernel(a_ref, b_ref, lse_a_ref, lse_b_ref, out_ref, lse_ref):
+def combine_kernel(a_ref, b_ref, lse_a_ref, lse_b_ref, *rest):
+    out_ref, lse_ref = rest[-2:]
     span = a_ref.shape[0]
     heads = lse_a_ref.shape[0]
     lse_a, lse_b = lse_a_ref[...], lse_b_ref[...]
@@ -173,7 +185,7 @@
         out_ref[:, cols] = mixed.astype(BF16)
 
 
-def combine(a, b, lse_a, lse_b):
+def combine(a, b, lse_a, lse_b, *behind):
     return pl.pallas_call(
         combine_kernel,
         out_shape=[
@@ -182,7 +194,7 @@
         ],
         compiler_params=params(),
         cost_estimate=cost(4 * a.size, 6 * a.size),
-    )(a, b, lse_a, lse_b)
+    )(a, b, lse_a, lse_b, *behind)
 
 
 def project_kernel(scalars, keep_ref, other_ref, weight_ref, *rest):
@@ -249,9 +261,38 @@
     )(scalars, keep, other, out_weight)
 
 
+def residual_kernel(scalars, resid_ref, first_ref, *rest):
+    out_ref, spread = rest[-2:]
+    rows = out_ref.shape[0]
+    spread[...] = resid_ref[...].astype(F32)
+    total = first_ref[...] + spread[pl.ds(pl.multiple_of(scalars[4] * rows, 8), rows), :]
+    for term in rest[:3]:
+        total += term[...].astype(F32)
+    out_ref[...] = total.astype(BF16)
+
+
+def add_residual(scalars, resid, first, others, *behind):
+    shape = first.shape
+    ins = [resid, first, *others, *behind]
+    return pl.pallas_call(
+        residual_kernel,
+        grid_spec=pltpu.PrefetchScalarGridSpec(
+            num_scalar_prefetch=1,
+            grid=(1,),
+            in_specs=[whole(part.shape) for part in ins],
+            out_specs=whole(shape),
+            scratch_shapes=[pltpu.VMEM(resid.shape, F32)],
+        ),
+        out_shape=jax.ShapeDtypeStruct(shape, BF16),
+        compiler_params=params(),
+        cost_estimate=cost(5 * first.size, 12 * first.size),
+    )(scalars, *ins)
+
+
 def scale_kernel(slots, scalars, *refs):
     count = 4 * slots
-    sources, gain_ref, scaled_ref, square_ref, ordered = refs[:count], *refs[count:]
+    sources, gain_ref = refs[:count], refs[count]
+    scaled_ref, square_ref, ordered = refs[-3:]
     gain = gain_ref[...].astype(F32)
     cols = gain.shape[1]
     for k in range(4):
@@ -269,7 +310,7 @@
     scaled_ref[...] = jnp.transpose(tall).astype(BF16)
 
 
-def scale_rows(scalars, sources, gain):
+def scale_rows(scalars, sources, gain, mark):
     slots = len(sources) // 4
     rows, cols = sources[0].shape
     high = rows * slots
@@ -278,7 +319,7 @@
         grid_spec=pltpu.PrefetchScalarGridSpec(
             num_scalar_prefetch=1,
             grid=(1,),
-            in_specs=[whole((rows, cols))] * len(sources) + [whole((1, cols))],
+            in_specs=[whole((rows, cols))] * len(sources) + [whole((1, cols)), whole(mark.shape)],
             out_specs=[whole((cols, 4 * high)), whole((4, high, 128))],
             scratch_shapes=[pltpu.VMEM((4, high, cols), F32)],
         ),
@@ -288,31 +329,51 @@
         ],
         compiler_params=params(),
         cost_estimate=cost(4 * 4 * high * cols, 4 * 4 * high * cols),
-    )(scalars, *sources, gain)
-
-
-def gate_up_kernel(scaled_ref, gate_ref, up_ref, keep_ref, cross_ref, send_ref):
+    )(scalars, *sources, gain, mark)
+
+
+def gate_up_kernel(tiles, scaled_ref, gate_ref, up_ref, *rest):
+    keep_ref, cross_ref, send_ref = rest[-3:]
     high = keep_ref.shape[1]
-    for which, weight in enumerate((gate_ref, up_ref)):
-        term = jnp.dot(weight[...], scaled_ref[...], preferred_element_type=F32)
-        term = jnp.transpose(term).astype(BF16)
-        keep_ref[which] = term[0:high]
-        cross_ref[which] = term[high : 2 * high]
-        send_ref[0, which] = term[2 * high : 3 * high]
-        send_ref[1, which] = term[3 * high :]
-
-
-def gate_up(scaled, gate_weight, up_weight, begin, width):
+    homes = (keep_ref, cross_ref, send_ref.at[0], send_ref.at[1])
+
+    def multiply():
+        for which, weight in enumerate((gate_ref, up_ref)):
+            term = jnp.dot(weight[...], scaled_ref[...], preferred_element_type=F32)
+            term = jnp.transpose(term).astype(BF16)
+            for place, home in enumerate(homes):
+                home[which] = term[place * high : (place + 1) * high]
+
+    if len(rest) == 3:
+        multiply()
+        return
+    square_ref = rest[0]
+    step = pl.program_id(0)
+    pl.when(step < tiles)(multiply)
+
+    @pl.when(step == tiles)
+    def squares():
+        for place, home in enumerate(homes):
+            home[0, :, 0:128] = square_ref[place].astype(BF16)
+            home[1, :, 0:128] = jnp.zeros((high, 128), BF16)
+
+
+def gate_up(scaled, gate_weight, up_weight, width, squares=None):
     depth, rows = scaled.shape
     high = rows // 4
     tiles = pl.cdiv(width, TILE)
-    first = begin // TILE
-    weight = pl.BlockSpec((TILE, depth), lambda j: (first + j, 0))
+    weight = pl.BlockSpec((TILE, depth), lambda j: (jnp.minimum(j, tiles - 1), 0))
     piece = pl.BlockSpec((2, high, TILE), lambda j: (0, 0, j))
+    ins = [scaled, gate_weight, up_weight]
+    specs = [whole(scaled.shape), weight, weight]
+    if squares is not None:
+        ins.append(squares)
+        specs.append(whole(squares.shape))
+        width += 128
     return pl.pallas_call(
-        gate_up_kernel,
-        grid=(tiles,),
-        in_specs=[whole(scaled.shape), weight, weight],
+        functools.partial(gate_up_kernel, tiles),
+        grid=(tiles + len(ins) - 3,),
+        in_specs=specs,
         out_specs=[piece, piece, pl.BlockSpec((2, 2, high, TILE), lambda j: (0, 0, 0, j))],
         out_shape=[
             jax.ShapeDtypeStruct((2, high, width), BF16),
@@ -321,7 +382,41 @@
         ],
         compiler_params=params(),
         cost_estimate=cost(4 * rows * depth * width, 4 * depth * width),
-    )(scaled, gate_weight, up_weight)
+    )(*ins)
+
+
+def activate_kernel(model, width, own_norm, keep_ref, got_ref, crossed_ref, *rest):
+    def total(which, low, high):
+        value = keep_ref[which, :, low:high].astype(F32)
+        value += got_ref[0, which, :, low:high].astype(F32)
+        return value + crossed_ref[which, :, low:high].astype(F32)
+
+    if own_norm:
+        hidden_ref, norm_ref = rest[-2:]
+        squares = jnp.sum(total(0, width, width + 128), axis=1, keepdims=True)
+        norm = lax.rsqrt(squares / model + 1e-06)
+        norm_ref[...] = jnp.broadcast_to(norm, norm_ref.shape)
+    else:
+        hidden_ref = rest[-1]
+        norm = rest[0][:, 0:1]
+    gate = total(0, 0, width) * norm
+    up = total(1, 0, width) * norm
+    hidden_ref[...] = (gate / (1.0 + jnp.exp(-gate)) * up).astype(BF16)
+
+
+def activate(model, width, keep, got, crossed, norm, *behind):
+    high = keep.shape[1]
+    shapes = [jax.ShapeDtypeStruct((high, width), BF16)]
+    if norm is None:
+        shapes.append(jax.ShapeDtypeStruct((high, 128), F32))
+    ins = [keep, got, crossed] + ([] if norm is None else [norm]) + list(behind)
+    result = pl.pallas_call(
+        functools.partial(activate_kernel, model, width, norm is None),
+        out_shape=shapes,
+        compiler_params=params(),
+        cost_estimate=cost(20 * high * width, 14 * high * width, high * width),
+    )(*ins)
+    return result if norm is None else (result[0], norm)
 
 
 def down_kernel(width, slots, has_start, last, scalars, *refs):
@@ -380,13 +475,12 @@
                 out[...] = block[s * rows : (s + 1) * rows].astype(out.dtype)
 
 
-def down(scalars, hidden, down_weight, begin, start, slots, last):
+def down(scalars, hidden, down_weight, start, slots, last):
     high, width = hidden[0].shape
     cols = down_weight.shape[1]
     steps = pl.cdiv(width, TILE)
-    first = begin // TILE
     rows = high // slots
-    ins = [whole((high, width))] * 4 + [pl.BlockSpec((TILE, cols), lambda i, s: (first + i, 0))]
+    ins = [whole((high, width))] * 4 + [pl.BlockSpec((TILE, cols), lambda i, s: (i, 0))]
     args = list(hidden) + [down_weight]
     if start is not None:
         ins.append(whole((4, high, cols)))
@@ -466,66 +560,63 @@
     usable = jnp.clip(prefixes[0] - f * cache_len, 0, cache_len)
     first = (f == 0).astype(jnp.int32)
     scalars = jnp.stack([core, usable, length, first, t, t ^ f]).astype(jnp.int32)
-    own_resid = lax.dynamic_slice_in_dim(resid, t * rows, rows, 0).astype(F32)
-    live = (t * rows + jnp.arange(rows, dtype=jnp.int32) < length)[:, None]
-    live = jnp.broadcast_to(live, (rows, 128)).astype(F32)
-    scalars, own_resid, live = lax.optimization_barrier((scalars, own_resid, live))
+    scalars = lax.optimization_barrier(scalars)
     sent, kept, sent_lse, kept_lse = attention(scalars, queries, kv_cache, new_kv)
     got, got_lse = to_core(sent), to_core(sent_lse)
     kept, kept_lse = combine(kept, got, kept_lse, got_lse)
-    out_held, zero, kept = fetch(out_weight, kept)
-    got, got_lse = to_x(kept), to_x(kept_lse) + zero
-    mine, unused = combine(kept, got, kept_lse, got_lse)
+    (out_held,), mark, kept = fetch([out_weight], [(0, out_weight.shape[0])], kept)
+    got, got_lse = to_x(kept), to_x(kept_lse)
+    mine, unused = combine(kept, got, kept_lse, got_lse, mark)
     other = to_core(mine)
 
     terms = list(project(scalars, mine, other, out_held, tp_size))
-    gate_held, zero, terms[1] = fetch(gate_weight.T, terms[1])
+    chunks = cut(gate_weight.shape[1])
+    pair = [gate_weight.T, up_weight.T]
+    (gate0, up0, gate1), mark, terms[1] = fetch(
+        pair + pair[:1], [chunks[0], chunks[0], chunks[1]], terms[1]
+    )
     passed = [to_z(terms[k], k) for k in (1, 3, 2)]
-    summed = terms[0] + own_resid + zero[0:1, 0:1]
-    for term in passed:
-        summed += term.astype(F32)
-    h1 = summed.astype(BF16)
+    h1 = add_residual(scalars, resid, terms[0], passed, mark)
 
     natural = g ^ jnp.arange(groups, dtype=jnp.int32)
-    by_z = [h1, to_z(h1, 1), to_z(h1, 2), to_z(h1, 3)]
-    up_held, unused, by_z[1] = fetch(up_weight.T, by_z[1])
+    by_z = [h1, to_z(h1, 1), to_z(h1, 2)]
+    across = None
+    if groups == 2:
+        by_z[2], across = lax.optimization_barrier((by_z[2], to_y(h1)))
+    by_z.append(to_z(by_z[2], 1))
+    (up1,), mark, by_z[1] = fetch(pair[1:], chunks[1:], by_z[1])
+    held = [(gate0, up0), (gate1, up1)]
     sources = []
     for part in by_z:
         if groups == 2:
-            sources += [part, to_y(part)]
+            sources += [part, to_y(part) if sources else across]
         else:
             everyone = jnp.take(lax.all_gather(part, "grp"), natural, axis=0)
             sources += [everyone[s] for s in range(groups)]
-    scaled, squares = scale_rows(scalars, sources, gain[None, :])
-
-    chunks = cut(gate_weight.shape[1])
+    scaled, squares = scale_rows(scalars, sources, gain[None, :], mark)
+
     reduced = []
-    for begin, width in chunks:
-        keep, cross, send = gate_up(scaled, gate_held, up_held, begin, width)
+    for index, (begin, width) in enumerate(chunks):
+        extra = squares if begin == 0 else None
+        keep, cross, send = gate_up(scaled, *held[index], width, extra)
+        if index == 0:
+            scaled, send = lax.optimization_barrier((scaled, send))
         got = to_core(send)
         cross = (cross.astype(F32) + got[1].astype(F32)).astype(BF16)
-        scaled, cross = lax.optimization_barrier((scaled, cross))
+        if index == 1:
+            held, mark, cross = fetch([down_weight] * 2, chunks, cross)
         reduced.append((keep, got, to_x(cross)))
-        if begin == 0:
-            squares, scaled = lax.optimization_barrier((squares, scaled))
-            pair = squares[0:2] + to_core(squares[2:4])
-            own_squares = pair[0] + to_x(pair[1])
-    inv_rms = lax.rsqrt(jnp.sum(own_squares, axis=1, keepdims=True) / model + 1e-06)
-    total = None
-    for index, (begin, width) in enumerate(chunks):
-        keep, got, crossed = reduced[index]
-        both = (keep.astype(F32) + got[0].astype(F32) + crossed.astype(F32)) * inv_rms
-        hidden = (jax.nn.silu(both[0]) * both[1]).astype(BF16)
-        if index == 0:
-            down_held, zero, hidden = fetch(down_weight, hidden)
-            inv_rms += zero[0:1, 0:1]
-        over = to_x(hidden)
-        if index > 0:
-            over, total = lax.optimization_barrier((over, total))
-        pieces = [hidden, over, to_core(hidden), to_core(over)]
-        is_last = index == len(chunks) - 1
-        result = down(scalars, pieces, down_held, begin, total, groups, is_last)
-        total = None if is_last else result[0]
+    first, second = (width for begin, width in chunks)
+    hidden, norm = activate(model, first, *reduced[0], None, mark)
+    over, near = to_x(hidden), to_core(hidden)
+    later, norm = activate(model, second, *reduced[1], norm, hidden)
+    far = to_x(later)
+    over, later = lax.optimization_barrier((over, later))
+    pieces = [hidden, over, near, to_core(over)]
+    (total,) = down(scalars, pieces, held[0], None, groups, False)
+    far, total = lax.optimization_barrier((far, total))
+    pieces = [later, far, to_core(later), to_core(far)]
+    result = down(scalars, pieces, held[1], total, groups, True)
 
     chunk_sums = []
     for k in range(4):
@@ -538,15 +629,21 @@
             stacked = jnp.take(stacked, natural, axis=0)
             moved = lax.all_to_all(stacked, "grp", split_axis=0, concat_axis=0, tiled=True)
             chunk_sums.append(jnp.sum(moved.astype(F32), axis=0))
-    out = h1.astype(F32)
+    parts = [h1]
     for k in (3, 2, 1, 0):
         if groups == 2:
             own, away = chunk_sums[k]
-            value = own + to_y(away).astype(F32)
+            away = to_y(away)
+            if k == 0:
+                parts += [own, away]
+                continue
+            value = own + away.astype(F32)
         else:
             value = chunk_sums[k]
-        out += value if k == 0 else to_z(value.astype(BF16), k).astype(F32)
-    return jnp.where(live[:, 0:1] > 0, out, 0.0).astype(BF16)
+        parts.append(value if k == 0 else to_z(value.astype(BF16), k))
+    total = sum(part.astype(F32) for part in parts)
+    live = t * rows + jnp.arange(rows, dtype=jnp.int32) < length
+    return jnp.where(live[:, None], total, 0.0).astype(BF16)
 
 
 def merged(x, axis, combine):

time: 127 us -> 124 us (0.976)
  other arithmetic: 3.9 us -> 0.98 us
  waiting for transfers between devices: 33.6 us -> 35.7 us
  starting transfers between devices: 32.5 us -> 30.6 us
    ppermute x7 -> x6, waiting for transfers between devices: 11.5 us -> 15.1 us  [to_x(): return lax.ppermute(x, 'ffn', [(i, i ^ 2) for i in range(4)])]
    ppermute x10 -> x9, waiting for transfers between devices: 6.14 us -> 4.05 us  [to_core(): return lax.ppermute(x, 'ffn', [(i, i ^ 1) for i in range(4)])]
    ppermute x8, waiting for transfers between devices: 2.28 us -> 4.18 us  [to_y(): return lax.ppermute(x, 'grp', [(0, 1), (1, 0)])]
    convert_element_type x9 -> x4, other arithmetic: 2.62 us -> 0.8 us  [the longest x1 0.72 us: body(): return jnp.where(live[:, None], total, 0.0).astype(BF16)]
    ppermute x9, waiting for transfers between devices: 13.7 us -> 12.4 us  [to_z(): return lax.ppermute(x, 'tp', [(i, i ^ k) for i in range(4)])]
    pallas_call x6 -> x9, Pallas kernels: 30.2 us -> 31.5 us  [the longest x4 19.4 us: fetch(): pl.pallas_call(functools.partial(fetch_kernel, pieces), in_specs=[pl.Bloc...]
    ppermute x7 -> x6, starting transfers between devices: 9.27 us -> 9.07 us  [to_x(): return lax.ppermute(x, 'ffn', [(i, i ^ 2) for i in range(4)])]
  transfers between devices with their start and end apart: 34 -> 32, of which waited for: 16 -> 19; matrix products, arithmetic and copies ran while one was open for 2% -> 0% of each run, Pallas kernels for 23% -> 23%
where the time goes in v3:
time: 124 us
  Pallas kernels  54.7 us (44%)
  waiting for transfers between devices  35.7 us (29%)
  starting transfers between devices  30.6 us (25%)
  between operations  1.5 us (1%)
    pallas_call x4, Pallas kernels, fetch(): pl.pallas_call(functools.partial(fetch_kernel, pieces), in_specs=[pl.Bloc...  19.4 us
    ppermute x6, waiting for transfers between devices, to_x(): return lax.ppermute(x, 'ffn', [(i, i ^ 2) for i in range(4)])  15.1 us
    ppermute x9, waiting for transfers between devices, to_z(): return lax.ppermute(x, 'tp', [(i, i ^ k) for i in range(4)])  12.4 us
    ppermute x9, starting transfers between devices, to_z(): return lax.ppermute(x, 'tp', [(i, i ^ k) for i in range(4)])  11.8 us
    pallas_call x1, Pallas kernels, attention(): return call(scalars, queries, kv_cache, kv_cache, new_kv, new_kv)  11.3 us
    pallas_call x2, Pallas kernels, gate_up(): pl.pallas_call(functools.partial(gate_up_kernel, tiles), grid=(tiles + le...  10.8 us
    ppermute x6, starting transfers between devices, to_x(): return lax.ppermute(x, 'ffn', [(i, i ^ 2) for i in range(4)])  9.07 us
    ppermute x8, starting transfers between devices, to_y(): return lax.ppermute(x, 'grp', [(0, 1), (1, 0)])  8.23 us
  transfers between devices with their start and end apart: 32, of which 19 were waited for; matrix products, arithmetic and copies ran while one was open for 0% of the time, Pallas kernels for 23%

profile of v3, /device:TPU:0, one launch (start us, length us, event | category | flops | bytes accessed | tf_op | source)
XLA Modules:
  0.0 123.5 jit_solution(6016440477620235194)
XLA Ops:
  1.4 11.3 %shard_map.109 = (bf16[96,1024]{1,0:T(8,128)(2,1)S(1)}, bf16[96,1024]{1,0:T(8,128)(2,1)S(1)}, f32[8,128]{1,0:T(8,128)S(1)}, f32[8,128]{1,0:T(8,128)S(1)}) custom-call(s32[6]{0:T(128)S(1)} %stack.27.scalars, bf16[96,2048]{1,0:T(8,128)(2,1)} %q_ref.1, bf16[2,1,2048,256]{3,2,1,0:T(8,128)(2,1)} %value_ref.1, bf16[2,1,2048,256]{3,2,1,0:T(8,128)(2,1)} %value_ref.1, ...), custom_call_target="tpu_custom_call" | custom-call | flops 1610612736 | bytes 2097152 | tf_op jit(solution)/shard_map/pallas_call | solution.py:167
  13.3 1.1 collective-permute-done.1.lse_b_ref
  14.8 2.8 %collective-permute-start.2 = (bf16[96,1024]{1,0:T(8,128)(2,1)S(1)}, bf16[96,1024]{1,0:T(8,128)(2,1)S(1)}, u32[]{:S(2)}, u32[]{:S(2)}) collective-permute-start(bf16[96,1024]{1,0:T(8,128)(2,1)S(1)} %get-tuple-element.69.a_ref), channel_id=1, source_target_pairs={{0,2},{1,3},{2,0},{3,1},{4,6},{5,7},{6,4},{7,5},{8,10},{9,11},{10,... | collective-permute-start | bytes 589832 | tf_op jit(solution)/shard_map/ppermute | solution.py:519
  17.7 3.4 %shard_map.111 = (bf16[2048,2048]{1,0:T(8,128)(2,1)S(1)}, f32[8,128]{1,0:T(8,128)S(1)}) custom-call(bf16[2048,2048]{1,0:T(8,128)(2,1)} %refs_0_), custom_call_target="tpu_custom_call" | custom-call | bytes 16777216 | tf_op jit(solution)/shard_map/pallas_call | solution.py:62
  21.1 1.9 %collective-permute-done.3.lse_b_ref = f32[8,128]{1,0:T(8,128)S(1)} collective-permute-done((f32[8,128]{1,0:T(8,128)S(1)}, f32[8,128]{1,0:T(8,128)S(1)}, u32[]{:S(2)}, u32[]{:S(2)}) %collective-permute-start.3) | collective-permute-done | bytes 4128 | tf_op jit(solution)/shard_map/ppermute | solution.py:519
  23.0 0.9 shard_map.112
  24.0 1.4 %collective-permute-done.4.other_ref = bf16[96,1024]{1,0:T(8,128)(2,1)S(1)} collective-permute-done((bf16[96,1024]{1,0:T(8,128)(2,1)S(1)}, bf16[96,1024]{1,0:T(8,128)(2,1)S(1)}, u32[]{:S(2)}, u32[]{:S(2)}) %collective-permute-start.4) | collective-permute-done | bytes 196640 | tf_op jit(solution)/shard_map/ppermute | solution.py:515
  25.4 2.7 %shard_map.113 = (f32[24,2048]{1,0:T(8,128)S(1)}, bf16[24,2048]{1,0:T(8,128)(2,1)S(1)}, bf16[24,2048]{1,0:T(8,128)(2,1)S(1)}, bf16[24,2048]{1,0:T(8,128)(2,1)S(1)}) custom-call(s32[6]{0:T(128)S(1)} %stack.27.scalars, bf16[96,1024]{1,0:T(8,128)(2,1)S(1)} %get-tuple-element.73.keep_ref, bf16[96,1024]{1,0:T(8,128)(2,1)S(1)} %collective-permute-done.4.other_ref, ...), custom_call_target="tpu_custom_call" | custom-call | flops 805306368 | bytes 8388608 | tf_op jit(solution)/shard_map/pallas_call | solution.py:240
  28.1 1.9 %collective-permute-start.5 = (bf16[24,2048]{1,0:T(8,128)(2,1)S(1)}, bf16[24,2048]{1,0:T(8,128)(2,1)S(1)}, u32[]{:S(2)}, u32[]{:S(2)}) collective-permute-start(bf16[24,2048]{1,0:T(8,128)(2,1)S(1)} %get-tuple-element.77), channel_id=1, source_target_pairs={{0,4},{4,0},{8,12},{12,8},{1,5},{5,1},{9,13},{13,9},{2,6},{6,2},{1... | collective-permute-start | bytes 294920 | tf_op jit(solution)/shard_map/ppermute | solution.py:523
  30.0 2.5 %collective-permute-start.6 = (bf16[24,2048]{1,0:T(8,128)(2,1)S(1)}, bf16[24,2048]{1,0:T(8,128)(2,1)S(1)}, u32[]{:S(2)}, u32[]{:S(2)}) collective-permute-start(bf16[24,2048]{1,0:T(8,128)(2,1)S(1)} %get-tuple-element.78), channel_id=1, source_target_pairs={{0,12},{4,8},{8,4},{12,0},{1,13},{5,9},{9,5},{13,1},{2,14},{6,10},... | collective-permute-start | bytes 294920 | tf_op jit(solution)/shard_map/ppermute | solution.py:523
  32.6 7.6 %shard_map.114 = (bf16[1920,2048]{1,0:T(8,128)(2,1)S(1)}, bf16[1920,2048]{1,0:T(8,128)(2,1)S(1)}, bf16[1776,2048]{1,0:T(8,128)(2,1)S(1)}, f32[8,128]{1,0:T(8,128)S(1)}) custom-call(bf16[3696,2048]{1,0:T(8,128)(2,1)} %bitcast.21, bf16[3696,2048]{1,0:T(8,128)(2,1)} %bitcast.23, bf16[3696,2048]{1,0:T(8,128)(2,1)} %bitcast.22), custom_call_target="tpu_custom_call" | custom-call | bytes 46006272 | tf_op jit(solution)/shard_map/pallas_call | solution.py:62
  40.2 1.5 %collective-permute-done.7.rest_2_ = bf16[24,2048]{1,0:T(8,128)(2,1)S(1)} collective-permute-done((bf16[24,2048]{1,0:T(8,128)(2,1)S(1)}, bf16[24,2048]{1,0:T(8,128)(2,1)S(1)}, u32[]{:S(2)}, u32[]{:S(2)}) %collective-permute-start.7) | collective-permute-done | bytes 98336 | tf_op jit(solution)/shard_map/ppermute | solution.py:523
  41.7 0.7 shard_map.115.refs_0_
  42.4 1.6 %collective-permute-start.9 = (bf16[24,2048]{1,0:T(8,128)(2,1)S(1)}, bf16[24,2048]{1,0:T(8,128)(2,1)S(1)}, u32[]{:S(2)}, u32[]{:S(2)}) collective-permute-start(bf16[24,2048]{1,0:T(8,128)(2,1)S(1)} %shard_map.115.refs_0_), channel_id=1, source_target_pairs={{0,16},{16,0},{1,17},{17,1},{2,18},{18,2},{3,19},{19,3},{4,20},{20... | collective-permute-start | bytes 294920 | tf_op jit(solution)/shard_map/ppermute | solution.py:527
  44.0 1.3 %collective-permute-start.8 = (bf16[24,2048]{1,0:T(8,128)(2,1)S(1)}, bf16[24,2048]{1,0:T(8,128)(2,1)S(1)}, u32[]{:S(2)}, u32[]{:S(2)}) collective-permute-start(bf16[24,2048]{1,0:T(8,128)(2,1)S(1)} %shard_map.115.refs_0_), channel_id=1, source_target_pairs={{0,8},{4,12},{8,0},{12,4},{1,9},{5,13},{9,1},{13,5},{2,10},{6,14},... | collective-permute-start | bytes 294920 | tf_op jit(solution)/shard_map/ppermute | solution.py:523
  45.3 1.9 %collective-permute-start.10 = (bf16[24,2048]{1,0:T(8,128)(2,1)S(1)}, bf16[24,2048]{1,0:T(8,128)(2,1)S(1)}, u32[]{:S(2)}, u32[]{:S(2)}) collective-permute-start(bf16[24,2048]{1,0:T(8,128)(2,1)S(1)} %shard_map.115.refs_0_), channel_id=1, source_target_pairs={{0,4},{4,0},{8,12},{12,8},{1,5},{5,1},{9,13},{13,9},{2,6},{6,2},{1... | collective-permute-start | bytes 294920 | tf_op jit(solution)/shard_map/ppermute | solution.py:523
  47.2 3.5 %collective-permute-done.8.refs_4_ = bf16[24,2048]{1,0:T(8,128)(2,1)S(1)} collective-permute-done((bf16[24,2048]{1,0:T(8,128)(2,1)S(1)}, bf16[24,2048]{1,0:T(8,128)(2,1)S(1)}, u32[]{:S(2)}, u32[]{:S(2)}) %collective-permute-start.8) | collective-permute-done | bytes 98336 | tf_op jit(solution)/shard_map/ppermute | solution.py:523
  51.4 1.5 %collective-permute-start.11 = (bf16[24,2048]{1,0:T(8,128)(2,1)S(1)}, bf16[24,2048]{1,0:T(8,128)(2,1)S(1)}, u32[]{:S(2)}, u32[]{:S(2)}) collective-permute-start(bf16[24,2048]{1,0:T(8,128)(2,1)S(1)} %collective-permute-done.10.refs_2_), channel_id=1, source_target_pairs={{0,16},{16,0},{1,17},{17,1},{2,18},{18,2},{3,19},{19,3},{4,20},{20... | collective-permute-start | bytes 294920 | tf_op jit(solution)/shard_map/ppermute | solution.py:527
  52.9 2.3 %collective-permute-done.13.refs_6_ = bf16[24,2048]{1,0:T(8,128)(2,1)S(1)} collective-permute-done((bf16[24,2048]{1,0:T(8,128)(2,1)S(1)}, bf16[24,2048]{1,0:T(8,128)(2,1)S(1)}, u32[]{:S(2)}, u32[]{:S(2)}) %collective-permute-start.13) | collective-permute-done | bytes 98336 | tf_op jit(solution)/shard_map/ppermute | solution.py:523
  55.8 3.1 %shard_map.116 = (bf16[1776,2048]{1,0:T(8,128)(2,1)S(1)}, f32[8,128]{1,0:T(8,128)S(1)}) custom-call(bf16[3696,2048]{1,0:T(8,128)(2,1)} %bitcast.24), custom_call_target="tpu_custom_call" | custom-call | bytes 14548992 | tf_op jit(solution)/shard_map/pallas_call | solution.py:62
  58.9 1.0 collective-permute-done.14.refs_7_
  59.9 1.2 shard_map.117
  61.1 5.5 %shard_map.118 = (bf16[2,48,2048]{2,1,0:T(8,128)(2,1)S(1)}, bf16[2,48,2048]{2,1,0:T(8,128)(2,1)S(1)}, bf16[2,2,48,2048]{3,2,1,0:T(8,128)(2,1)S(1)}) custom-call(bf16[2048,192]{1,0:T(8,128)(2,1)S(1)} %get-tuple-element.97.scaled_ref, bf16[1920,2048]{1,0:T(8,128)(2,1)S(1)} %get-tuple-element.90.gate_ref, bf16[1920,2048]{1,0:T(8,128)(2,1)S(1)} %get-tuple-element.91.up_ref, ...), custom_call_target="tpu_custom_call" | custom-call | flops 3221225472 | bytes 16777216 | tf_op jit(solution)/shard_map/pallas_call | solution.py:373
  66.7 5.3 %shard_map.119 = (bf16[2,48,1776]{2,1,0:T(8,128)(2,1)S(1)}, bf16[2,48,1776]{2,1,0:T(8,128)(2,1)S(1)}, bf16[2,2,48,1776]{3,2,1,0:T(8,128)(2,1)S(1)}) custom-call(bf16[2048,192]{1,0:T(8,128)(2,1)S(1)} %get-tuple-element.97.scaled_ref, bf16[1776,2048]{1,0:T(8,128)(2,1)S(1)} %get-tuple-element.98.gate_ref, bf16[1776,2048]{1,0:T(8,128)(2,1)S(1)} %get-tuple-element.99.up_ref), custom_call_target="tpu_custom_call" | custom-call | flops 2793406464 | bytes 14548992 | tf_op jit(solution)/shard_map/pallas_call | solution.py:373
  72.0 0.6 collective-permute-start.17
  72.6 1.6 %collective-permute-start.16 = (bf16[2,48,2048]{2,1,0:T(8,128)(2,1)S(1)}, bf16[2,48,2048]{2,1,0:T(8,128)(2,1)S(1)}, u32[]{:S(2)}, u32[]{:S(2)}) collective-permute-start(bf16[2,48,2048]{2,1,0:T(8,128)(2,1)S(1)} %fusion), channel_id=1, source_target_pairs={{0,2},{1,3},{2,0},{3,1},{4,6},{5,7},{6,4},{7,5},{8,10},{9,11},{10,... | collective-permute-start | bytes 1179656 | tf_op jit(solution)/shard_map/ppermute | solution.py:519
  74.4 1.6 %collective-permute-start.19 = (bf16[2,48,1776]{2,1,0:T(8,128)(2,1)S(1)}, bf16[2,48,1776]{2,1,0:T(8,128)(2,1)S(1)}, u32[]{:S(2)}, u32[]{:S(2)}) collective-permute-start(bf16[2,48,1776]{2,1,0:T(8,128)(2,1)S(1)} %fusion.1), channel_id=1, source_target_pairs={{0,2},{1,3},{2,0},{3,1},{4,6},{5,7},{6,4},{7,5},{8,10},{9,11},{10,... | collective-permute-start | bytes 1022984 | tf_op jit(solution)/shard_map/ppermute | solution.py:519
  76.0 5.3 %shard_map.120 = (bf16[1920,2048]{1,0:T(8,128)(2,1)S(1)}, bf16[1776,2048]{1,0:T(8,128)(2,1)S(1)}, f32[8,128]{1,0:T(8,128)S(1)}) custom-call(bf16[3696,2048]{1,0:T(8,128)(2,1)} %refs_1_, bf16[3696,2048]{1,0:T(8,128)(2,1)} %refs_1_), custom_call_target="tpu_custom_call" | custom-call | bytes 30277632 | tf_op jit(solution)/shard_map/pallas_call | solution.py:62
  81.3 3.4 %collective-permute-done.16.crossed_ref = bf16[2,48,2048]{2,1,0:T(8,128)(2,1)S(1)} collective-permute-done((bf16[2,48,2048]{2,1,0:T(8,128)(2,1)S(1)}, bf16[2,48,2048]{2,1,0:T(8,128)(2,1)S(1)}, u32[]{:S(2)}, u32[]{:S(2)}) %collective-permute-start.16) | collective-permute-done | bytes 393248 | tf_op jit(solution)/shard_map/ppermute | solution.py:519
  85.0 1.6 %collective-permute-start.18 = (bf16[48,1920]{1,0:T(8,128)(2,1)S(1)}, bf16[48,1920]{1,0:T(8,128)(2,1)S(1)}, u32[]{:S(2)}, u32[]{:S(2)}) collective-permute-start(bf16[48,1920]{1,0:T(8,128)(2,1)S(1)} %get-tuple-element.105.rest_1_.refs_0_), channel_id=1, source_target_pairs={{0,2},{1,3},{2,0},{3,1},{4,6},{5,7},{6,4},{7,5},{8,10},{9,11},{10,... | collective-permute-start | bytes 552968 | tf_op jit(solution)/shard_map/ppermute | solution.py:519
  86.6 5.5 %collective-permute-done.19.crossed_ref = bf16[2,48,1776]{2,1,0:T(8,128)(2,1)S(1)} collective-permute-done((bf16[2,48,1776]{2,1,0:T(8,128)(2,1)S(1)}, bf16[2,48,1776]{2,1,0:T(8,128)(2,1)S(1)}, u32[]{:S(2)}, u32[]{:S(2)}) %collective-permute-start.19) | collective-permute-done | bytes 341024 | tf_op jit(solution)/shard_map/ppermute | solution.py:519
  92.3 2.7 %collective-permute-done.18.refs_1_ = bf16[48,1920]{1,0:T(8,128)(2,1)S(1)} collective-permute-done((bf16[48,1920]{1,0:T(8,128)(2,1)S(1)}, bf16[48,1920]{1,0:T(8,128)(2,1)S(1)}, u32[]{:S(2)}, u32[]{:S(2)}) %collective-permute-start.18) | collective-permute-done | bytes 184352 | tf_op jit(solution)/shard_map/ppermute | solution.py:519
  95.1 1.5 %collective-permute-start.20 = (bf16[48,1776]{1,0:T(8,128)(2,1)S(1)}, bf16[48,1776]{1,0:T(8,128)(2,1)S(1)}, u32[]{:S(2)}, u32[]{:S(2)}) collective-permute-start(bf16[48,1776]{1,0:T(8,128)(2,1)S(1)} %shard_map.122.refs_0_), channel_id=1, source_target_pairs={{0,2},{1,3},{2,0},{3,1},{4,6},{5,7},{6,4},{7,5},{8,10},{9,11},{10,... | collective-permute-start | bytes 511496 | tf_op jit(solution)/shard_map/ppermute | solution.py:519
  96.8 3.4 %shard_map.123.refs_5_ = f32[4,48,2048]{2,1,0:T(8,128)S(1)} custom-call(s32[6]{0:T(128)S(1)} %stack.27.scalars, bf16[48,1920]{1,0:T(8,128)(2,1)S(1)} %get-tuple-element.105.rest_1_.refs_0_, bf16[48,1920]{1,0:T(8,128)(2,1)S(1)} %collective-permute-done.18.refs_1_, bf16[48,1920]{1,0:T(8,128)(2,1)S(1)} %collective-permute-done.21.refs_2_, ...), custom_call_target="tpu_custom_call" | custom-call | flops 1509949440 | bytes 7864320 | tf_op jit(solution)/shard_map/pallas_call | solution.py:496
  100.3 1.6 %collective-permute-done.20.refs_1_ = bf16[48,1776]{1,0:T(8,128)(2,1)S(1)} collective-permute-done((bf16[48,1776]{1,0:T(8,128)(2,1)S(1)}, bf16[48,1776]{1,0:T(8,128)(2,1)S(1)}, u32[]{:S(2)}, u32[]{:S(2)}) %collective-permute-start.20) | collective-permute-done | bytes 170528 | tf_op jit(solution)/shard_map/ppermute | solution.py:519
  101.9 1.4 %collective-permute-done.24.refs_3_ = bf16[48,1776]{1,0:T(8,128)(2,1)S(1)} collective-permute-done((bf16[48,1776]{1,0:T(8,128)(2,1)S(1)}, bf16[48,1776]{1,0:T(8,128)(2,1)S(1)}, u32[]{:S(2)}, u32[]{:S(2)}) %collective-permute-start.24) | collective-permute-done | bytes 170528 | tf_op jit(solution)/shard_map/ppermute | solution.py:515
  103.3 3.3 %shard_map.124 = (f32[24,2048]{1,0:T(8,128)S(1)}, bf16[24,2048]{1,0:T(8,128)(2,1)S(1)}, f32[24,2048]{1,0:T(8,128)S(1)}, bf16[24,2048]{1,0:T(8,128)(2,1)S(1)}, f3...) custom-call(s32[6]{0:T(128)S(1)} %stack.27.scalars, ...), custom_call_target="tpu_custom_call" | custom-call | flops 1396703232 | bytes 7274496 | tf_op jit(solution)/shard_map/pallas_call | solution.py:496
  106.5 0.6 collective-permute-start.25
  107.2 1.5 %collective-permute-start.27 = (bf16[24,2048]{1,0:T(8,128)(2,1)S(1)}, bf16[24,2048]{1,0:T(8,128)(2,1)S(1)}, u32[]{:S(2)}, u32[]{:S(2)}) collective-permute-start(bf16[24,2048]{1,0:T(8,128)(2,1)S(1)} %get-tuple-element.118), channel_id=1, source_target_pairs={{0,16},{16,0},{1,17},{17,1},{2,18},{18,2},{3,19},{19,3},{4,20},{20... | collective-permute-start | bytes 294920 | tf_op jit(solution)/shard_map/ppermute | solution.py:527
  109.2 1.5 %collective-permute-start.31 = (bf16[24,2048]{1,0:T(8,128)(2,1)S(1)}, bf16[24,2048]{1,0:T(8,128)(2,1)S(1)}, u32[]{:S(2)}, u32[]{:S(2)}) collective-permute-start(bf16[24,2048]{1,0:T(8,128)(2,1)S(1)} %get-tuple-element.122), channel_id=1, source_target_pairs={{0,16},{16,0},{1,17},{17,1},{2,18},{18,2},{3,19},{19,3},{4,20},{20... | collective-permute-start | bytes 294920 | tf_op jit(solution)/shard_map/ppermute | solution.py:527
  110.7 1.6 %collective-permute-done.25 = bf16[24,2048]{1,0:T(8,128)(2,1)S(1)} collective-permute-done((bf16[24,2048]{1,0:T(8,128)(2,1)S(1)}, bf16[24,2048]{1,0:T(8,128)(2,1)S(1)}, u32[]{:S(2)}, u32[]{:S(2)}) %collective-permute-start.25) | collective-permute-done | bytes 98336 | tf_op jit(solution)/shard_map/ppermute | solution.py:527
  112.3 2.3 %collective-permute-start.26 = (bf16[24,2048]{1,0:T(8,128)(2,1)S(1)}, bf16[24,2048]{1,0:T(8,128)(2,1)S(1)}, u32[]{:S(2)}, u32[]{:S(2)}) collective-permute-start(bf16[24,2048]{1,0:T(8,128)(2,1)S(1)} %add_convert_fusion.2), channel_id=1, source_target_pairs={{0,12},{4,8},{8,4},{12,0},{1,13},{5,9},{9,5},{13,1},{2,14},{6,10},... | collective-permute-start | bytes 294920 | tf_op jit(solution)/shard_map/ppermute | solution.py:523
  114.6 0.6 collective-permute-start.28
  115.3 1.2 collective-permute-done.29
  116.5 0.9 collective-permute-start.30
  117.8 1.6 %collective-permute-done.26 = bf16[24,2048]{1,0:T(8,128)(2,1)S(1)} collective-permute-done((bf16[24,2048]{1,0:T(8,128)(2,1)S(1)}, bf16[24,2048]{1,0:T(8,128)(2,1)S(1)}, u32[]{:S(2)}, u32[]{:S(2)}) %collective-permute-start.26) | collective-permute-done | bytes 98336 | tf_op jit(solution)/shard_map/ppermute | solution.py:523
  119.4 3.4 %collective-permute-done.28 = bf16[24,2048]{1,0:T(8,128)(2,1)S(1)} collective-permute-done((bf16[24,2048]{1,0:T(8,128)(2,1)S(1)}, bf16[24,2048]{1,0:T(8,128)(2,1)S(1)}, u32[]{:S(2)}, u32[]{:S(2)}) %collective-permute-start.28) | collective-permute-done | bytes 98336 | tf_op jit(solution)/shard_map/ppermute | solution.py:523
  122.8 0.7 select_convert_fusion
  (45 shorter events, 5.0 us)
Async XLA Ops:
  12.7 1.7 %collective-permute-start = (bf16[96,1024]{1,0:T(8,128)(2,1)S(1)}, bf16[96,1024]{1,0:T(8,128)(2,1)S(1)}, u32[]{:S(2)}, u32[]{:S(2)}) collective-permute-start(bf16[96,1024]{1,0:T(8,128)(2,1)S(1)} %get-tuple-element.65), channel_id=1, source_target_pairs={{0,1},{1,0},{2,3},{3,2},{4,5},{5,4},{6,7},{7,6},{8,9},{9,8},{10,11... | collective-permute-start | bytes 589832 | tf_op jit(solution)/shard_map/ppermute | solution.py:515
  13.2 1.2 collective-permute-start.1
  14.8 8.2 %collective-permute-start.2 = (bf16[96,1024]{1,0:T(8,128)(2,1)S(1)}, bf16[96,1024]{1,0:T(8,128)(2,1)S(1)}, u32[]{:S(2)}, u32[]{:S(2)}) collective-permute-start(bf16[96,1024]{1,0:T(8,128)(2,1)S(1)} %get-tuple-element.69.a_ref), channel_id=1, source_target_pairs={{0,2},{1,3},{2,0},{3,1},{4,6},{5,7},{6,4},{7,5},{8,10},{9,11},{10,... | collective-permute-start | bytes 589832 | tf_op jit(solution)/shard_map/ppermute | solution.py:519
  17.6 5.4 %collective-permute-start.3 = (f32[8,128]{1,0:T(8,128)S(1)}, f32[8,128]{1,0:T(8,128)S(1)}, u32[]{:S(2)}, u32[]{:S(2)}) collective-permute-start(f32[8,128]{1,0:T(8,128)S(1)} %get-tuple-element.70.lse_a_ref), channel_id=1, source_target_pairs={{0,2},{1,3},{2,0},{3,1},{4,6},{5,7},{6,4},{7,5},{8,10},{9,11},{10,... | collective-permute-start | bytes 12296 | tf_op jit(solution)/shard_map/ppermute | solution.py:519
  24.0 1.4 %collective-permute-start.4 = (bf16[96,1024]{1,0:T(8,128)(2,1)S(1)}, bf16[96,1024]{1,0:T(8,128)(2,1)S(1)}, u32[]{:S(2)}, u32[]{:S(2)}) collective-permute-start(bf16[96,1024]{1,0:T(8,128)(2,1)S(1)} %get-tuple-element.73.keep_ref), channel_id=1, source_target_pairs={{0,1},{1,0},{2,3},{3,2},{4,5},{5,4},{6,7},{7,6},{8,9},{9,8},{10,11... | collective-permute-start | bytes 589832 | tf_op jit(solution)/shard_map/ppermute | solution.py:515
  28.1 12.1 %collective-permute-start.5 = (bf16[24,2048]{1,0:T(8,128)(2,1)S(1)}, bf16[24,2048]{1,0:T(8,128)(2,1)S(1)}, u32[]{:S(2)}, u32[]{:S(2)}) collective-permute-start(bf16[24,2048]{1,0:T(8,128)(2,1)S(1)} %get-tuple-element.77), channel_id=1, source_target_pairs={{0,4},{4,0},{8,12},{12,8},{1,5},{5,1},{9,13},{13,9},{2,6},{6,2},{1... | collective-permute-start | bytes 294920 | tf_op jit(solution)/shard_map/ppermute | solution.py:523
  30.0 10.2 %collective-permute-start.6 = (bf16[24,2048]{1,0:T(8,128)(2,1)S(1)}, bf16[24,2048]{1,0:T(8,128)(2,1)S(1)}, u32[]{:S(2)}, u32[]{:S(2)}) collective-permute-start(bf16[24,2048]{1,0:T(8,128)(2,1)S(1)} %get-tuple-element.78), channel_id=1, source_target_pairs={{0,12},{4,8},{8,4},{12,0},{1,13},{5,9},{9,5},{13,1},{2,14},{6,10},... | collective-permute-start | bytes 294920 | tf_op jit(solution)/shard_map/ppermute | solution.py:523
  32.5 9.2 %copy-start = (bf16[96,2048]{1,0:T(8,128)(2,1)S(1)}, bf16[96,2048]{1,0:T(8,128)(2,1)}, u32[]{:S(2)}) copy-start(bf16[96,2048]{1,0:T(8,128)(2,1)} %resid_ref.1) | copy-start | bytes 1179652
  32.5 23.3 %copy-start.1 = (bf16[2048]{0:T(1024)(128)(2,1)S(1)}, bf16[2048]{0:T(1024)(128)(2,1)}, u32[]{:S(2)}) copy-start(bf16[2048]{0:T(1024)(128)(2,1)} %param.18) | copy-start | bytes 12292
  32.5 9.2 %collective-permute-start.7 = (bf16[24,2048]{1,0:T(8,128)(2,1)S(1)}, bf16[24,2048]{1,0:T(8,128)(2,1)S(1)}, u32[]{:S(2)}, u32[]{:S(2)}) collective-permute-start(bf16[24,2048]{1,0:T(8,128)(2,1)S(1)} %get-tuple-element.79), channel_id=1, source_target_pairs={{0,8},{4,12},{8,0},{12,4},{1,9},{5,13},{9,1},{13,5},{2,10},{6,14},... | collective-permute-start | bytes 294920 | tf_op jit(solution)/shard_map/ppermute | solution.py:523
  42.4 4.8 %collective-permute-start.9 = (bf16[24,2048]{1,0:T(8,128)(2,1)S(1)}, bf16[24,2048]{1,0:T(8,128)(2,1)S(1)}, u32[]{:S(2)}, u32[]{:S(2)}) collective-permute-start(bf16[24,2048]{1,0:T(8,128)(2,1)S(1)} %shard_map.115.refs_0_), channel_id=1, source_target_pairs={{0,16},{16,0},{1,17},{17,1},{2,18},{18,2},{3,19},{19,3},{4,20},{20... | collective-permute-start | bytes 294920 | tf_op jit(solution)/shard_map/ppermute | solution.py:527
  44.0 6.7 %collective-permute-start.8 = (bf16[24,2048]{1,0:T(8,128)(2,1)S(1)}, bf16[24,2048]{1,0:T(8,128)(2,1)S(1)}, u32[]{:S(2)}, u32[]{:S(2)}) collective-permute-start(bf16[24,2048]{1,0:T(8,128)(2,1)S(1)} %shard_map.115.refs_0_), channel_id=1, source_target_pairs={{0,8},{4,12},{8,0},{12,4},{1,9},{5,13},{9,1},{13,5},{2,10},{6,14},... | collective-permute-start | bytes 294920 | tf_op jit(solution)/shard_map/ppermute | solution.py:523
  45.3 6.2 %collective-permute-start.10 = (bf16[24,2048]{1,0:T(8,128)(2,1)S(1)}, bf16[24,2048]{1,0:T(8,128)(2,1)S(1)}, u32[]{:S(2)}, u32[]{:S(2)}) collective-permute-start(bf16[24,2048]{1,0:T(8,128)(2,1)S(1)} %shard_map.115.refs_0_), channel_id=1, source_target_pairs={{0,4},{4,0},{8,12},{12,8},{1,5},{5,1},{9,13},{13,9},{2,6},{6,2},{1... | collective-permute-start | bytes 294920 | tf_op jit(solution)/shard_map/ppermute | solution.py:523
  50.6 4.6 %collective-permute-start.13 = (bf16[24,2048]{1,0:T(8,128)(2,1)S(1)}, bf16[24,2048]{1,0:T(8,128)(2,1)S(1)}, u32[]{:S(2)}, u32[]{:S(2)}) collective-permute-start(bf16[24,2048]{1,0:T(8,128)(2,1)S(1)} %collective-permute-done.8.refs_4_), channel_id=1, source_target_pairs={{0,4},{4,0},{8,12},{12,8},{1,5},{5,1},{9,13},{13,9},{2,6},{6,2},{1... | collective-permute-start | bytes 294920 | tf_op jit(solution)/shard_map/ppermute | solution.py:523
  50.9 8.0 %collective-permute-start.12 = (bf16[24,2048]{1,0:T(8,128)(2,1)S(1)}, bf16[24,2048]{1,0:T(8,128)(2,1)S(1)}, u32[]{:S(2)}, u32[]{:S(2)}) collective-permute-start(bf16[24,2048]{1,0:T(8,128)(2,1)S(1)} %collective-permute-done.8.refs_4_), channel_id=1, source_target_pairs={{0,16},{16,0},{1,17},{17,1},{2,18},{18,2},{3,19},{19,3},{4,20},{20... | collective-permute-start | bytes 294920 | tf_op jit(solution)/shard_map/ppermute | solution.py:527
  51.4 7.5 %collective-permute-start.11 = (bf16[24,2048]{1,0:T(8,128)(2,1)S(1)}, bf16[24,2048]{1,0:T(8,128)(2,1)S(1)}, u32[]{:S(2)}, u32[]{:S(2)}) collective-permute-start(bf16[24,2048]{1,0:T(8,128)(2,1)S(1)} %collective-permute-done.10.refs_2_), channel_id=1, source_target_pairs={{0,16},{16,0},{1,17},{17,1},{2,18},{18,2},{3,19},{19,3},{4,20},{20... | collective-permute-start | bytes 294920 | tf_op jit(solution)/shard_map/ppermute | solution.py:527
  55.3 4.6 %collective-permute-start.14 = (bf16[24,2048]{1,0:T(8,128)(2,1)S(1)}, bf16[24,2048]{1,0:T(8,128)(2,1)S(1)}, u32[]{:S(2)}, u32[]{:S(2)}) collective-permute-start(bf16[24,2048]{1,0:T(8,128)(2,1)S(1)} %collective-permute-done.13.refs_6_), channel_id=1, source_target_pairs={{0,16},{16,0},{1,17},{17,1},{2,18},{18,2},{3,19},{19,3},{4,20},{20... | collective-permute-start | bytes 294920 | tf_op jit(solution)/shard_map/ppermute | solution.py:527
  66.6 6.0 %collective-permute-start.15 = (bf16[2,2,48,2048]{3,2,1,0:T(8,128)(2,1)S(1)}, bf16[2,2,48,2048]{3,2,1,0:T(8,128)(2,1)S(1)}, u32[]{:S(2)}, u32[]{:S(2)}) collective-permute-start(bf16[2,2,48,2048]{3,2,1,0:T(8,128)(2,1)S(1)} %get-tuple-element.95), channel_id=1, source_target_pairs={{0,1},{1,0},{2,3},{3,2},{4,5},{5,4},{6,7},{7,6},{8,9},{9,8},{10,11... | collective-permute-start | bytes 2359304 | tf_op jit(solution)/shard_map/ppermute | solution.py:515
  72.0 2.3 %collective-permute-start.17 = (bf16[2,2,48,1776]{3,2,1,0:T(8,128)(2,1)S(1)}, bf16[2,2,48,1776]{3,2,1,0:T(8,128)(2,1)S(1)}, u32[]{:S(2)}, u32[]{:S(2)}) collective-permute-start(bf16[2,2,48,1776]{3,2,1,0:T(8,128)(2,1)S(1)} %get-tuple-element.101), channel_id=1, source_target_pairs={{0,1},{1,0},{2,3},{3,2},{4,5},{5,4},{6,7},{7,6},{8,9},{9,8},{10,11... | collective-permute-start | bytes 2045960 | tf_op jit(solution)/shard_map/ppermute | solution.py:515
  72.6 12.0 %collective-permute-start.16 = (bf16[2,48,2048]{2,1,0:T(8,128)(2,1)S(1)}, bf16[2,48,2048]{2,1,0:T(8,128)(2,1)S(1)}, u32[]{:S(2)}, u32[]{:S(2)}) collective-permute-start(bf16[2,48,2048]{2,1,0:T(8,128)(2,1)S(1)} %fusion), channel_id=1, source_target_pairs={{0,2},{1,3},{2,0},{3,1},{4,6},{5,7},{6,4},{7,5},{8,10},{9,11},{10,... | collective-permute-start | bytes 1179656 | tf_op jit(solution)/shard_map/ppermute | solution.py:519
  74.4 17.7 %collective-permute-start.19 = (bf16[2,48,1776]{2,1,0:T(8,128)(2,1)S(1)}, bf16[2,48,1776]{2,1,0:T(8,128)(2,1)S(1)}, u32[]{:S(2)}, u32[]{:S(2)}) collective-permute-start(bf16[2,48,1776]{2,1,0:T(8,128)(2,1)S(1)} %fusion.1), channel_id=1, source_target_pairs={{0,2},{1,3},{2,0},{3,1},{4,6},{5,7},{6,4},{7,5},{8,10},{9,11},{10,... | collective-permute-start | bytes 1022984 | tf_op jit(solution)/shard_map/ppermute | solution.py:519
  85.0 10.0 %collective-permute-start.18 = (bf16[48,1920]{1,0:T(8,128)(2,1)S(1)}, bf16[48,1920]{1,0:T(8,128)(2,1)S(1)}, u32[]{:S(2)}, u32[]{:S(2)}) collective-permute-start(bf16[48,1920]{1,0:T(8,128)(2,1)S(1)} %get-tuple-element.105.rest_1_.refs_0_), channel_id=1, source_target_pairs={{0,2},{1,3},{2,0},{3,1},{4,6},{5,7},{6,4},{7,5},{8,10},{9,11},{10,... | collective-permute-start | bytes 552968 | tf_op jit(solution)/shard_map/ppermute | solution.py:519
  86.6 10.2 %collective-permute-start.21 = (bf16[48,1920]{1,0:T(8,128)(2,1)S(1)}, bf16[48,1920]{1,0:T(8,128)(2,1)S(1)}, u32[]{:S(2)}, u32[]{:S(2)}) collective-permute-start(bf16[48,1920]{1,0:T(8,128)(2,1)S(1)} %get-tuple-element.105.rest_1_.refs_0_), channel_id=1, source_target_pairs={{0,1},{1,0},{2,3},{3,2},{4,5},{5,4},{6,7},{7,6},{8,9},{9,8},{10,11... | collective-permute-start | bytes 552968 | tf_op jit(solution)/shard_map/ppermute | solution.py:515
  95.1 1.7 %collective-permute-start.22 = (bf16[48,1920]{1,0:T(8,128)(2,1)S(1)}, bf16[48,1920]{1,0:T(8,128)(2,1)S(1)}, u32[]{:S(2)}, u32[]{:S(2)}) collective-permute-start(bf16[48,1920]{1,0:T(8,128)(2,1)S(1)} %collective-permute-done.18.refs_1_), channel_id=1, source_target_pairs={{0,1},{1,0},{2,3},{3,2},{4,5},{5,4},{6,7},{7,6},{8,9},{9,8},{10,11... | collective-permute-start | bytes 552968 | tf_op jit(solution)/shard_map/ppermute | solution.py:515
  95.1 6.8 %collective-permute-start.20 = (bf16[48,1776]{1,0:T(8,128)(2,1)S(1)}, bf16[48,1776]{1,0:T(8,128)(2,1)S(1)}, u32[]{:S(2)}, u32[]{:S(2)}) collective-permute-start(bf16[48,1776]{1,0:T(8,128)(2,1)S(1)} %shard_map.122.refs_0_), channel_id=1, source_target_pairs={{0,2},{1,3},{2,0},{3,1},{4,6},{5,7},{6,4},{7,5},{8,10},{9,11},{10,... | collective-permute-start | bytes 511496 | tf_op jit(solution)/shard_map/ppermute | solution.py:519
  96.6 5.3 %collective-permute-start.23 = (bf16[48,1776]{1,0:T(8,128)(2,1)S(1)}, bf16[48,1776]{1,0:T(8,128)(2,1)S(1)}, u32[]{:S(2)}, u32[]{:S(2)}) collective-permute-start(bf16[48,1776]{1,0:T(8,128)(2,1)S(1)} %shard_map.122.refs_0_), channel_id=1, source_target_pairs={{0,1},{1,0},{2,3},{3,2},{4,5},{5,4},{6,7},{7,6},{8,9},{9,8},{10,11... | collective-permute-start | bytes 511496 | tf_op jit(solution)/shard_map/ppermute | solution.py:515
  101.9 1.4 %collective-permute-start.24 = (bf16[48,1776]{1,0:T(8,128)(2,1)S(1)}, bf16[48,1776]{1,0:T(8,128)(2,1)S(1)}, u32[]{:S(2)}, u32[]{:S(2)}) collective-permute-start(bf16[48,1776]{1,0:T(8,128)(2,1)S(1)} %collective-permute-done.20.refs_1_), channel_id=1, source_target_pairs={{0,1},{1,0},{2,3},{3,2},{4,5},{5,4},{6,7},{7,6},{8,9},{9,8},{10,11... | collective-permute-start | bytes 511496 | tf_op jit(solution)/shard_map/ppermute | solution.py:515
  106.5 5.7 %collective-permute-start.25 = (bf16[24,2048]{1,0:T(8,128)(2,1)S(1)}, bf16[24,2048]{1,0:T(8,128)(2,1)S(1)}, u32[]{:S(2)}, u32[]{:S(2)}) collective-permute-start(bf16[24,2048]{1,0:T(8,128)(2,1)S(1)} %get-tuple-element.116), channel_id=1, source_target_pairs={{0,16},{16,0},{1,17},{17,1},{2,18},{18,2},{3,19},{19,3},{4,20},{20... | collective-permute-start | bytes 294920 | tf_op jit(solution)/shard_map/ppermute | solution.py:527
  107.2 7.5 %collective-permute-start.27 = (bf16[24,2048]{1,0:T(8,128)(2,1)S(1)}, bf16[24,2048]{1,0:T(8,128)(2,1)S(1)}, u32[]{:S(2)}, u32[]{:S(2)}) collective-permute-start(bf16[24,2048]{1,0:T(8,128)(2,1)S(1)} %get-tuple-element.118), channel_id=1, source_target_pairs={{0,16},{16,0},{1,17},{17,1},{2,18},{18,2},{3,19},{19,3},{4,20},{20... | collective-permute-start | bytes 294920 | tf_op jit(solution)/shard_map/ppermute | solution.py:527
  108.6 7.8 %collective-permute-start.29 = (bf16[24,2048]{1,0:T(8,128)(2,1)S(1)}, bf16[24,2048]{1,0:T(8,128)(2,1)S(1)}, u32[]{:S(2)}, u32[]{:S(2)}) collective-permute-start(bf16[24,2048]{1,0:T(8,128)(2,1)S(1)} %get-tuple-element.120), channel_id=1, source_target_pairs={{0,16},{16,0},{1,17},{17,1},{2,18},{18,2},{3,19},{19,3},{4,20},{20... | collective-permute-start | bytes 294920 | tf_op jit(solution)/shard_map/ppermute | solution.py:527
  109.2 8.6 %collective-permute-start.31 = (bf16[24,2048]{1,0:T(8,128)(2,1)S(1)}, bf16[24,2048]{1,0:T(8,128)(2,1)S(1)}, u32[]{:S(2)}, u32[]{:S(2)}) collective-permute-start(bf16[24,2048]{1,0:T(8,128)(2,1)S(1)} %get-tuple-element.122), channel_id=1, source_target_pairs={{0,16},{16,0},{1,17},{17,1},{2,18},{18,2},{3,19},{19,3},{4,20},{20... | collective-permute-start | bytes 294920 | tf_op jit(solution)/shard_map/ppermute | solution.py:527
  112.3 7.1 %collective-permute-start.26 = (bf16[24,2048]{1,0:T(8,128)(2,1)S(1)}, bf16[24,2048]{1,0:T(8,128)(2,1)S(1)}, u32[]{:S(2)}, u32[]{:S(2)}) collective-permute-start(bf16[24,2048]{1,0:T(8,128)(2,1)S(1)} %add_convert_fusion.2), channel_id=1, source_target_pairs={{0,12},{4,8},{8,4},{12,0},{1,13},{5,9},{9,5},{13,1},{2,14},{6,10},... | collective-permute-start | bytes 294920 | tf_op jit(solution)/shard_map/ppermute | solution.py:523
  114.6 8.1 %collective-permute-start.28 = (bf16[24,2048]{1,0:T(8,128)(2,1)S(1)}, bf16[24,2048]{1,0:T(8,128)(2,1)S(1)}, u32[]{:S(2)}, u32[]{:S(2)}) collective-permute-start(bf16[24,2048]{1,0:T(8,128)(2,1)S(1)} %add_convert_fusion.1), channel_id=1, source_target_pairs={{0,8},{4,12},{8,0},{12,4},{1,9},{5,13},{9,1},{13,5},{2,10},{6,14},... | collective-permute-start | bytes 294920 | tf_op jit(solution)/shard_map/ppermute | solution.py:523
  116.5 6.3 %collective-permute-start.30 = (bf16[24,2048]{1,0:T(8,128)(2,1)S(1)}, bf16[24,2048]{1,0:T(8,128)(2,1)S(1)}, u32[]{:S(2)}, u32[]{:S(2)}) collective-permute-start(bf16[24,2048]{1,0:T(8,128)(2,1)S(1)} %add_convert_fusion), channel_id=1, source_target_pairs={{0,4},{4,0},{8,12},{12,8},{1,5},{5,1},{9,13},{13,9},{2,6},{6,2},{1... | collective-permute-start | bytes 294920 | tf_op jit(solution)/shard_map/ppermute | solution.py:523

commit v4 on v3

--- a/solution.py
+++ b/solution.py
@@ -333,9 +333,8 @@
 
 
 def gate_up_kernel(tiles, scaled_ref, gate_ref, up_ref, *rest):
-    keep_ref, cross_ref, send_ref = rest[-3:]
-    high = keep_ref.shape[1]
-    homes = (keep_ref, cross_ref, send_ref.at[0], send_ref.at[1])
+    homes = rest[-4:]
+    high = homes[0].shape[1]
 
     def multiply():
         for which, weight in enumerate((gate_ref, up_ref)):
@@ -344,7 +343,7 @@
             for place, home in enumerate(homes):
                 home[which] = term[place * high : (place + 1) * high]
 
-    if len(rest) == 3:
+    if len(rest) == 4:
         multiply()
         return
     square_ref = rest[0]
@@ -374,12 +373,8 @@
         functools.partial(gate_up_kernel, tiles),
         grid=(tiles + len(ins) - 3,),
         in_specs=specs,
-        out_specs=[piece, piece, pl.BlockSpec((2, 2, high, TILE), lambda j: (0, 0, 0, j))],
-        out_shape=[
-            jax.ShapeDtypeStruct((2, high, width), BF16),
-            jax.ShapeDtypeStruct((2, high, width), BF16),
-            jax.ShapeDtypeStruct((2, 2, high, width), BF16),
-        ],
+        out_specs=[piece] * 4,
+        out_shape=[jax.ShapeDtypeStruct((2, high, width), BF16)] * 4,
         compiler_params=params(),
         cost_estimate=cost(4 * rows * depth * width, 4 * depth * width),
     )(*ins)
@@ -388,7 +383,7 @@
 def activate_kernel(model, width, own_norm, keep_ref, got_ref, crossed_ref, *rest):
     def total(which, low, high):
         value = keep_ref[which, :, low:high].astype(F32)
-        value += got_ref[0, which, :, low:high].astype(F32)
+        value += got_ref[which, :, low:high].astype(F32)
         return value + crossed_ref[which, :, low:high].astype(F32)
 
     if own_norm:
@@ -595,21 +590,21 @@
             sources += [everyone[s] for s in range(groups)]
     scaled, squares = scale_rows(scalars, sources, gain[None, :], mark)
 
-    reduced = []
-    for index, (begin, width) in enumerate(chunks):
-        extra = squares if begin == 0 else None
-        keep, cross, send = gate_up(scaled, *held[index], width, extra)
-        if index == 0:
-            scaled, send = lax.optimization_barrier((scaled, send))
-        got = to_core(send)
-        cross = (cross.astype(F32) + got[1].astype(F32)).astype(BF16)
-        if index == 1:
-            held, mark, cross = fetch([down_weight] * 2, chunks, cross)
-        reduced.append((keep, got, to_x(cross)))
     first, second = (width for begin, width in chunks)
-    hidden, norm = activate(model, first, *reduced[0], None, mark)
+    keep0, cross, side, far_side = gate_up(scaled, *held[0], first, squares)
+    cross = (cross.astype(F32) + to_core(far_side).astype(F32)).astype(BF16)
+    got0 = to_core(side)
+    scaled, cross = lax.optimization_barrier((scaled, cross))
+    crossed0 = to_x(cross)
+    keep1, cross, side, far_side = gate_up(scaled, *held[1], second)
+    got, crossed0 = lax.optimization_barrier((to_core(far_side), crossed0))
+    cross = (cross.astype(F32) + got.astype(F32)).astype(BF16)
+    got1 = to_core(side)
+    held, mark, cross = fetch([down_weight] * 2, chunks, cross)
+    crossed1 = to_x(cross)
+    hidden, norm = activate(model, first, keep0, got0, crossed0, None, mark)
     over, near = to_x(hidden), to_core(hidden)
-    later, norm = activate(model, second, *reduced[1], norm, hidden)
+    later, norm = activate(model, second, keep1, got1, crossed1, norm, hidden)
     far = to_x(later)
     over, later = lax.optimization_barrier((over, later))
     pieces = [hidden, over, near, to_core(over)]

time: 124 us -> 122 us (0.984)
    ppermute x6, waiting for transfers between devices: 15.1 us -> 11.2 us  [to_x(): return lax.ppermute(x, 'ffn', [(i, i ^ 2) for i in range(4)])]
    ppermute x9 -> x11, waiting for transfers between devices: 4.05 us -> 6.71 us  [to_core(): return lax.ppermute(x, 'ffn', [(i, i ^ 1) for i in range(4)])]
  transfers between devices with their start and end apart: 32 -> 34, of which waited for: 19 -> 20; matrix products, arithmetic and copies ran while one was open for 0% -> 0% of each run, Pallas kernels for 23% -> 24%
where the time goes in v4:
time: 122 us
  Pallas kernels  54.8 us (45%)
  waiting for transfers between devices  34.5 us (28%)
  starting transfers between devices  29.7 us (24%)
  between operations  1.52 us (1%)
    pallas_call x4, Pallas kernels, fetch(): pl.pallas_call(functools.partial(fetch_kernel, pieces), in_specs=[pl.Bloc...  19.4 us
    ppermute x9, waiting for transfers between devices, to_z(): return lax.ppermute(x, 'tp', [(i, i ^ k) for i in range(4)])  12.4 us
    ppermute x9, starting transfers between devices, to_z(): return lax.ppermute(x, 'tp', [(i, i ^ k) for i in range(4)])  11.8 us
    pallas_call x1, Pallas kernels, attention(): return call(scalars, queries, kv_cache, kv_cache, new_kv, new_kv)  11.3 us
    ppermute x6, waiting for transfers between devices, to_x(): return lax.ppermute(x, 'ffn', [(i, i ^ 2) for i in range(4)])  11.2 us
    pallas_call x2, Pallas kernels, gate_up(): pl.pallas_call(functools.partial(gate_up_kernel, tiles), grid=(tiles + le...  11.2 us
    ppermute x8, starting transfers between devices, to_y(): return lax.ppermute(x, 'grp', [(0, 1), (1, 0)])  8.23 us
    ppermute x6, starting transfers between devices, to_x(): return lax.ppermute(x, 'ffn', [(i, i ^ 2) for i in range(4)])  8.1 us
  transfers between devices with their start and end apart: 34, of which 20 were waited for; matrix products, arithmetic and copies ran while one was open for 0% of the time, Pallas kernels for 24%

profile of v4, /device:TPU:0, one launch (start us, length us, event | category | flops | bytes accessed | tf_op | source)
XLA Modules:
  0.0 121.6 jit_solution(12656529056080728235)
XLA Ops:
  1.4 11.3 %shard_map.109 = (bf16[96,1024]{1,0:T(8,128)(2,1)S(1)}, bf16[96,1024]{1,0:T(8,128)(2,1)S(1)}, f32[8,128]{1,0:T(8,128)S(1)}, f32[8,128]{1,0:T(8,128)S(1)}) custom-call(s32[6]{0:T(128)S(1)} %stack.27.scalars, bf16[96,2048]{1,0:T(8,128)(2,1)} %q_ref.1, bf16[2,1,2048,256]{3,2,1,0:T(8,128)(2,1)} %value_ref.1, bf16[2,1,2048,256]{3,2,1,0:T(8,128)(2,1)} %value_ref.1, ...), custom_call_target="tpu_custom_call" | custom-call | flops 1610612736 | bytes 2097152 | tf_op jit(solution)/shard_map/pallas_call | solution.py:167
  13.3 1.1 collective-permute-done.1.lse_b_ref
  14.8 2.8 %collective-permute-start.2 = (bf16[96,1024]{1,0:T(8,128)(2,1)S(1)}, bf16[96,1024]{1,0:T(8,128)(2,1)S(1)}, u32[]{:S(2)}, u32[]{:S(2)}) collective-permute-start(bf16[96,1024]{1,0:T(8,128)(2,1)S(1)} %get-tuple-element.73.a_ref), channel_id=1, source_target_pairs={{0,2},{1,3},{2,0},{3,1},{4,6},{5,7},{6,4},{7,5},{8,10},{9,11},{10,... | collective-permute-start | bytes 589832 | tf_op jit(solution)/shard_map/ppermute | solution.py:514
  17.7 3.4 %shard_map.111 = (bf16[2048,2048]{1,0:T(8,128)(2,1)S(1)}, f32[8,128]{1,0:T(8,128)S(1)}) custom-call(bf16[2048,2048]{1,0:T(8,128)(2,1)} %refs_0_), custom_call_target="tpu_custom_call" | custom-call | bytes 16777216 | tf_op jit(solution)/shard_map/pallas_call | solution.py:62
  21.1 1.9 %collective-permute-done.3.lse_b_ref = f32[8,128]{1,0:T(8,128)S(1)} collective-permute-done((f32[8,128]{1,0:T(8,128)S(1)}, f32[8,128]{1,0:T(8,128)S(1)}, u32[]{:S(2)}, u32[]{:S(2)}) %collective-permute-start.3) | collective-permute-done | bytes 4128 | tf_op jit(solution)/shard_map/ppermute | solution.py:514
  23.0 0.9 shard_map.112
  24.0 1.4 %collective-permute-done.4.other_ref = bf16[96,1024]{1,0:T(8,128)(2,1)S(1)} collective-permute-done((bf16[96,1024]{1,0:T(8,128)(2,1)S(1)}, bf16[96,1024]{1,0:T(8,128)(2,1)S(1)}, u32[]{:S(2)}, u32[]{:S(2)}) %collective-permute-start.4) | collective-permute-done | bytes 196640 | tf_op jit(solution)/shard_map/ppermute | solution.py:510
  25.4 2.7 %shard_map.113 = (f32[24,2048]{1,0:T(8,128)S(1)}, bf16[24,2048]{1,0:T(8,128)(2,1)S(1)}, bf16[24,2048]{1,0:T(8,128)(2,1)S(1)}, bf16[24,2048]{1,0:T(8,128)(2,1)S(1)}) custom-call(s32[6]{0:T(128)S(1)} %stack.27.scalars, bf16[96,1024]{1,0:T(8,128)(2,1)S(1)} %get-tuple-element.77.keep_ref, bf16[96,1024]{1,0:T(8,128)(2,1)S(1)} %collective-permute-done.4.other_ref, ...), custom_call_target="tpu_custom_call" | custom-call | flops 805306368 | bytes 8388608 | tf_op jit(solution)/shard_map/pallas_call | solution.py:240
  28.1 1.9 %collective-permute-start.5 = (bf16[24,2048]{1,0:T(8,128)(2,1)S(1)}, bf16[24,2048]{1,0:T(8,128)(2,1)S(1)}, u32[]{:S(2)}, u32[]{:S(2)}) collective-permute-start(bf16[24,2048]{1,0:T(8,128)(2,1)S(1)} %get-tuple-element.81), channel_id=1, source_target_pairs={{0,4},{4,0},{8,12},{12,8},{1,5},{5,1},{9,13},{13,9},{2,6},{6,2},{1... | collective-permute-start | bytes 294920 | tf_op jit(solution)/shard_map/ppermute | solution.py:518
  30.0 2.5 %collective-permute-start.6 = (bf16[24,2048]{1,0:T(8,128)(2,1)S(1)}, bf16[24,2048]{1,0:T(8,128)(2,1)S(1)}, u32[]{:S(2)}, u32[]{:S(2)}) collective-permute-start(bf16[24,2048]{1,0:T(8,128)(2,1)S(1)} %get-tuple-element.82), channel_id=1, source_target_pairs={{0,12},{4,8},{8,4},{12,0},{1,13},{5,9},{9,5},{13,1},{2,14},{6,10},... | collective-permute-start | bytes 294920 | tf_op jit(solution)/shard_map/ppermute | solution.py:518
  32.6 7.6 %shard_map.114 = (bf16[1920,2048]{1,0:T(8,128)(2,1)S(1)}, bf16[1920,2048]{1,0:T(8,128)(2,1)S(1)}, bf16[1776,2048]{1,0:T(8,128)(2,1)S(1)}, f32[8,128]{1,0:T(8,128)S(1)}) custom-call(bf16[3696,2048]{1,0:T(8,128)(2,1)} %bitcast.11, bf16[3696,2048]{1,0:T(8,128)(2,1)} %bitcast.13, bf16[3696,2048]{1,0:T(8,128)(2,1)} %bitcast.12), custom_call_target="tpu_custom_call" | custom-call | bytes 46006272 | tf_op jit(solution)/shard_map/pallas_call | solution.py:62
  40.2 1.5 %collective-permute-done.7.rest_2_ = bf16[24,2048]{1,0:T(8,128)(2,1)S(1)} collective-permute-done((bf16[24,2048]{1,0:T(8,128)(2,1)S(1)}, bf16[24,2048]{1,0:T(8,128)(2,1)S(1)}, u32[]{:S(2)}, u32[]{:S(2)}) %collective-permute-start.7) | collective-permute-done | bytes 98336 | tf_op jit(solution)/shard_map/ppermute | solution.py:518
  41.7 0.7 shard_map.115.refs_0_
  42.4 1.6 %collective-permute-start.9 = (bf16[24,2048]{1,0:T(8,128)(2,1)S(1)}, bf16[24,2048]{1,0:T(8,128)(2,1)S(1)}, u32[]{:S(2)}, u32[]{:S(2)}) collective-permute-start(bf16[24,2048]{1,0:T(8,128)(2,1)S(1)} %shard_map.115.refs_0_), channel_id=1, source_target_pairs={{0,16},{16,0},{1,17},{17,1},{2,18},{18,2},{3,19},{19,3},{4,20},{20... | collective-permute-start | bytes 294920 | tf_op jit(solution)/shard_map/ppermute | solution.py:522
  44.0 1.3 %collective-permute-start.8 = (bf16[24,2048]{1,0:T(8,128)(2,1)S(1)}, bf16[24,2048]{1,0:T(8,128)(2,1)S(1)}, u32[]{:S(2)}, u32[]{:S(2)}) collective-permute-start(bf16[24,2048]{1,0:T(8,128)(2,1)S(1)} %shard_map.115.refs_0_), channel_id=1, source_target_pairs={{0,8},{4,12},{8,0},{12,4},{1,9},{5,13},{9,1},{13,5},{2,10},{6,14},... | collective-permute-start | bytes 294920 | tf_op jit(solution)/shard_map/ppermute | solution.py:518
  45.3 1.9 %collective-permute-start.10 = (bf16[24,2048]{1,0:T(8,128)(2,1)S(1)}, bf16[24,2048]{1,0:T(8,128)(2,1)S(1)}, u32[]{:S(2)}, u32[]{:S(2)}) collective-permute-start(bf16[24,2048]{1,0:T(8,128)(2,1)S(1)} %shard_map.115.refs_0_), channel_id=1, source_target_pairs={{0,4},{4,0},{8,12},{12,8},{1,5},{5,1},{9,13},{13,9},{2,6},{6,2},{1... | collective-permute-start | bytes 294920 | tf_op jit(solution)/shard_map/ppermute | solution.py:518
  47.2 3.5 %collective-permute-done.8.refs_4_ = bf16[24,2048]{1,0:T(8,128)(2,1)S(1)} collective-permute-done((bf16[24,2048]{1,0:T(8,128)(2,1)S(1)}, bf16[24,2048]{1,0:T(8,128)(2,1)S(1)}, u32[]{:S(2)}, u32[]{:S(2)}) %collective-permute-start.8) | collective-permute-done | bytes 98336 | tf_op jit(solution)/shard_map/ppermute | solution.py:518
  51.4 1.5 %collective-permute-start.11 = (bf16[24,2048]{1,0:T(8,128)(2,1)S(1)}, bf16[24,2048]{1,0:T(8,128)(2,1)S(1)}, u32[]{:S(2)}, u32[]{:S(2)}) collective-permute-start(bf16[24,2048]{1,0:T(8,128)(2,1)S(1)} %collective-permute-done.10.refs_2_), channel_id=1, source_target_pairs={{0,16},{16,0},{1,17},{17,1},{2,18},{18,2},{3,19},{19,3},{4,20},{20... | collective-permute-start | bytes 294920 | tf_op jit(solution)/shard_map/ppermute | solution.py:522
  52.9 2.3 %collective-permute-done.13.refs_6_ = bf16[24,2048]{1,0:T(8,128)(2,1)S(1)} collective-permute-done((bf16[24,2048]{1,0:T(8,128)(2,1)S(1)}, bf16[24,2048]{1,0:T(8,128)(2,1)S(1)}, u32[]{:S(2)}, u32[]{:S(2)}) %collective-permute-start.13) | collective-permute-done | bytes 98336 | tf_op jit(solution)/shard_map/ppermute | solution.py:518
  55.8 3.1 %shard_map.116 = (bf16[1776,2048]{1,0:T(8,128)(2,1)S(1)}, f32[8,128]{1,0:T(8,128)S(1)}) custom-call(bf16[3696,2048]{1,0:T(8,128)(2,1)} %bitcast.14), custom_call_target="tpu_custom_call" | custom-call | bytes 14548992 | tf_op jit(solution)/shard_map/pallas_call | solution.py:62
  58.9 1.0 collective-permute-done.14.refs_7_
  59.9 1.2 shard_map.117
  61.1 5.6 %shard_map.118 = (bf16[2,48,2048]{2,1,0:T(8,128)(2,1)S(1)}, bf16[2,48,2048]{2,1,0:T(8,128)(2,1)S(1)}, bf16[2,48,2048]{2,1,0:T(8,128)(2,1)S(1)}, bf16[2,48,2048]{2,1,0:T(8,128)(2,1)S(1)}) custom-call(bf16[2048,192]{1,0:T(8,128)(2,1)S(1)} %get-tuple-element.101.scaled_ref, bf16[1920,2048]{1,0:T(8,128)(2,1)S(1)} %get-tuple-element.94.gate_ref, ...), custom_call_target="tpu_custom_call" | custom-call | flops 3221225472 | bytes 16777216 | tf_op jit(solution)/shard_map/pallas_call | solution.py:372
  66.7 1.7 %collective-permute-done.16 = bf16[2,48,2048]{2,1,0:T(8,128)(2,1)S(1)} collective-permute-done((bf16[2,48,2048]{2,1,0:T(8,128)(2,1)S(1)}, bf16[2,48,2048]{2,1,0:T(8,128)(2,1)S(1)}, u32[]{:S(2)}, u32[]{:S(2)}) %collective-permute-start.16) | collective-permute-done | bytes 393248 | tf_op jit(solution)/shard_map/ppermute | solution.py:510
  68.6 1.6 %collective-permute-start.18 = (bf16[2,48,2048]{2,1,0:T(8,128)(2,1)S(1)}, bf16[2,48,2048]{2,1,0:T(8,128)(2,1)S(1)}, u32[]{:S(2)}, u32[]{:S(2)}) collective-permute-start(bf16[2,48,2048]{2,1,0:T(8,128)(2,1)S(1)} %add_convert_fusion), channel_id=1, source_target_pairs={{0,2},{1,3},{2,0},{3,1},{4,6},{5,7},{6,4},{7,5},{8,10},{9,11},{10,... | collective-permute-start | bytes 1179656 | tf_op jit(solution)/shard_map/ppermute | solution.py:514
  70.1 5.6 %shard_map.119 = (bf16[2,48,1776]{2,1,0:T(8,128)(2,1)S(1)}, bf16[2,48,1776]{2,1,0:T(8,128)(2,1)S(1)}, bf16[2,48,1776]{2,1,0:T(8,128)(2,1)S(1)}, bf16[2,48,1776]{2,1,0:T(8,128)(2,1)S(1)}) custom-call(bf16[2048,192]{1,0:T(8,128)(2,1)S(1)} %get-tuple-element.101.scaled_ref, bf16[1776,2048]{1,0:T(8,128)(2,1)S(1)} %get-tuple-element.102.gate_ref, ...), custom_call_target="tpu_custom_call" | custom-call | flops 2793406464 | bytes 14548992 | tf_op jit(solution)/shard_map/pallas_call | solution.py:372
  76.3 1.1 collective-permute-done.17
  77.4 2.4 %collective-permute-done.18.crossed_ref = bf16[2,48,2048]{2,1,0:T(8,128)(2,1)S(1)} collective-permute-done((bf16[2,48,2048]{2,1,0:T(8,128)(2,1)S(1)}, bf16[2,48,2048]{2,1,0:T(8,128)(2,1)S(1)}, u32[]{:S(2)}, u32[]{:S(2)}) %collective-permute-start.18) | collective-permute-done | bytes 393248 | tf_op jit(solution)/shard_map/ppermute | solution.py:514
  79.9 1.6 %collective-permute-start.21 = (bf16[2,48,1776]{2,1,0:T(8,128)(2,1)S(1)}, bf16[2,48,1776]{2,1,0:T(8,128)(2,1)S(1)}, u32[]{:S(2)}, u32[]{:S(2)}) collective-permute-start(bf16[2,48,1776]{2,1,0:T(8,128)(2,1)S(1)} %add_convert_fusion.1), channel_id=1, source_target_pairs={{0,2},{1,3},{2,0},{3,1},{4,6},{5,7},{6,4},{7,5},{8,10},{9,11},{10,... | collective-permute-start | bytes 1022984 | tf_op jit(solution)/shard_map/ppermute | solution.py:514
  81.4 5.3 %shard_map.120 = (bf16[1920,2048]{1,0:T(8,128)(2,1)S(1)}, bf16[1776,2048]{1,0:T(8,128)(2,1)S(1)}, f32[8,128]{1,0:T(8,128)S(1)}) custom-call(bf16[3696,2048]{1,0:T(8,128)(2,1)} %refs_1_, bf16[3696,2048]{1,0:T(8,128)(2,1)} %refs_1_), custom_call_target="tpu_custom_call" | custom-call | bytes 30277632 | tf_op jit(solution)/shard_map/pallas_call | solution.py:62
  87.1 0.6 collective-permute-start.19
  87.7 1.8 %collective-permute-done.21.crossed_ref = bf16[2,48,1776]{2,1,0:T(8,128)(2,1)S(1)} collective-permute-done((bf16[2,48,1776]{2,1,0:T(8,128)(2,1)S(1)}, bf16[2,48,1776]{2,1,0:T(8,128)(2,1)S(1)}, u32[]{:S(2)}, u32[]{:S(2)}) %collective-permute-start.21) | collective-permute-done | bytes 341024 | tf_op jit(solution)/shard_map/ppermute | solution.py:514
  89.8 3.3 %collective-permute-done.19.refs_1_ = bf16[48,1920]{1,0:T(8,128)(2,1)S(1)} collective-permute-done((bf16[48,1920]{1,0:T(8,128)(2,1)S(1)}, bf16[48,1920]{1,0:T(8,128)(2,1)S(1)}, u32[]{:S(2)}, u32[]{:S(2)}) %collective-permute-start.19) | collective-permute-done | bytes 184352 | tf_op jit(solution)/shard_map/ppermute | solution.py:514
  93.2 1.5 %collective-permute-start.22 = (bf16[48,1776]{1,0:T(8,128)(2,1)S(1)}, bf16[48,1776]{1,0:T(8,128)(2,1)S(1)}, u32[]{:S(2)}, u32[]{:S(2)}) collective-permute-start(bf16[48,1776]{1,0:T(8,128)(2,1)S(1)} %shard_map.122.refs_0_), channel_id=1, source_target_pairs={{0,2},{1,3},{2,0},{3,1},{4,6},{5,7},{6,4},{7,5},{8,10},{9,11},{10,... | collective-permute-start | bytes 511496 | tf_op jit(solution)/shard_map/ppermute | solution.py:514
  94.9 3.3 %shard_map.123.refs_5_ = f32[4,48,2048]{2,1,0:T(8,128)S(1)} custom-call(s32[6]{0:T(128)S(1)} %stack.27.scalars, bf16[48,1920]{1,0:T(8,128)(2,1)S(1)} %get-tuple-element.112.rest_1_.refs_0_, bf16[48,1920]{1,0:T(8,128)(2,1)S(1)} %collective-permute-done.19.refs_1_, bf16[48,1920]{1,0:T(8,128)(2,1)S(1)} %collective-permute-done.23.refs_2_, ...), custom_call_target="tpu_custom_call" | custom-call | flops 1509949440 | bytes 7864320 | tf_op jit(solution)/shard_map/pallas_call | solution.py:491
  98.1 1.8 %collective-permute-done.22.refs_1_ = bf16[48,1776]{1,0:T(8,128)(2,1)S(1)} collective-permute-done((bf16[48,1776]{1,0:T(8,128)(2,1)S(1)}, bf16[48,1776]{1,0:T(8,128)(2,1)S(1)}, u32[]{:S(2)}, u32[]{:S(2)}) %collective-permute-start.22) | collective-permute-done | bytes 170528 | tf_op jit(solution)/shard_map/ppermute | solution.py:514
  100.0 1.4 %collective-permute-done.26.refs_3_ = bf16[48,1776]{1,0:T(8,128)(2,1)S(1)} collective-permute-done((bf16[48,1776]{1,0:T(8,128)(2,1)S(1)}, bf16[48,1776]{1,0:T(8,128)(2,1)S(1)}, u32[]{:S(2)}, u32[]{:S(2)}) %collective-permute-start.26) | collective-permute-done | bytes 170528 | tf_op jit(solution)/shard_map/ppermute | solution.py:510
  101.4 3.3 %shard_map.124 = (f32[24,2048]{1,0:T(8,128)S(1)}, bf16[24,2048]{1,0:T(8,128)(2,1)S(1)}, f32[24,2048]{1,0:T(8,128)S(1)}, bf16[24,2048]{1,0:T(8,128)(2,1)S(1)}, f3...) custom-call(s32[6]{0:T(128)S(1)} %stack.27.scalars, ...), custom_call_target="tpu_custom_call" | custom-call | flops 1396703232 | bytes 7274496 | tf_op jit(solution)/shard_map/pallas_call | solution.py:491
  104.6 0.6 collective-permute-start.27
  105.2 1.5 %collective-permute-start.29 = (bf16[24,2048]{1,0:T(8,128)(2,1)S(1)}, bf16[24,2048]{1,0:T(8,128)(2,1)S(1)}, u32[]{:S(2)}, u32[]{:S(2)}) collective-permute-start(bf16[24,2048]{1,0:T(8,128)(2,1)S(1)} %get-tuple-element.126), channel_id=1, source_target_pairs={{0,16},{16,0},{1,17},{17,1},{2,18},{18,2},{3,19},{19,3},{4,20},{20... | collective-permute-start | bytes 294920 | tf_op jit(solution)/shard_map/ppermute | solution.py:522
  107.3 1.5 %collective-permute-start.33 = (bf16[24,2048]{1,0:T(8,128)(2,1)S(1)}, bf16[24,2048]{1,0:T(8,128)(2,1)S(1)}, u32[]{:S(2)}, u32[]{:S(2)}) collective-permute-start(bf16[24,2048]{1,0:T(8,128)(2,1)S(1)} %get-tuple-element.130), channel_id=1, source_target_pairs={{0,16},{16,0},{1,17},{17,1},{2,18},{18,2},{3,19},{19,3},{4,20},{20... | collective-permute-start | bytes 294920 | tf_op jit(solution)/shard_map/ppermute | solution.py:522
  108.7 1.6 %collective-permute-done.27 = bf16[24,2048]{1,0:T(8,128)(2,1)S(1)} collective-permute-done((bf16[24,2048]{1,0:T(8,128)(2,1)S(1)}, bf16[24,2048]{1,0:T(8,128)(2,1)S(1)}, u32[]{:S(2)}, u32[]{:S(2)}) %collective-permute-start.27) | collective-permute-done | bytes 98336 | tf_op jit(solution)/shard_map/ppermute | solution.py:522
  110.4 2.4 %collective-permute-start.28 = (bf16[24,2048]{1,0:T(8,128)(2,1)S(1)}, bf16[24,2048]{1,0:T(8,128)(2,1)S(1)}, u32[]{:S(2)}, u32[]{:S(2)}) collective-permute-start(bf16[24,2048]{1,0:T(8,128)(2,1)S(1)} %add_convert_fusion.4), channel_id=1, source_target_pairs={{0,12},{4,8},{8,4},{12,0},{1,13},{5,9},{9,5},{13,1},{2,14},{6,10},... | collective-permute-start | bytes 294920 | tf_op jit(solution)/shard_map/ppermute | solution.py:518
  113.3 1.2 collective-permute-done.31
  114.6 0.9 collective-permute-start.32
  115.9 1.7 %collective-permute-done.28 = bf16[24,2048]{1,0:T(8,128)(2,1)S(1)} collective-permute-done((bf16[24,2048]{1,0:T(8,128)(2,1)S(1)}, bf16[24,2048]{1,0:T(8,128)(2,1)S(1)}, u32[]{:S(2)}, u32[]{:S(2)}) %collective-permute-start.28) | collective-permute-done | bytes 98336 | tf_op jit(solution)/shard_map/ppermute | solution.py:518
  117.5 3.3 %collective-permute-done.30 = bf16[24,2048]{1,0:T(8,128)(2,1)S(1)} collective-permute-done((bf16[24,2048]{1,0:T(8,128)(2,1)S(1)}, bf16[24,2048]{1,0:T(8,128)(2,1)S(1)}, u32[]{:S(2)}, u32[]{:S(2)}) %collective-permute-start.30) | collective-permute-done | bytes 98336 | tf_op jit(solution)/shard_map/ppermute | solution.py:518
  120.9 0.7 select_convert_fusion
  (49 shorter events, 6.0 us)
Async XLA Ops:
  12.7 1.7 %collective-permute-start = (bf16[96,1024]{1,0:T(8,128)(2,1)S(1)}, bf16[96,1024]{1,0:T(8,128)(2,1)S(1)}, u32[]{:S(2)}, u32[]{:S(2)}) collective-permute-start(bf16[96,1024]{1,0:T(8,128)(2,1)S(1)} %get-tuple-element.69), channel_id=1, source_target_pairs={{0,1},{1,0},{2,3},{3,2},{4,5},{5,4},{6,7},{7,6},{8,9},{9,8},{10,11... | collective-permute-start | bytes 589832 | tf_op jit(solution)/shard_map/ppermute | solution.py:510
  13.2 1.2 collective-permute-start.1
  14.8 8.2 %collective-permute-start.2 = (bf16[96,1024]{1,0:T(8,128)(2,1)S(1)}, bf16[96,1024]{1,0:T(8,128)(2,1)S(1)}, u32[]{:S(2)}, u32[]{:S(2)}) collective-permute-start(bf16[96,1024]{1,0:T(8,128)(2,1)S(1)} %get-tuple-element.73.a_ref), channel_id=1, source_target_pairs={{0,2},{1,3},{2,0},{3,1},{4,6},{5,7},{6,4},{7,5},{8,10},{9,11},{10,... | collective-permute-start | bytes 589832 | tf_op jit(solution)/shard_map/ppermute | solution.py:514
  17.6 5.4 %collective-permute-start.3 = (f32[8,128]{1,0:T(8,128)S(1)}, f32[8,128]{1,0:T(8,128)S(1)}, u32[]{:S(2)}, u32[]{:S(2)}) collective-permute-start(f32[8,128]{1,0:T(8,128)S(1)} %get-tuple-element.74.lse_a_ref), channel_id=1, source_target_pairs={{0,2},{1,3},{2,0},{3,1},{4,6},{5,7},{6,4},{7,5},{8,10},{9,11},{10,... | collective-permute-start | bytes 12296 | tf_op jit(solution)/shard_map/ppermute | solution.py:514
  24.0 1.4 %collective-permute-start.4 = (bf16[96,1024]{1,0:T(8,128)(2,1)S(1)}, bf16[96,1024]{1,0:T(8,128)(2,1)S(1)}, u32[]{:S(2)}, u32[]{:S(2)}) collective-permute-start(bf16[96,1024]{1,0:T(8,128)(2,1)S(1)} %get-tuple-element.77.keep_ref), channel_id=1, source_target_pairs={{0,1},{1,0},{2,3},{3,2},{4,5},{5,4},{6,7},{7,6},{8,9},{9,8},{10,11... | collective-permute-start | bytes 589832 | tf_op jit(solution)/shard_map/ppermute | solution.py:510
  28.1 12.1 %collective-permute-start.5 = (bf16[24,2048]{1,0:T(8,128)(2,1)S(1)}, bf16[24,2048]{1,0:T(8,128)(2,1)S(1)}, u32[]{:S(2)}, u32[]{:S(2)}) collective-permute-start(bf16[24,2048]{1,0:T(8,128)(2,1)S(1)} %get-tuple-element.81), channel_id=1, source_target_pairs={{0,4},{4,0},{8,12},{12,8},{1,5},{5,1},{9,13},{13,9},{2,6},{6,2},{1... | collective-permute-start | bytes 294920 | tf_op jit(solution)/shard_map/ppermute | solution.py:518
  30.0 10.2 %collective-permute-start.6 = (bf16[24,2048]{1,0:T(8,128)(2,1)S(1)}, bf16[24,2048]{1,0:T(8,128)(2,1)S(1)}, u32[]{:S(2)}, u32[]{:S(2)}) collective-permute-start(bf16[24,2048]{1,0:T(8,128)(2,1)S(1)} %get-tuple-element.82), channel_id=1, source_target_pairs={{0,12},{4,8},{8,4},{12,0},{1,13},{5,9},{9,5},{13,1},{2,14},{6,10},... | collective-permute-start | bytes 294920 | tf_op jit(solution)/shard_map/ppermute | solution.py:518
  32.5 9.2 %copy-start = (bf16[96,2048]{1,0:T(8,128)(2,1)S(1)}, bf16[96,2048]{1,0:T(8,128)(2,1)}, u32[]{:S(2)}) copy-start(bf16[96,2048]{1,0:T(8,128)(2,1)} %resid_ref.1) | copy-start | bytes 1179652
  32.5 23.3 %copy-start.1 = (bf16[2048]{0:T(1024)(128)(2,1)S(1)}, bf16[2048]{0:T(1024)(128)(2,1)}, u32[]{:S(2)}) copy-start(bf16[2048]{0:T(1024)(128)(2,1)} %param.18) | copy-start | bytes 12292
  32.5 9.2 %collective-permute-start.7 = (bf16[24,2048]{1,0:T(8,128)(2,1)S(1)}, bf16[24,2048]{1,0:T(8,128)(2,1)S(1)}, u32[]{:S(2)}, u32[]{:S(2)}) collective-permute-start(bf16[24,2048]{1,0:T(8,128)(2,1)S(1)} %get-tuple-element.83), channel_id=1, source_target_pairs={{0,8},{4,12},{8,0},{12,4},{1,9},{5,13},{9,1},{13,5},{2,10},{6,14},... | collective-permute-start | bytes 294920 | tf_op jit(solution)/shard_map/ppermute | solution.py:518
  42.4 4.8 %collective-permute-start.9 = (bf16[24,2048]{1,0:T(8,128)(2,1)S(1)}, bf16[24,2048]{1,0:T(8,128)(2,1)S(1)}, u32[]{:S(2)}, u32[]{:S(2)}) collective-permute-start(bf16[24,2048]{1,0:T(8,128)(2,1)S(1)} %shard_map.115.refs_0_), channel_id=1, source_target_pairs={{0,16},{16,0},{1,17},{17,1},{2,18},{18,2},{3,19},{19,3},{4,20},{20... | collective-permute-start | bytes 294920 | tf_op jit(solution)/shard_map/ppermute | solution.py:522
  44.0 6.7 %collective-permute-start.8 = (bf16[24,2048]{1,0:T(8,128)(2,1)S(1)}, bf16[24,2048]{1,0:T(8,128)(2,1)S(1)}, u32[]{:S(2)}, u32[]{:S(2)}) collective-permute-start(bf16[24,2048]{1,0:T(8,128)(2,1)S(1)} %shard_map.115.refs_0_), channel_id=1, source_target_pairs={{0,8},{4,12},{8,0},{12,4},{1,9},{5,13},{9,1},{13,5},{2,10},{6,14},... | collective-permute-start | bytes 294920 | tf_op jit(solution)/shard_map/ppermute | solution.py:518
  45.3 6.2 %collective-permute-start.10 = (bf16[24,2048]{1,0:T(8,128)(2,1)S(1)}, bf16[24,2048]{1,0:T(8,128)(2,1)S(1)}, u32[]{:S(2)}, u32[]{:S(2)}) collective-permute-start(bf16[24,2048]{1,0:T(8,128)(2,1)S(1)} %shard_map.115.refs_0_), channel_id=1, source_target_pairs={{0,4},{4,0},{8,12},{12,8},{1,5},{5,1},{9,13},{13,9},{2,6},{6,2},{1... | collective-permute-start | bytes 294920 | tf_op jit(solution)/shard_map/ppermute | solution.py:518
  50.6 4.6 %collective-permute-start.13 = (bf16[24,2048]{1,0:T(8,128)(2,1)S(1)}, bf16[24,2048]{1,0:T(8,128)(2,1)S(1)}, u32[]{:S(2)}, u32[]{:S(2)}) collective-permute-start(bf16[24,2048]{1,0:T(8,128)(2,1)S(1)} %collective-permute-done.8.refs_4_), channel_id=1, source_target_pairs={{0,4},{4,0},{8,12},{12,8},{1,5},{5,1},{9,13},{13,9},{2,6},{6,2},{1... | collective-permute-start | bytes 294920 | tf_op jit(solution)/shard_map/ppermute | solution.py:518
  50.9 8.0 %collective-permute-start.12 = (bf16[24,2048]{1,0:T(8,128)(2,1)S(1)}, bf16[24,2048]{1,0:T(8,128)(2,1)S(1)}, u32[]{:S(2)}, u32[]{:S(2)}) collective-permute-start(bf16[24,2048]{1,0:T(8,128)(2,1)S(1)} %collective-permute-done.8.refs_4_), channel_id=1, source_target_pairs={{0,16},{16,0},{1,17},{17,1},{2,18},{18,2},{3,19},{19,3},{4,20},{20... | collective-permute-start | bytes 294920 | tf_op jit(solution)/shard_map/ppermute | solution.py:522
  51.4 7.5 %collective-permute-start.11 = (bf16[24,2048]{1,0:T(8,128)(2,1)S(1)}, bf16[24,2048]{1,0:T(8,128)(2,1)S(1)}, u32[]{:S(2)}, u32[]{:S(2)}) collective-permute-start(bf16[24,2048]{1,0:T(8,128)(2,1)S(1)} %collective-permute-done.10.refs_2_), channel_id=1, source_target_pairs={{0,16},{16,0},{1,17},{17,1},{2,18},{18,2},{3,19},{19,3},{4,20},{20... | collective-permute-start | bytes 294920 | tf_op jit(solution)/shard_map/ppermute | solution.py:522
  55.3 4.6 %collective-permute-start.14 = (bf16[24,2048]{1,0:T(8,128)(2,1)S(1)}, bf16[24,2048]{1,0:T(8,128)(2,1)S(1)}, u32[]{:S(2)}, u32[]{:S(2)}) collective-permute-start(bf16[24,2048]{1,0:T(8,128)(2,1)S(1)} %collective-permute-done.13.refs_6_), channel_id=1, source_target_pairs={{0,16},{16,0},{1,17},{17,1},{2,18},{18,2},{3,19},{19,3},{4,20},{20... | collective-permute-start | bytes 294920 | tf_op jit(solution)/shard_map/ppermute | solution.py:522
  66.7 1.8 %collective-permute-start.16 = (bf16[2,48,2048]{2,1,0:T(8,128)(2,1)S(1)}, bf16[2,48,2048]{2,1,0:T(8,128)(2,1)S(1)}, u32[]{:S(2)}, u32[]{:S(2)}) collective-permute-start(bf16[2,48,2048]{2,1,0:T(8,128)(2,1)S(1)} %get-tuple-element.100), channel_id=1, source_target_pairs={{0,1},{1,0},{2,3},{3,2},{4,5},{5,4},{6,7},{7,6},{8,9},{9,8},{10,11... | collective-permute-start | bytes 1179656 | tf_op jit(solution)/shard_map/ppermute | solution.py:510
  68.6 11.2 %collective-permute-start.18 = (bf16[2,48,2048]{2,1,0:T(8,128)(2,1)S(1)}, bf16[2,48,2048]{2,1,0:T(8,128)(2,1)S(1)}, u32[]{:S(2)}, u32[]{:S(2)}) collective-permute-start(bf16[2,48,2048]{2,1,0:T(8,128)(2,1)S(1)} %add_convert_fusion), channel_id=1, source_target_pairs={{0,2},{1,3},{2,0},{3,1},{4,6},{5,7},{6,4},{7,5},{8,10},{9,11},{10,... | collective-permute-start | bytes 1179656 | tf_op jit(solution)/shard_map/ppermute | solution.py:514
  75.7 1.7 %collective-permute-start.17 = (bf16[2,48,1776]{2,1,0:T(8,128)(2,1)S(1)}, bf16[2,48,1776]{2,1,0:T(8,128)(2,1)S(1)}, u32[]{:S(2)}, u32[]{:S(2)}) collective-permute-start(bf16[2,48,1776]{2,1,0:T(8,128)(2,1)S(1)} %get-tuple-element.104), channel_id=1, source_target_pairs={{0,1},{1,0},{2,3},{3,2},{4,5},{5,4},{6,7},{7,6},{8,9},{9,8},{10,11... | collective-permute-start | bytes 1022984 | tf_op jit(solution)/shard_map/ppermute | solution.py:510
  75.8 11.0 %collective-permute-start.15 = (bf16[2,48,2048]{2,1,0:T(8,128)(2,1)S(1)}, bf16[2,48,2048]{2,1,0:T(8,128)(2,1)S(1)}, u32[]{:S(2)}, u32[]{:S(2)}) collective-permute-start(bf16[2,48,2048]{2,1,0:T(8,128)(2,1)S(1)} %get-tuple-element.98), channel_id=1, source_target_pairs={{0,1},{1,0},{2,3},{3,2},{4,5},{5,4},{6,7},{7,6},{8,9},{9,8},{10,11... | collective-permute-start | bytes 1179656 | tf_op jit(solution)/shard_map/ppermute | solution.py:510
  76.3 11.5 %collective-permute-start.20 = (bf16[2,48,1776]{2,1,0:T(8,128)(2,1)S(1)}, bf16[2,48,1776]{2,1,0:T(8,128)(2,1)S(1)}, u32[]{:S(2)}, u32[]{:S(2)}) collective-permute-start(bf16[2,48,1776]{2,1,0:T(8,128)(2,1)S(1)} %get-tuple-element.114), channel_id=1, source_target_pairs={{0,1},{1,0},{2,3},{3,2},{4,5},{5,4},{6,7},{7,6},{8,9},{9,8},{10,11... | collective-permute-start | bytes 1022984 | tf_op jit(solution)/shard_map/ppermute | solution.py:510
  79.9 9.7 %collective-permute-start.21 = (bf16[2,48,1776]{2,1,0:T(8,128)(2,1)S(1)}, bf16[2,48,1776]{2,1,0:T(8,128)(2,1)S(1)}, u32[]{:S(2)}, u32[]{:S(2)}) collective-permute-start(bf16[2,48,1776]{2,1,0:T(8,128)(2,1)S(1)} %add_convert_fusion.1), channel_id=1, source_target_pairs={{0,2},{1,3},{2,0},{3,1},{4,6},{5,7},{6,4},{7,5},{8,10},{9,11},{10,... | collective-permute-start | bytes 1022984 | tf_op jit(solution)/shard_map/ppermute | solution.py:514
  87.1 6.0 %collective-permute-start.19 = (bf16[48,1920]{1,0:T(8,128)(2,1)S(1)}, bf16[48,1920]{1,0:T(8,128)(2,1)S(1)}, u32[]{:S(2)}, u32[]{:S(2)}) collective-permute-start(bf16[48,1920]{1,0:T(8,128)(2,1)S(1)} %get-tuple-element.112.rest_1_.refs_0_), channel_id=1, source_target_pairs={{0,2},{1,3},{2,0},{3,1},{4,6},{5,7},{6,4},{7,5},{8,10},{9,11},{10,... | collective-permute-start | bytes 552968 | tf_op jit(solution)/shard_map/ppermute | solution.py:514
  87.7 7.2 %collective-permute-start.23 = (bf16[48,1920]{1,0:T(8,128)(2,1)S(1)}, bf16[48,1920]{1,0:T(8,128)(2,1)S(1)}, u32[]{:S(2)}, u32[]{:S(2)}) collective-permute-start(bf16[48,1920]{1,0:T(8,128)(2,1)S(1)} %get-tuple-element.112.rest_1_.refs_0_), channel_id=1, source_target_pairs={{0,1},{1,0},{2,3},{3,2},{4,5},{5,4},{6,7},{7,6},{8,9},{9,8},{10,11... | collective-permute-start | bytes 552968 | tf_op jit(solution)/shard_map/ppermute | solution.py:510
  93.2 1.7 %collective-permute-start.24 = (bf16[48,1920]{1,0:T(8,128)(2,1)S(1)}, bf16[48,1920]{1,0:T(8,128)(2,1)S(1)}, u32[]{:S(2)}, u32[]{:S(2)}) collective-permute-start(bf16[48,1920]{1,0:T(8,128)(2,1)S(1)} %collective-permute-done.19.refs_1_), channel_id=1, source_target_pairs={{0,1},{1,0},{2,3},{3,2},{4,5},{5,4},{6,7},{7,6},{8,9},{9,8},{10,11... | collective-permute-start | bytes 552968 | tf_op jit(solution)/shard_map/ppermute | solution.py:510
  93.2 6.8 %collective-permute-start.22 = (bf16[48,1776]{1,0:T(8,128)(2,1)S(1)}, bf16[48,1776]{1,0:T(8,128)(2,1)S(1)}, u32[]{:S(2)}, u32[]{:S(2)}) collective-permute-start(bf16[48,1776]{1,0:T(8,128)(2,1)S(1)} %shard_map.122.refs_0_), channel_id=1, source_target_pairs={{0,2},{1,3},{2,0},{3,1},{4,6},{5,7},{6,4},{7,5},{8,10},{9,11},{10,... | collective-permute-start | bytes 511496 | tf_op jit(solution)/shard_map/ppermute | solution.py:514
  94.7 5.3 %collective-permute-start.25 = (bf16[48,1776]{1,0:T(8,128)(2,1)S(1)}, bf16[48,1776]{1,0:T(8,128)(2,1)S(1)}, u32[]{:S(2)}, u32[]{:S(2)}) collective-permute-start(bf16[48,1776]{1,0:T(8,128)(2,1)S(1)} %shard_map.122.refs_0_), channel_id=1, source_target_pairs={{0,1},{1,0},{2,3},{3,2},{4,5},{5,4},{6,7},{7,6},{8,9},{9,8},{10,11... | collective-permute-start | bytes 511496 | tf_op jit(solution)/shard_map/ppermute | solution.py:510
  99.9 1.4 %collective-permute-start.26 = (bf16[48,1776]{1,0:T(8,128)(2,1)S(1)}, bf16[48,1776]{1,0:T(8,128)(2,1)S(1)}, u32[]{:S(2)}, u32[]{:S(2)}) collective-permute-start(bf16[48,1776]{1,0:T(8,128)(2,1)S(1)} %collective-permute-done.22.refs_1_), channel_id=1, source_target_pairs={{0,1},{1,0},{2,3},{3,2},{4,5},{5,4},{6,7},{7,6},{8,9},{9,8},{10,11... | collective-permute-start | bytes 511496 | tf_op jit(solution)/shard_map/ppermute | solution.py:510
  104.6 5.7 %collective-permute-start.27 = (bf16[24,2048]{1,0:T(8,128)(2,1)S(1)}, bf16[24,2048]{1,0:T(8,128)(2,1)S(1)}, u32[]{:S(2)}, u32[]{:S(2)}) collective-permute-start(bf16[24,2048]{1,0:T(8,128)(2,1)S(1)} %get-tuple-element.124), channel_id=1, source_target_pairs={{0,16},{16,0},{1,17},{17,1},{2,18},{18,2},{3,19},{19,3},{4,20},{20... | collective-permute-start | bytes 294920 | tf_op jit(solution)/shard_map/ppermute | solution.py:522
  105.2 7.5 %collective-permute-start.29 = (bf16[24,2048]{1,0:T(8,128)(2,1)S(1)}, bf16[24,2048]{1,0:T(8,128)(2,1)S(1)}, u32[]{:S(2)}, u32[]{:S(2)}) collective-permute-start(bf16[24,2048]{1,0:T(8,128)(2,1)S(1)} %get-tuple-element.126), channel_id=1, source_target_pairs={{0,16},{16,0},{1,17},{17,1},{2,18},{18,2},{3,19},{19,3},{4,20},{20... | collective-permute-start | bytes 294920 | tf_op jit(solution)/shard_map/ppermute | solution.py:522
  106.7 7.8 %collective-permute-start.31 = (bf16[24,2048]{1,0:T(8,128)(2,1)S(1)}, bf16[24,2048]{1,0:T(8,128)(2,1)S(1)}, u32[]{:S(2)}, u32[]{:S(2)}) collective-permute-start(bf16[24,2048]{1,0:T(8,128)(2,1)S(1)} %get-tuple-element.128), channel_id=1, source_target_pairs={{0,16},{16,0},{1,17},{17,1},{2,18},{18,2},{3,19},{19,3},{4,20},{20... | collective-permute-start | bytes 294920 | tf_op jit(solution)/shard_map/ppermute | solution.py:522
  107.3 8.6 %collective-permute-start.33 = (bf16[24,2048]{1,0:T(8,128)(2,1)S(1)}, bf16[24,2048]{1,0:T(8,128)(2,1)S(1)}, u32[]{:S(2)}, u32[]{:S(2)}) collective-permute-start(bf16[24,2048]{1,0:T(8,128)(2,1)S(1)} %get-tuple-element.130), channel_id=1, source_target_pairs={{0,16},{16,0},{1,17},{17,1},{2,18},{18,2},{3,19},{19,3},{4,20},{20... | collective-permute-start | bytes 294920 | tf_op jit(solution)/shard_map/ppermute | solution.py:522
  110.4 7.2 %collective-permute-start.28 = (bf16[24,2048]{1,0:T(8,128)(2,1)S(1)}, bf16[24,2048]{1,0:T(8,128)(2,1)S(1)}, u32[]{:S(2)}, u32[]{:S(2)}) collective-permute-start(bf16[24,2048]{1,0:T(8,128)(2,1)S(1)} %add_convert_fusion.4), channel_id=1, source_target_pairs={{0,12},{4,8},{8,4},{12,0},{1,13},{5,9},{9,5},{13,1},{2,14},{6,10},... | collective-permute-start | bytes 294920 | tf_op jit(solution)/shard_map/ppermute | solution.py:518
  112.8 8.0 %collective-permute-start.30 = (bf16[24,2048]{1,0:T(8,128)(2,1)S(1)}, bf16[24,2048]{1,0:T(8,128)(2,1)S(1)}, u32[]{:S(2)}, u32[]{:S(2)}) collective-permute-start(bf16[24,2048]{1,0:T(8,128)(2,1)S(1)} %add_convert_fusion.3), channel_id=1, source_target_pairs={{0,8},{4,12},{8,0},{12,4},{1,9},{5,13},{9,1},{13,5},{2,10},{6,14},... | collective-permute-start | bytes 294920 | tf_op jit(solution)/shard_map/ppermute | solution.py:518
  114.6 6.3 %collective-permute-start.32 = (bf16[24,2048]{1,0:T(8,128)(2,1)S(1)}, bf16[24,2048]{1,0:T(8,128)(2,1)S(1)}, u32[]{:S(2)}, u32[]{:S(2)}) collective-permute-start(bf16[24,2048]{1,0:T(8,128)(2,1)S(1)} %add_convert_fusion.2), channel_id=1, source_target_pairs={{0,4},{4,0},{8,12},{12,8},{1,5},{5,1},{9,13},{13,9},{2,6},{6,2},{1... | collective-permute-start | bytes 294920 | tf_op jit(solution)/shard_map/ppermute | solution.py:518

commit v5 on v4

--- a/solution.py
+++ b/solution.py
@@ -9,8 +9,8 @@
 from jax.sharding import PartitionSpec as P
 
 DH = 128
-TILE = 640
-CHUNKS = (3, 3)
+TILE = 1920
+CHUNKS = (1, 1)
 HEADS = 4
 THIN = 1
 NEGATIVE = -1e30
@@ -167,17 +167,18 @@
     return call(scalars, queries, kv_cache, kv_cache, new_kv, new_kv)
 
 
-def combine_kernel(a_ref, b_ref, lse_a_ref, lse_b_ref, *rest):
-    out_ref, lse_ref = rest[-2:]
+def combine_kernel(last, a_ref, b_ref, lse_a_ref, lse_b_ref, *rest):
+    out_ref = rest[-1] if last else rest[-2]
     span = a_ref.shape[0]
     heads = lse_a_ref.shape[0]
     lse_a, lse_b = lse_a_ref[...], lse_b_ref[...]
     top = jnp.maximum(lse_a, lse_b)
     left, right = jnp.exp(lse_a - top), jnp.exp(lse_b - top)
     total = left + right
-    lse_ref[...] = top + jnp.log(total)
-    rest = jnp.zeros((128 - 2 * heads, 128), F32)
-    table = jnp.transpose(jnp.concatenate([left / total, right / total, rest], axis=0))
+    if not last:
+        rest[-1][...] = top + jnp.log(total)
+    pad = jnp.zeros((128 - 2 * heads, 128), F32)
+    table = jnp.transpose(jnp.concatenate([left / total, right / total, pad], axis=0))
     for h in range(heads):
         cols = slice(h * DH, (h + 1) * DH)
         mixed = a_ref[:, cols].astype(F32) * table[0:span, h : h + 1]
@@ -185,13 +186,13 @@
         out_ref[:, cols] = mixed.astype(BF16)
 
 
-def combine(a, b, lse_a, lse_b, *behind):
+def combine(a, b, lse_a, lse_b, last, *behind):
+    shapes = [jax.ShapeDtypeStruct(a.shape, BF16)]
+    if not last:
+        shapes.append(jax.ShapeDtypeStruct(lse_a.shape, F32))
     return pl.pallas_call(
-        combine_kernel,
-        out_shape=[
-            jax.ShapeDtypeStruct(a.shape, BF16),
-            jax.ShapeDtypeStruct(lse_a.shape, F32),
-        ],
+        functools.partial(combine_kernel, last),
+        out_shape=shapes,
         compiler_params=params(),
         cost_estimate=cost(4 * a.size, 6 * a.size),
     )(a, b, lse_a, lse_b, *behind)
@@ -233,7 +234,7 @@
 
 def project(scalars, keep, other, out_weight, tp_size):
     span, width = keep.shape
-    depth = 512
+    depth = width
     half = width // depth
     cols = out_weight.shape[1]
     rows = span // tp_size
@@ -332,51 +333,34 @@
     )(scalars, *sources, gain, mark)
 
 
-def gate_up_kernel(tiles, scaled_ref, gate_ref, up_ref, *rest):
+def gate_up_kernel(scaled_ref, gate_ref, up_ref, *rest):
     homes = rest[-4:]
     high = homes[0].shape[1]
-
-    def multiply():
-        for which, weight in enumerate((gate_ref, up_ref)):
-            term = jnp.dot(weight[...], scaled_ref[...], preferred_element_type=F32)
-            term = jnp.transpose(term).astype(BF16)
-            for place, home in enumerate(homes):
-                home[which] = term[place * high : (place + 1) * high]
-
-    if len(rest) == 4:
-        multiply()
-        return
-    square_ref = rest[0]
-    step = pl.program_id(0)
-    pl.when(step < tiles)(multiply)
-
-    @pl.when(step == tiles)
-    def squares():
+    width = gate_ref.shape[0]
+    for which, weight in enumerate((gate_ref, up_ref)):
+        term = jnp.dot(weight[...], scaled_ref[...], preferred_element_type=F32)
+        term = jnp.transpose(term).astype(BF16)
         for place, home in enumerate(homes):
-            home[0, :, 0:128] = square_ref[place].astype(BF16)
-            home[1, :, 0:128] = jnp.zeros((high, 128), BF16)
+            home[which, :, 0:width] = term[place * high : (place + 1) * high]
+    if len(rest) > 4:
+        for place, home in enumerate(homes):
+            home[0, :, width:] = rest[0][place].astype(BF16)
+            home[1, :, width:] = jnp.zeros((high, 128), BF16)
 
 
 def gate_up(scaled, gate_weight, up_weight, width, squares=None):
     depth, rows = scaled.shape
     high = rows // 4
-    tiles = pl.cdiv(width, TILE)
-    weight = pl.BlockSpec((TILE, depth), lambda j: (jnp.minimum(j, tiles - 1), 0))
-    piece = pl.BlockSpec((2, high, TILE), lambda j: (0, 0, j))
+    flops, moved = 4 * rows * depth * width, 4 * depth * width
     ins = [scaled, gate_weight, up_weight]
-    specs = [whole(scaled.shape), weight, weight]
     if squares is not None:
         ins.append(squares)
-        specs.append(whole(squares.shape))
         width += 128
     return pl.pallas_call(
-        functools.partial(gate_up_kernel, tiles),
-        grid=(tiles + len(ins) - 3,),
-        in_specs=specs,
-        out_specs=[piece] * 4,
+        gate_up_kernel,
         out_shape=[jax.ShapeDtypeStruct((2, high, width), BF16)] * 4,
         compiler_params=params(),
-        cost_estimate=cost(4 * rows * depth * width, 4 * depth * width),
+        cost_estimate=cost(flops, moved),
     )(*ins)
 
 
@@ -437,10 +421,12 @@
         else:
             acc[...] = jnp.zeros_like(acc)
 
-    start = pl.multiple_of(step * depth, depth)
-
     def add(weight):
-        term = jnp.dot(packed[:, pl.ds(start, depth)], weight, preferred_element_type=F32)
+        if packed.shape[1] == depth:
+            part = packed[...]
+        else:
+            part = packed[:, pl.ds(pl.multiple_of(step * depth, depth), depth)]
+        term = jnp.dot(part, weight, preferred_element_type=F32)
         acc[...] += term.reshape(acc.shape)
 
     if width % depth:
@@ -473,9 +459,10 @@
 def down(scalars, hidden, down_weight, start, slots, last):
     high, width = hidden[0].shape
     cols = down_weight.shape[1]
-    steps = pl.cdiv(width, TILE)
+    tile = min(TILE, width)
+    steps = pl.cdiv(width, tile)
     rows = high // slots
-    ins = [whole((high, width))] * 4 + [pl.BlockSpec((TILE, cols), lambda i, s: (i, 0))]
+    ins = [whole((high, width))] * 4 + [pl.BlockSpec((tile, cols), lambda i, s: (i, 0))]
     args = list(hidden) + [down_weight]
     if start is not None:
         ins.append(whole((4, high, cols)))
@@ -497,7 +484,7 @@
             out_specs=[whole(shape.shape) for shape in shapes],
             scratch_shapes=[
                 pltpu.VMEM((4, high, cols), F32),
-                pltpu.VMEM((4 * high, steps * TILE), BF16),
+                pltpu.VMEM((4 * high, steps * tile), BF16),
             ],
         ),
         out_shape=shapes,
@@ -558,10 +545,10 @@
     scalars = lax.optimization_barrier(scalars)
     sent, kept, sent_lse, kept_lse = attention(scalars, queries, kv_cache, new_kv)
     got, got_lse = to_core(sent), to_core(sent_lse)
-    kept, kept_lse = combine(kept, got, kept_lse, got_lse)
+    kept, kept_lse = combine(kept, got, kept_lse, got_lse, False)
     (out_held,), mark, kept = fetch([out_weight], [(0, out_weight.shape[0])], kept)
     got, got_lse = to_x(kept), to_x(kept_lse)
-    mine, unused = combine(kept, got, kept_lse, got_lse, mark)
+    (mine,) = combine(kept, got, kept_lse, got_lse, True, mark)
     other = to_core(mine)
 
     terms = list(project(scalars, mine, other, out_held, tp_size))

time: 122 us -> 119 us (0.975)
  Pallas kernels: 54.8 us -> 49.9 us
  waiting for transfers between devices: 34.5 us -> 36.7 us
    pallas_call x4, Pallas kernels: 12.5 us -> 9.69 us  [the longest x2 8.85 us: gate_up(): pl.pallas_call(gate_up_kernel, out_shape=[jax.ShapeDtypeStruct((2, high,...]
    ppermute x6, waiting for transfers between devices: 11.2 us -> 13.5 us  [to_x(): return lax.ppermute(x, 'ffn', [(i, i ^ 2) for i in range(4)])]
    pallas_call x2, Pallas kernels: 6.51 us -> 4.63 us  [down(): pl.pallas_call(functools.partial(down_kernel, width, slots, start is not...]
  transfers between devices with their start and end apart: 34 -> 34, of which waited for: 20 -> 20; matrix products, arithmetic and copies ran while one was open for 0% -> 0% of each run, Pallas kernels for 24% -> 22%
where the time goes in v5:
time: 119 us
  Pallas kernels  49.9 us (42%)
  waiting for transfers between devices  36.7 us (31%)
  starting transfers between devices  29.8 us (25%)
  between operations  1.52 us (1%)
    pallas_call x4, Pallas kernels, fetch(): pl.pallas_call(functools.partial(fetch_kernel, pieces), in_specs=[pl.Bloc...  19.4 us
    ppermute x6, waiting for transfers between devices, to_x(): return lax.ppermute(x, 'ffn', [(i, i ^ 2) for i in range(4)])  13.5 us
    ppermute x9, waiting for transfers between devices, to_z(): return lax.ppermute(x, 'tp', [(i, i ^ k) for i in range(4)])  12.3 us
    ppermute x9, starting transfers between devices, to_z(): return lax.ppermute(x, 'tp', [(i, i ^ k) for i in range(4)])  11.8 us
    pallas_call x1, Pallas kernels, attention(): return call(scalars, queries, kv_cache, kv_cache, new_kv, new_kv)  11.3 us
    pallas_call x2, Pallas kernels, gate_up(): pl.pallas_call(gate_up_kernel, out_shape=[jax.ShapeDtypeStruct((2, high,...  8.85 us
    ppermute x8, starting transfers between devices, to_y(): return lax.ppermute(x, 'grp', [(0, 1), (1, 0)])  8.23 us
    ppermute x6, starting transfers between devices, to_x(): return lax.ppermute(x, 'ffn', [(i, i ^ 2) for i in range(4)])  8.1 us
  transfers between devices with their start and end apart: 34, of which 20 were waited for; matrix products, arithmetic and copies ran while one was open for 0% of the time, Pallas kernels for 22%

profile of v5, /device:TPU:0, one launch (start us, length us, event | category | flops | bytes accessed | tf_op | source)
XLA Modules:
  0.0 119.0 jit_solution(15202345418051389969)
XLA Ops:
  1.4 11.3 %shard_map.109 = (bf16[96,1024]{1,0:T(8,128)(2,1)S(1)}, bf16[96,1024]{1,0:T(8,128)(2,1)S(1)}, f32[8,128]{1,0:T(8,128)S(1)}, f32[8,128]{1,0:T(8,128)S(1)}) custom-call(s32[6]{0:T(128)S(1)} %stack.27.scalars, bf16[96,2048]{1,0:T(8,128)(2,1)} %q_ref.1, bf16[2,1,2048,256]{3,2,1,0:T(8,128)(2,1)} %value_ref.1, bf16[2,1,2048,256]{3,2,1,0:T(8,128)(2,1)} %value_ref.1, ...), custom_call_target="tpu_custom_call" | custom-call | flops 1610612736 | bytes 2097152 | tf_op jit(solution)/shard_map/pallas_call | solution.py:167
  13.3 1.1 collective-permute-done.1.lse_b_ref
  14.8 2.8 %collective-permute-start.2 = (bf16[96,1024]{1,0:T(8,128)(2,1)S(1)}, bf16[96,1024]{1,0:T(8,128)(2,1)S(1)}, u32[]{:S(2)}, u32[]{:S(2)}) collective-permute-start(bf16[96,1024]{1,0:T(8,128)(2,1)S(1)} %get-tuple-element.72.a_ref), channel_id=1, source_target_pairs={{0,2},{1,3},{2,0},{3,1},{4,6},{5,7},{6,4},{7,5},{8,10},{9,11},{10,... | collective-permute-start | bytes 589832 | tf_op jit(solution)/shard_map/ppermute | solution.py:501
  17.7 3.4 %shard_map.111 = (bf16[2048,2048]{1,0:T(8,128)(2,1)S(1)}, f32[8,128]{1,0:T(8,128)S(1)}) custom-call(bf16[2048,2048]{1,0:T(8,128)(2,1)} %refs_0_), custom_call_target="tpu_custom_call" | custom-call | bytes 16777216 | tf_op jit(solution)/shard_map/pallas_call | solution.py:62
  21.1 1.9 %collective-permute-done.3.lse_b_ref = f32[8,128]{1,0:T(8,128)S(1)} collective-permute-done((f32[8,128]{1,0:T(8,128)S(1)}, f32[8,128]{1,0:T(8,128)S(1)}, u32[]{:S(2)}, u32[]{:S(2)}) %collective-permute-start.3) | collective-permute-done | bytes 4128 | tf_op jit(solution)/shard_map/ppermute | solution.py:501
  23.5 1.4 %collective-permute-done.4.other_ref = bf16[96,1024]{1,0:T(8,128)(2,1)S(1)} collective-permute-done((bf16[96,1024]{1,0:T(8,128)(2,1)S(1)}, bf16[96,1024]{1,0:T(8,128)(2,1)S(1)}, u32[]{:S(2)}, u32[]{:S(2)}) %collective-permute-start.4) | collective-permute-done | bytes 196640 | tf_op jit(solution)/shard_map/ppermute | solution.py:497
  25.0 2.5 %shard_map.113 = (f32[24,2048]{1,0:T(8,128)S(1)}, bf16[24,2048]{1,0:T(8,128)(2,1)S(1)}, bf16[24,2048]{1,0:T(8,128)(2,1)S(1)}, bf16[24,2048]{1,0:T(8,128)(2,1)S(1)}) custom-call(s32[6]{0:T(128)S(1)} %stack.27.scalars, bf16[96,1024]{1,0:T(8,128)(2,1)S(1)} %shard_map.112.keep_ref, bf16[96,1024]{1,0:T(8,128)(2,1)S(1)} %collective-permute-done.4.other_ref, ...), custom_call_target="tpu_custom_call" | custom-call | flops 805306368 | bytes 8388608 | tf_op jit(solution)/shard_map/pallas_call | solution.py:241
  27.4 1.9 %collective-permute-start.5 = (bf16[24,2048]{1,0:T(8,128)(2,1)S(1)}, bf16[24,2048]{1,0:T(8,128)(2,1)S(1)}, u32[]{:S(2)}, u32[]{:S(2)}) collective-permute-start(bf16[24,2048]{1,0:T(8,128)(2,1)S(1)} %get-tuple-element.79), channel_id=1, source_target_pairs={{0,4},{4,0},{8,12},{12,8},{1,5},{5,1},{9,13},{13,9},{2,6},{6,2},{1... | collective-permute-start | bytes 294920 | tf_op jit(solution)/shard_map/ppermute | solution.py:505
  29.3 2.5 %collective-permute-start.6 = (bf16[24,2048]{1,0:T(8,128)(2,1)S(1)}, bf16[24,2048]{1,0:T(8,128)(2,1)S(1)}, u32[]{:S(2)}, u32[]{:S(2)}) collective-permute-start(bf16[24,2048]{1,0:T(8,128)(2,1)S(1)} %get-tuple-element.80), channel_id=1, source_target_pairs={{0,12},{4,8},{8,4},{12,0},{1,13},{5,9},{9,5},{13,1},{2,14},{6,10},... | collective-permute-start | bytes 294920 | tf_op jit(solution)/shard_map/ppermute | solution.py:505
  31.9 7.6 %shard_map.114 = (bf16[1920,2048]{1,0:T(8,128)(2,1)S(1)}, bf16[1920,2048]{1,0:T(8,128)(2,1)S(1)}, bf16[1776,2048]{1,0:T(8,128)(2,1)S(1)}, f32[8,128]{1,0:T(8,128)S(1)}) custom-call(bf16[3696,2048]{1,0:T(8,128)(2,1)} %bitcast.11, bf16[3696,2048]{1,0:T(8,128)(2,1)} %bitcast.13, bf16[3696,2048]{1,0:T(8,128)(2,1)} %bitcast.12), custom_call_target="tpu_custom_call" | custom-call | bytes 46006272 | tf_op jit(solution)/shard_map/pallas_call | solution.py:62
  39.5 1.5 %collective-permute-done.7.rest_2_ = bf16[24,2048]{1,0:T(8,128)(2,1)S(1)} collective-permute-done((bf16[24,2048]{1,0:T(8,128)(2,1)S(1)}, bf16[24,2048]{1,0:T(8,128)(2,1)S(1)}, u32[]{:S(2)}, u32[]{:S(2)}) %collective-permute-start.7) | collective-permute-done | bytes 98336 | tf_op jit(solution)/shard_map/ppermute | solution.py:505
  41.1 0.7 shard_map.115.refs_0_
  41.7 1.6 %collective-permute-start.9 = (bf16[24,2048]{1,0:T(8,128)(2,1)S(1)}, bf16[24,2048]{1,0:T(8,128)(2,1)S(1)}, u32[]{:S(2)}, u32[]{:S(2)}) collective-permute-start(bf16[24,2048]{1,0:T(8,128)(2,1)S(1)} %shard_map.115.refs_0_), channel_id=1, source_target_pairs={{0,16},{16,0},{1,17},{17,1},{2,18},{18,2},{3,19},{19,3},{4,20},{20... | collective-permute-start | bytes 294920 | tf_op jit(solution)/shard_map/ppermute | solution.py:509
  43.3 1.3 %collective-permute-start.8 = (bf16[24,2048]{1,0:T(8,128)(2,1)S(1)}, bf16[24,2048]{1,0:T(8,128)(2,1)S(1)}, u32[]{:S(2)}, u32[]{:S(2)}) collective-permute-start(bf16[24,2048]{1,0:T(8,128)(2,1)S(1)} %shard_map.115.refs_0_), channel_id=1, source_target_pairs={{0,8},{4,12},{8,0},{12,4},{1,9},{5,13},{9,1},{13,5},{2,10},{6,14},... | collective-permute-start | bytes 294920 | tf_op jit(solution)/shard_map/ppermute | solution.py:505
  44.6 1.9 %collective-permute-start.10 = (bf16[24,2048]{1,0:T(8,128)(2,1)S(1)}, bf16[24,2048]{1,0:T(8,128)(2,1)S(1)}, u32[]{:S(2)}, u32[]{:S(2)}) collective-permute-start(bf16[24,2048]{1,0:T(8,128)(2,1)S(1)} %shard_map.115.refs_0_), channel_id=1, source_target_pairs={{0,4},{4,0},{8,12},{12,8},{1,5},{5,1},{9,13},{13,9},{2,6},{6,2},{1... | collective-permute-start | bytes 294920 | tf_op jit(solution)/shard_map/ppermute | solution.py:505
  46.5 3.5 %collective-permute-done.8.refs_4_ = bf16[24,2048]{1,0:T(8,128)(2,1)S(1)} collective-permute-done((bf16[24,2048]{1,0:T(8,128)(2,1)S(1)}, bf16[24,2048]{1,0:T(8,128)(2,1)S(1)}, u32[]{:S(2)}, u32[]{:S(2)}) %collective-permute-start.8) | collective-permute-done | bytes 98336 | tf_op jit(solution)/shard_map/ppermute | solution.py:505
  50.8 1.5 %collective-permute-start.11 = (bf16[24,2048]{1,0:T(8,128)(2,1)S(1)}, bf16[24,2048]{1,0:T(8,128)(2,1)S(1)}, u32[]{:S(2)}, u32[]{:S(2)}) collective-permute-start(bf16[24,2048]{1,0:T(8,128)(2,1)S(1)} %collective-permute-done.10.refs_2_), channel_id=1, source_target_pairs={{0,16},{16,0},{1,17},{17,1},{2,18},{18,2},{3,19},{19,3},{4,20},{20... | collective-permute-start | bytes 294920 | tf_op jit(solution)/shard_map/ppermute | solution.py:509
  52.3 2.3 %collective-permute-done.13.refs_6_ = bf16[24,2048]{1,0:T(8,128)(2,1)S(1)} collective-permute-done((bf16[24,2048]{1,0:T(8,128)(2,1)S(1)}, bf16[24,2048]{1,0:T(8,128)(2,1)S(1)}, u32[]{:S(2)}, u32[]{:S(2)}) %collective-permute-start.13) | collective-permute-done | bytes 98336 | tf_op jit(solution)/shard_map/ppermute | solution.py:505
  55.1 3.1 %shard_map.116 = (bf16[1776,2048]{1,0:T(8,128)(2,1)S(1)}, f32[8,128]{1,0:T(8,128)S(1)}) custom-call(bf16[3696,2048]{1,0:T(8,128)(2,1)} %bitcast.14), custom_call_target="tpu_custom_call" | custom-call | bytes 14548992 | tf_op jit(solution)/shard_map/pallas_call | solution.py:62
  58.2 1.0 collective-permute-done.14.refs_7_
  59.2 1.2 shard_map.117
  60.4 4.6 %shard_map.118 = (bf16[2,48,2048]{2,1,0:T(8,128)(2,1)S(1)}, bf16[2,48,2048]{2,1,0:T(8,128)(2,1)S(1)}, bf16[2,48,2048]{2,1,0:T(8,128)(2,1)S(1)}, bf16[2,48,2048]{2,1,0:T(8,128)(2,1)S(1)}) custom-call(bf16[2048,192]{1,0:T(8,128)(2,1)S(1)} %get-tuple-element.99.scaled_ref, bf16[1920,2048]{1,0:T(8,128)(2,1)S(1)} %get-tuple-element.92.gate_ref, ...), custom_call_target="tpu_custom_call" | custom-call | flops 3019898880 | bytes 15728640 | tf_op jit(solution)/shard_map/pallas_call | solution.py:359
  65.1 1.7 %collective-permute-done.16 = bf16[2,48,2048]{2,1,0:T(8,128)(2,1)S(1)} collective-permute-done((bf16[2,48,2048]{2,1,0:T(8,128)(2,1)S(1)}, bf16[2,48,2048]{2,1,0:T(8,128)(2,1)S(1)}, u32[]{:S(2)}, u32[]{:S(2)}) %collective-permute-start.16) | collective-permute-done | bytes 393248 | tf_op jit(solution)/shard_map/ppermute | solution.py:497
  66.9 1.6 %collective-permute-start.18 = (bf16[2,48,2048]{2,1,0:T(8,128)(2,1)S(1)}, bf16[2,48,2048]{2,1,0:T(8,128)(2,1)S(1)}, u32[]{:S(2)}, u32[]{:S(2)}) collective-permute-start(bf16[2,48,2048]{2,1,0:T(8,128)(2,1)S(1)} %add_convert_fusion), channel_id=1, source_target_pairs={{0,2},{1,3},{2,0},{3,1},{4,6},{5,7},{6,4},{7,5},{8,10},{9,11},{10,... | collective-permute-start | bytes 1179656 | tf_op jit(solution)/shard_map/ppermute | solution.py:501
  68.5 4.3 %shard_map.119 = (bf16[2,48,1776]{2,1,0:T(8,128)(2,1)S(1)}, bf16[2,48,1776]{2,1,0:T(8,128)(2,1)S(1)}, bf16[2,48,1776]{2,1,0:T(8,128)(2,1)S(1)}, bf16[2,48,1776]{2,1,0:T(8,128)(2,1)S(1)}) custom-call(bf16[2048,192]{1,0:T(8,128)(2,1)S(1)} %get-tuple-element.99.scaled_ref, bf16[1776,2048]{1,0:T(8,128)(2,1)S(1)} %get-tuple-element.100.gate_ref, ...), custom_call_target="tpu_custom_call" | custom-call | flops 2793406464 | bytes 14548992 | tf_op jit(solution)/shard_map/pallas_call | solution.py:359
  73.4 1.1 collective-permute-done.17
  74.4 3.7 %collective-permute-done.18.crossed_ref = bf16[2,48,2048]{2,1,0:T(8,128)(2,1)S(1)} collective-permute-done((bf16[2,48,2048]{2,1,0:T(8,128)(2,1)S(1)}, bf16[2,48,2048]{2,1,0:T(8,128)(2,1)S(1)}, u32[]{:S(2)}, u32[]{:S(2)}) %collective-permute-start.18) | collective-permute-done | bytes 393248 | tf_op jit(solution)/shard_map/ppermute | solution.py:501
  78.2 1.6 %collective-permute-start.21 = (bf16[2,48,1776]{2,1,0:T(8,128)(2,1)S(1)}, bf16[2,48,1776]{2,1,0:T(8,128)(2,1)S(1)}, u32[]{:S(2)}, u32[]{:S(2)}) collective-permute-start(bf16[2,48,1776]{2,1,0:T(8,128)(2,1)S(1)} %add_convert_fusion.1), channel_id=1, source_target_pairs={{0,2},{1,3},{2,0},{3,1},{4,6},{5,7},{6,4},{7,5},{8,10},{9,11},{10,... | collective-permute-start | bytes 1022984 | tf_op jit(solution)/shard_map/ppermute | solution.py:501
  79.8 5.3 %shard_map.120 = (bf16[1920,2048]{1,0:T(8,128)(2,1)S(1)}, bf16[1776,2048]{1,0:T(8,128)(2,1)S(1)}, f32[8,128]{1,0:T(8,128)S(1)}) custom-call(bf16[3696,2048]{1,0:T(8,128)(2,1)} %refs_1_, bf16[3696,2048]{1,0:T(8,128)(2,1)} %refs_1_), custom_call_target="tpu_custom_call" | custom-call | bytes 30277632 | tf_op jit(solution)/shard_map/pallas_call | solution.py:62
  85.5 0.6 collective-permute-start.19
  86.1 1.8 %collective-permute-done.21.crossed_ref = bf16[2,48,1776]{2,1,0:T(8,128)(2,1)S(1)} collective-permute-done((bf16[2,48,1776]{2,1,0:T(8,128)(2,1)S(1)}, bf16[2,48,1776]{2,1,0:T(8,128)(2,1)S(1)}, u32[]{:S(2)}, u32[]{:S(2)}) %collective-permute-start.21) | collective-permute-done | bytes 341024 | tf_op jit(solution)/shard_map/ppermute | solution.py:501
  88.2 3.3 %collective-permute-done.19.refs_1_ = bf16[48,1920]{1,0:T(8,128)(2,1)S(1)} collective-permute-done((bf16[48,1920]{1,0:T(8,128)(2,1)S(1)}, bf16[48,1920]{1,0:T(8,128)(2,1)S(1)}, u32[]{:S(2)}, u32[]{:S(2)}) %collective-permute-start.19) | collective-permute-done | bytes 184352 | tf_op jit(solution)/shard_map/ppermute | solution.py:501
  91.5 1.5 %collective-permute-start.22 = (bf16[48,1776]{1,0:T(8,128)(2,1)S(1)}, bf16[48,1776]{1,0:T(8,128)(2,1)S(1)}, u32[]{:S(2)}, u32[]{:S(2)}) collective-permute-start(bf16[48,1776]{1,0:T(8,128)(2,1)S(1)} %shard_map.122.refs_0_), channel_id=1, source_target_pairs={{0,2},{1,3},{2,0},{3,1},{4,6},{5,7},{6,4},{7,5},{8,10},{9,11},{10,... | collective-permute-start | bytes 511496 | tf_op jit(solution)/shard_map/ppermute | solution.py:501
  93.2 2.4 %shard_map.123.refs_5_ = f32[4,48,2048]{2,1,0:T(8,128)S(1)} custom-call(s32[6]{0:T(128)S(1)} %stack.27.scalars, bf16[48,1920]{1,0:T(8,128)(2,1)S(1)} %get-tuple-element.110.rest_1_.refs_0_, bf16[48,1920]{1,0:T(8,128)(2,1)S(1)} %collective-permute-done.19.refs_1_, bf16[48,1920]{1,0:T(8,128)(2,1)S(1)} %collective-permute-done.23.refs_2_, ...), custom_call_target="tpu_custom_call" | custom-call | flops 1509949440 | bytes 7864320 | tf_op jit(solution)/shard_map/pallas_call | solution.py:478
  95.6 2.7 %collective-permute-done.22.refs_1_ = bf16[48,1776]{1,0:T(8,128)(2,1)S(1)} collective-permute-done((bf16[48,1776]{1,0:T(8,128)(2,1)S(1)}, bf16[48,1776]{1,0:T(8,128)(2,1)S(1)}, u32[]{:S(2)}, u32[]{:S(2)}) %collective-permute-start.22) | collective-permute-done | bytes 170528 | tf_op jit(solution)/shard_map/ppermute | solution.py:501
  98.3 1.4 %collective-permute-done.26.refs_3_ = bf16[48,1776]{1,0:T(8,128)(2,1)S(1)} collective-permute-done((bf16[48,1776]{1,0:T(8,128)(2,1)S(1)}, bf16[48,1776]{1,0:T(8,128)(2,1)S(1)}, u32[]{:S(2)}, u32[]{:S(2)}) %collective-permute-start.26) | collective-permute-done | bytes 170528 | tf_op jit(solution)/shard_map/ppermute | solution.py:497
  99.7 2.3 %shard_map.124 = (f32[24,2048]{1,0:T(8,128)S(1)}, bf16[24,2048]{1,0:T(8,128)(2,1)S(1)}, f32[24,2048]{1,0:T(8,128)S(1)}, bf16[24,2048]{1,0:T(8,128)(2,1)S(1)}, f3...) custom-call(s32[6]{0:T(128)S(1)} %stack.27.scalars, ...), custom_call_target="tpu_custom_call" | custom-call | flops 1396703232 | bytes 7274496 | tf_op jit(solution)/shard_map/pallas_call | solution.py:478
  102.0 0.6 collective-permute-start.27
  102.6 1.5 %collective-permute-start.29 = (bf16[24,2048]{1,0:T(8,128)(2,1)S(1)}, bf16[24,2048]{1,0:T(8,128)(2,1)S(1)}, u32[]{:S(2)}, u32[]{:S(2)}) collective-permute-start(bf16[24,2048]{1,0:T(8,128)(2,1)S(1)} %get-tuple-element.124), channel_id=1, source_target_pairs={{0,16},{16,0},{1,17},{17,1},{2,18},{18,2},{3,19},{19,3},{4,20},{20... | collective-permute-start | bytes 294920 | tf_op jit(solution)/shard_map/ppermute | solution.py:509
  104.6 1.5 %collective-permute-start.33 = (bf16[24,2048]{1,0:T(8,128)(2,1)S(1)}, bf16[24,2048]{1,0:T(8,128)(2,1)S(1)}, u32[]{:S(2)}, u32[]{:S(2)}) collective-permute-start(bf16[24,2048]{1,0:T(8,128)(2,1)S(1)} %get-tuple-element.128), channel_id=1, source_target_pairs={{0,16},{16,0},{1,17},{17,1},{2,18},{18,2},{3,19},{19,3},{4,20},{20... | collective-permute-start | bytes 294920 | tf_op jit(solution)/shard_map/ppermute | solution.py:509
  106.1 1.6 %collective-permute-done.27 = bf16[24,2048]{1,0:T(8,128)(2,1)S(1)} collective-permute-done((bf16[24,2048]{1,0:T(8,128)(2,1)S(1)}, bf16[24,2048]{1,0:T(8,128)(2,1)S(1)}, u32[]{:S(2)}, u32[]{:S(2)}) %collective-permute-start.27) | collective-permute-done | bytes 98336 | tf_op jit(solution)/shard_map/ppermute | solution.py:509
  107.7 2.3 %collective-permute-start.28 = (bf16[24,2048]{1,0:T(8,128)(2,1)S(1)}, bf16[24,2048]{1,0:T(8,128)(2,1)S(1)}, u32[]{:S(2)}, u32[]{:S(2)}) collective-permute-start(bf16[24,2048]{1,0:T(8,128)(2,1)S(1)} %add_convert_fusion.4), channel_id=1, source_target_pairs={{0,12},{4,8},{8,4},{12,0},{1,13},{5,9},{9,5},{13,1},{2,14},{6,10},... | collective-permute-start | bytes 294920 | tf_op jit(solution)/shard_map/ppermute | solution.py:505
  110.1 0.6 collective-permute-start.30
  110.7 1.2 %collective-permute-done.31 = bf16[24,2048]{1,0:T(8,128)(2,1)S(1)} collective-permute-done((bf16[24,2048]{1,0:T(8,128)(2,1)S(1)}, bf16[24,2048]{1,0:T(8,128)(2,1)S(1)}, u32[]{:S(2)}, u32[]{:S(2)}) %collective-permute-start.31) | collective-permute-done | bytes 98336 | tf_op jit(solution)/shard_map/ppermute | solution.py:509
  111.9 0.9 collective-permute-start.32
  113.2 1.6 %collective-permute-done.28 = bf16[24,2048]{1,0:T(8,128)(2,1)S(1)} collective-permute-done((bf16[24,2048]{1,0:T(8,128)(2,1)S(1)}, bf16[24,2048]{1,0:T(8,128)(2,1)S(1)}, u32[]{:S(2)}, u32[]{:S(2)}) %collective-permute-start.28) | collective-permute-done | bytes 98336 | tf_op jit(solution)/shard_map/ppermute | solution.py:505
  114.8 3.3 %collective-permute-done.30 = bf16[24,2048]{1,0:T(8,128)(2,1)S(1)} collective-permute-done((bf16[24,2048]{1,0:T(8,128)(2,1)S(1)}, bf16[24,2048]{1,0:T(8,128)(2,1)S(1)}, u32[]{:S(2)}, u32[]{:S(2)}) %collective-permute-start.30) | collective-permute-done | bytes 98336 | tf_op jit(solution)/shard_map/ppermute | solution.py:505
  118.2 0.7 select_convert_fusion
  (49 shorter events, 6.0 us)
Async XLA Ops:
  12.7 1.7 %collective-permute-start = (bf16[96,1024]{1,0:T(8,128)(2,1)S(1)}, bf16[96,1024]{1,0:T(8,128)(2,1)S(1)}, u32[]{:S(2)}, u32[]{:S(2)}) collective-permute-start(bf16[96,1024]{1,0:T(8,128)(2,1)S(1)} %get-tuple-element.68), channel_id=1, source_target_pairs={{0,1},{1,0},{2,3},{3,2},{4,5},{5,4},{6,7},{7,6},{8,9},{9,8},{10,11... | collective-permute-start | bytes 589832 | tf_op jit(solution)/shard_map/ppermute | solution.py:497
  13.2 1.2 collective-permute-start.1
  14.8 8.2 %collective-permute-start.2 = (bf16[96,1024]{1,0:T(8,128)(2,1)S(1)}, bf16[96,1024]{1,0:T(8,128)(2,1)S(1)}, u32[]{:S(2)}, u32[]{:S(2)}) collective-permute-start(bf16[96,1024]{1,0:T(8,128)(2,1)S(1)} %get-tuple-element.72.a_ref), channel_id=1, source_target_pairs={{0,2},{1,3},{2,0},{3,1},{4,6},{5,7},{6,4},{7,5},{8,10},{9,11},{10,... | collective-permute-start | bytes 589832 | tf_op jit(solution)/shard_map/ppermute | solution.py:501
  17.6 5.4 %collective-permute-start.3 = (f32[8,128]{1,0:T(8,128)S(1)}, f32[8,128]{1,0:T(8,128)S(1)}, u32[]{:S(2)}, u32[]{:S(2)}) collective-permute-start(f32[8,128]{1,0:T(8,128)S(1)} %get-tuple-element.73.lse_a_ref), channel_id=1, source_target_pairs={{0,2},{1,3},{2,0},{3,1},{4,6},{5,7},{6,4},{7,5},{8,10},{9,11},{10,... | collective-permute-start | bytes 12296 | tf_op jit(solution)/shard_map/ppermute | solution.py:501
  23.4 1.5 %collective-permute-start.4 = (bf16[96,1024]{1,0:T(8,128)(2,1)S(1)}, bf16[96,1024]{1,0:T(8,128)(2,1)S(1)}, u32[]{:S(2)}, u32[]{:S(2)}) collective-permute-start(bf16[96,1024]{1,0:T(8,128)(2,1)S(1)} %shard_map.112.keep_ref), channel_id=1, source_target_pairs={{0,1},{1,0},{2,3},{3,2},{4,5},{5,4},{6,7},{7,6},{8,9},{9,8},{10,11... | collective-permute-start | bytes 589832 | tf_op jit(solution)/shard_map/ppermute | solution.py:497
  27.4 12.1 %collective-permute-start.5 = (bf16[24,2048]{1,0:T(8,128)(2,1)S(1)}, bf16[24,2048]{1,0:T(8,128)(2,1)S(1)}, u32[]{:S(2)}, u32[]{:S(2)}) collective-permute-start(bf16[24,2048]{1,0:T(8,128)(2,1)S(1)} %get-tuple-element.79), channel_id=1, source_target_pairs={{0,4},{4,0},{8,12},{12,8},{1,5},{5,1},{9,13},{13,9},{2,6},{6,2},{1... | collective-permute-start | bytes 294920 | tf_op jit(solution)/shard_map/ppermute | solution.py:505
  29.3 10.2 %collective-permute-start.6 = (bf16[24,2048]{1,0:T(8,128)(2,1)S(1)}, bf16[24,2048]{1,0:T(8,128)(2,1)S(1)}, u32[]{:S(2)}, u32[]{:S(2)}) collective-permute-start(bf16[24,2048]{1,0:T(8,128)(2,1)S(1)} %get-tuple-element.80), channel_id=1, source_target_pairs={{0,12},{4,8},{8,4},{12,0},{1,13},{5,9},{9,5},{13,1},{2,14},{6,10},... | collective-permute-start | bytes 294920 | tf_op jit(solution)/shard_map/ppermute | solution.py:505
  31.8 9.2 %copy-start = (bf16[96,2048]{1,0:T(8,128)(2,1)S(1)}, bf16[96,2048]{1,0:T(8,128)(2,1)}, u32[]{:S(2)}) copy-start(bf16[96,2048]{1,0:T(8,128)(2,1)} %resid_ref.1) | copy-start | bytes 1179652
  31.8 23.3 %copy-start.1 = (bf16[2048]{0:T(1024)(128)(2,1)S(1)}, bf16[2048]{0:T(1024)(128)(2,1)}, u32[]{:S(2)}) copy-start(bf16[2048]{0:T(1024)(128)(2,1)} %param.18) | copy-start | bytes 12292
  31.8 9.2 %collective-permute-start.7 = (bf16[24,2048]{1,0:T(8,128)(2,1)S(1)}, bf16[24,2048]{1,0:T(8,128)(2,1)S(1)}, u32[]{:S(2)}, u32[]{:S(2)}) collective-permute-start(bf16[24,2048]{1,0:T(8,128)(2,1)S(1)} %get-tuple-element.81), channel_id=1, source_target_pairs={{0,8},{4,12},{8,0},{12,4},{1,9},{5,13},{9,1},{13,5},{2,10},{6,14},... | collective-permute-start | bytes 294920 | tf_op jit(solution)/shard_map/ppermute | solution.py:505
  41.7 4.8 %collective-permute-start.9 = (bf16[24,2048]{1,0:T(8,128)(2,1)S(1)}, bf16[24,2048]{1,0:T(8,128)(2,1)S(1)}, u32[]{:S(2)}, u32[]{:S(2)}) collective-permute-start(bf16[24,2048]{1,0:T(8,128)(2,1)S(1)} %shard_map.115.refs_0_), channel_id=1, source_target_pairs={{0,16},{16,0},{1,17},{17,1},{2,18},{18,2},{3,19},{19,3},{4,20},{20... | collective-permute-start | bytes 294920 | tf_op jit(solution)/shard_map/ppermute | solution.py:509
  43.3 6.7 %collective-permute-start.8 = (bf16[24,2048]{1,0:T(8,128)(2,1)S(1)}, bf16[24,2048]{1,0:T(8,128)(2,1)S(1)}, u32[]{:S(2)}, u32[]{:S(2)}) collective-permute-start(bf16[24,2048]{1,0:T(8,128)(2,1)S(1)} %shard_map.115.refs_0_), channel_id=1, source_target_pairs={{0,8},{4,12},{8,0},{12,4},{1,9},{5,13},{9,1},{13,5},{2,10},{6,14},... | collective-permute-start | bytes 294920 | tf_op jit(solution)/shard_map/ppermute | solution.py:505
  44.6 6.2 %collective-permute-start.10 = (bf16[24,2048]{1,0:T(8,128)(2,1)S(1)}, bf16[24,2048]{1,0:T(8,128)(2,1)S(1)}, u32[]{:S(2)}, u32[]{:S(2)}) collective-permute-start(bf16[24,2048]{1,0:T(8,128)(2,1)S(1)} %shard_map.115.refs_0_), channel_id=1, source_target_pairs={{0,4},{4,0},{8,12},{12,8},{1,5},{5,1},{9,13},{13,9},{2,6},{6,2},{1... | collective-permute-start | bytes 294920 | tf_op jit(solution)/shard_map/ppermute | solution.py:505
  50.0 4.6 %collective-permute-start.13 = (bf16[24,2048]{1,0:T(8,128)(2,1)S(1)}, bf16[24,2048]{1,0:T(8,128)(2,1)S(1)}, u32[]{:S(2)}, u32[]{:S(2)}) collective-permute-start(bf16[24,2048]{1,0:T(8,128)(2,1)S(1)} %collective-permute-done.8.refs_4_), channel_id=1, source_target_pairs={{0,4},{4,0},{8,12},{12,8},{1,5},{5,1},{9,13},{13,9},{2,6},{6,2},{1... | collective-permute-start | bytes 294920 | tf_op jit(solution)/shard_map/ppermute | solution.py:505
  50.3 8.0 %collective-permute-start.12 = (bf16[24,2048]{1,0:T(8,128)(2,1)S(1)}, bf16[24,2048]{1,0:T(8,128)(2,1)S(1)}, u32[]{:S(2)}, u32[]{:S(2)}) collective-permute-start(bf16[24,2048]{1,0:T(8,128)(2,1)S(1)} %collective-permute-done.8.refs_4_), channel_id=1, source_target_pairs={{0,16},{16,0},{1,17},{17,1},{2,18},{18,2},{3,19},{19,3},{4,20},{20... | collective-permute-start | bytes 294920 | tf_op jit(solution)/shard_map/ppermute | solution.py:509
  50.8 7.4 %collective-permute-start.11 = (bf16[24,2048]{1,0:T(8,128)(2,1)S(1)}, bf16[24,2048]{1,0:T(8,128)(2,1)S(1)}, u32[]{:S(2)}, u32[]{:S(2)}) collective-permute-start(bf16[24,2048]{1,0:T(8,128)(2,1)S(1)} %collective-permute-done.10.refs_2_), channel_id=1, source_target_pairs={{0,16},{16,0},{1,17},{17,1},{2,18},{18,2},{3,19},{19,3},{4,20},{20... | collective-permute-start | bytes 294920 | tf_op jit(solution)/shard_map/ppermute | solution.py:509
  54.6 4.6 %collective-permute-start.14 = (bf16[24,2048]{1,0:T(8,128)(2,1)S(1)}, bf16[24,2048]{1,0:T(8,128)(2,1)S(1)}, u32[]{:S(2)}, u32[]{:S(2)}) collective-permute-start(bf16[24,2048]{1,0:T(8,128)(2,1)S(1)} %collective-permute-done.13.refs_6_), channel_id=1, source_target_pairs={{0,16},{16,0},{1,17},{17,1},{2,18},{18,2},{3,19},{19,3},{4,20},{20... | collective-permute-start | bytes 294920 | tf_op jit(solution)/shard_map/ppermute | solution.py:509
  65.0 1.8 %collective-permute-start.16 = (bf16[2,48,2048]{2,1,0:T(8,128)(2,1)S(1)}, bf16[2,48,2048]{2,1,0:T(8,128)(2,1)S(1)}, u32[]{:S(2)}, u32[]{:S(2)}) collective-permute-start(bf16[2,48,2048]{2,1,0:T(8,128)(2,1)S(1)} %get-tuple-element.98), channel_id=1, source_target_pairs={{0,1},{1,0},{2,3},{3,2},{4,5},{5,4},{6,7},{7,6},{8,9},{9,8},{10,11... | collective-permute-start | bytes 1179656 | tf_op jit(solution)/shard_map/ppermute | solution.py:497
  66.9 11.2 %collective-permute-start.18 = (bf16[2,48,2048]{2,1,0:T(8,128)(2,1)S(1)}, bf16[2,48,2048]{2,1,0:T(8,128)(2,1)S(1)}, u32[]{:S(2)}, u32[]{:S(2)}) collective-permute-start(bf16[2,48,2048]{2,1,0:T(8,128)(2,1)S(1)} %add_convert_fusion), channel_id=1, source_target_pairs={{0,2},{1,3},{2,0},{3,1},{4,6},{5,7},{6,4},{7,5},{8,10},{9,11},{10,... | collective-permute-start | bytes 1179656 | tf_op jit(solution)/shard_map/ppermute | solution.py:501
  72.7 1.7 %collective-permute-start.17 = (bf16[2,48,1776]{2,1,0:T(8,128)(2,1)S(1)}, bf16[2,48,1776]{2,1,0:T(8,128)(2,1)S(1)}, u32[]{:S(2)}, u32[]{:S(2)}) collective-permute-start(bf16[2,48,1776]{2,1,0:T(8,128)(2,1)S(1)} %get-tuple-element.102), channel_id=1, source_target_pairs={{0,1},{1,0},{2,3},{3,2},{4,5},{5,4},{6,7},{7,6},{8,9},{9,8},{10,11... | collective-permute-start | bytes 1022984 | tf_op jit(solution)/shard_map/ppermute | solution.py:497
  72.8 12.3 %collective-permute-start.15 = (bf16[2,48,2048]{2,1,0:T(8,128)(2,1)S(1)}, bf16[2,48,2048]{2,1,0:T(8,128)(2,1)S(1)}, u32[]{:S(2)}, u32[]{:S(2)}) collective-permute-start(bf16[2,48,2048]{2,1,0:T(8,128)(2,1)S(1)} %get-tuple-element.96), channel_id=1, source_target_pairs={{0,1},{1,0},{2,3},{3,2},{4,5},{5,4},{6,7},{7,6},{8,9},{9,8},{10,11... | collective-permute-start | bytes 1179656 | tf_op jit(solution)/shard_map/ppermute | solution.py:497
  73.3 12.8 %collective-permute-start.20 = (bf16[2,48,1776]{2,1,0:T(8,128)(2,1)S(1)}, bf16[2,48,1776]{2,1,0:T(8,128)(2,1)S(1)}, u32[]{:S(2)}, u32[]{:S(2)}) collective-permute-start(bf16[2,48,1776]{2,1,0:T(8,128)(2,1)S(1)} %get-tuple-element.112), channel_id=1, source_target_pairs={{0,1},{1,0},{2,3},{3,2},{4,5},{5,4},{6,7},{7,6},{8,9},{9,8},{10,11... | collective-permute-start | bytes 1022984 | tf_op jit(solution)/shard_map/ppermute | solution.py:497
  78.2 9.7 %collective-permute-start.21 = (bf16[2,48,1776]{2,1,0:T(8,128)(2,1)S(1)}, bf16[2,48,1776]{2,1,0:T(8,128)(2,1)S(1)}, u32[]{:S(2)}, u32[]{:S(2)}) collective-permute-start(bf16[2,48,1776]{2,1,0:T(8,128)(2,1)S(1)} %add_convert_fusion.1), channel_id=1, source_target_pairs={{0,2},{1,3},{2,0},{3,1},{4,6},{5,7},{6,4},{7,5},{8,10},{9,11},{10,... | collective-permute-start | bytes 1022984 | tf_op jit(solution)/shard_map/ppermute | solution.py:501
  85.5 6.0 %collective-permute-start.19 = (bf16[48,1920]{1,0:T(8,128)(2,1)S(1)}, bf16[48,1920]{1,0:T(8,128)(2,1)S(1)}, u32[]{:S(2)}, u32[]{:S(2)}) collective-permute-start(bf16[48,1920]{1,0:T(8,128)(2,1)S(1)} %get-tuple-element.110.rest_1_.refs_0_), channel_id=1, source_target_pairs={{0,2},{1,3},{2,0},{3,1},{4,6},{5,7},{6,4},{7,5},{8,10},{9,11},{10,... | collective-permute-start | bytes 552968 | tf_op jit(solution)/shard_map/ppermute | solution.py:501
  86.1 7.2 %collective-permute-start.23 = (bf16[48,1920]{1,0:T(8,128)(2,1)S(1)}, bf16[48,1920]{1,0:T(8,128)(2,1)S(1)}, u32[]{:S(2)}, u32[]{:S(2)}) collective-permute-start(bf16[48,1920]{1,0:T(8,128)(2,1)S(1)} %get-tuple-element.110.rest_1_.refs_0_), channel_id=1, source_target_pairs={{0,1},{1,0},{2,3},{3,2},{4,5},{5,4},{6,7},{7,6},{8,9},{9,8},{10,11... | collective-permute-start | bytes 552968 | tf_op jit(solution)/shard_map/ppermute | solution.py:497
  91.5 1.7 %collective-permute-start.24 = (bf16[48,1920]{1,0:T(8,128)(2,1)S(1)}, bf16[48,1920]{1,0:T(8,128)(2,1)S(1)}, u32[]{:S(2)}, u32[]{:S(2)}) collective-permute-start(bf16[48,1920]{1,0:T(8,128)(2,1)S(1)} %collective-permute-done.19.refs_1_), channel_id=1, source_target_pairs={{0,1},{1,0},{2,3},{3,2},{4,5},{5,4},{6,7},{7,6},{8,9},{9,8},{10,11... | collective-permute-start | bytes 552968 | tf_op jit(solution)/shard_map/ppermute | solution.py:497
  91.5 6.8 %collective-permute-start.22 = (bf16[48,1776]{1,0:T(8,128)(2,1)S(1)}, bf16[48,1776]{1,0:T(8,128)(2,1)S(1)}, u32[]{:S(2)}, u32[]{:S(2)}) collective-permute-start(bf16[48,1776]{1,0:T(8,128)(2,1)S(1)} %shard_map.122.refs_0_), channel_id=1, source_target_pairs={{0,2},{1,3},{2,0},{3,1},{4,6},{5,7},{6,4},{7,5},{8,10},{9,11},{10,... | collective-permute-start | bytes 511496 | tf_op jit(solution)/shard_map/ppermute | solution.py:501
  93.0 5.3 %collective-permute-start.25 = (bf16[48,1776]{1,0:T(8,128)(2,1)S(1)}, bf16[48,1776]{1,0:T(8,128)(2,1)S(1)}, u32[]{:S(2)}, u32[]{:S(2)}) collective-permute-start(bf16[48,1776]{1,0:T(8,128)(2,1)S(1)} %shard_map.122.refs_0_), channel_id=1, source_target_pairs={{0,1},{1,0},{2,3},{3,2},{4,5},{5,4},{6,7},{7,6},{8,9},{9,8},{10,11... | collective-permute-start | bytes 511496 | tf_op jit(solution)/shard_map/ppermute | solution.py:497
  98.3 1.4 %collective-permute-start.26 = (bf16[48,1776]{1,0:T(8,128)(2,1)S(1)}, bf16[48,1776]{1,0:T(8,128)(2,1)S(1)}, u32[]{:S(2)}, u32[]{:S(2)}) collective-permute-start(bf16[48,1776]{1,0:T(8,128)(2,1)S(1)} %collective-permute-done.22.refs_1_), channel_id=1, source_target_pairs={{0,1},{1,0},{2,3},{3,2},{4,5},{5,4},{6,7},{7,6},{8,9},{9,8},{10,11... | collective-permute-start | bytes 511496 | tf_op jit(solution)/shard_map/ppermute | solution.py:497
  102.0 5.7 %collective-permute-start.27 = (bf16[24,2048]{1,0:T(8,128)(2,1)S(1)}, bf16[24,2048]{1,0:T(8,128)(2,1)S(1)}, u32[]{:S(2)}, u32[]{:S(2)}) collective-permute-start(bf16[24,2048]{1,0:T(8,128)(2,1)S(1)} %get-tuple-element.122), channel_id=1, source_target_pairs={{0,16},{16,0},{1,17},{17,1},{2,18},{18,2},{3,19},{19,3},{4,20},{20... | collective-permute-start | bytes 294920 | tf_op jit(solution)/shard_map/ppermute | solution.py:509
  102.6 7.5 %collective-permute-start.29 = (bf16[24,2048]{1,0:T(8,128)(2,1)S(1)}, bf16[24,2048]{1,0:T(8,128)(2,1)S(1)}, u32[]{:S(2)}, u32[]{:S(2)}) collective-permute-start(bf16[24,2048]{1,0:T(8,128)(2,1)S(1)} %get-tuple-element.124), channel_id=1, source_target_pairs={{0,16},{16,0},{1,17},{17,1},{2,18},{18,2},{3,19},{19,3},{4,20},{20... | collective-permute-start | bytes 294920 | tf_op jit(solution)/shard_map/ppermute | solution.py:509
  104.1 7.8 %collective-permute-start.31 = (bf16[24,2048]{1,0:T(8,128)(2,1)S(1)}, bf16[24,2048]{1,0:T(8,128)(2,1)S(1)}, u32[]{:S(2)}, u32[]{:S(2)}) collective-permute-start(bf16[24,2048]{1,0:T(8,128)(2,1)S(1)} %get-tuple-element.126), channel_id=1, source_target_pairs={{0,16},{16,0},{1,17},{17,1},{2,18},{18,2},{3,19},{19,3},{4,20},{20... | collective-permute-start | bytes 294920 | tf_op jit(solution)/shard_map/ppermute | solution.py:509
  104.6 8.6 %collective-permute-start.33 = (bf16[24,2048]{1,0:T(8,128)(2,1)S(1)}, bf16[24,2048]{1,0:T(8,128)(2,1)S(1)}, u32[]{:S(2)}, u32[]{:S(2)}) collective-permute-start(bf16[24,2048]{1,0:T(8,128)(2,1)S(1)} %get-tuple-element.128), channel_id=1, source_target_pairs={{0,16},{16,0},{1,17},{17,1},{2,18},{18,2},{3,19},{19,3},{4,20},{20... | collective-permute-start | bytes 294920 | tf_op jit(solution)/shard_map/ppermute | solution.py:509
  107.7 7.1 %collective-permute-start.28 = (bf16[24,2048]{1,0:T(8,128)(2,1)S(1)}, bf16[24,2048]{1,0:T(8,128)(2,1)S(1)}, u32[]{:S(2)}, u32[]{:S(2)}) collective-permute-start(bf16[24,2048]{1,0:T(8,128)(2,1)S(1)} %add_convert_fusion.4), channel_id=1, source_target_pairs={{0,12},{4,8},{8,4},{12,0},{1,13},{5,9},{9,5},{13,1},{2,14},{6,10},... | collective-permute-start | bytes 294920 | tf_op jit(solution)/shard_map/ppermute | solution.py:505
  110.1 8.1 %collective-permute-start.30 = (bf16[24,2048]{1,0:T(8,128)(2,1)S(1)}, bf16[24,2048]{1,0:T(8,128)(2,1)S(1)}, u32[]{:S(2)}, u32[]{:S(2)}) collective-permute-start(bf16[24,2048]{1,0:T(8,128)(2,1)S(1)} %add_convert_fusion.3), channel_id=1, source_target_pairs={{0,8},{4,12},{8,0},{12,4},{1,9},{5,13},{9,1},{13,5},{2,10},{6,14},... | collective-permute-start | bytes 294920 | tf_op jit(solution)/shard_map/ppermute | solution.py:505
  111.9 6.3 %collective-permute-start.32 = (bf16[24,2048]{1,0:T(8,128)(2,1)S(1)}, bf16[24,2048]{1,0:T(8,128)(2,1)S(1)}, u32[]{:S(2)}, u32[]{:S(2)}) collective-permute-start(bf16[24,2048]{1,0:T(8,128)(2,1)S(1)} %add_convert_fusion.2), channel_id=1, source_target_pairs={{0,4},{4,0},{8,12},{12,8},{1,5},{5,1},{9,13},{13,9},{2,6},{6,2},{1... | collective-permute-start | bytes 294920 | tf_op jit(solution)/shard_map/ppermute | solution.py:505

commit v6 on v5

--- a/solution.py
+++ b/solution.py
@@ -9,8 +9,7 @@
 from jax.sharding import PartitionSpec as P
 
 DH = 128
-TILE = 1920
-CHUNKS = (1, 1)
+SPLIT = 1792
 HEADS = 4
 THIN = 1
 NEGATIVE = -1e30
@@ -459,8 +458,7 @@
 def down(scalars, hidden, down_weight, start, slots, last):
     high, width = hidden[0].shape
     cols = down_weight.shape[1]
-    tile = min(TILE, width)
-    steps = pl.cdiv(width, tile)
+    tile, steps = width, 1
     rows = high // slots
     ins = [whole((high, width))] * 4 + [pl.BlockSpec((tile, cols), lambda i, s: (i, 0))]
     args = list(hidden) + [down_weight]
@@ -510,10 +508,7 @@
 
 
 def cut(total):
-    edges = [0]
-    for tiles in CHUNKS:
-        edges.append(min(edges[-1] + tiles * TILE, total))
-    return [(low, high - low) for low, high in zip(edges, edges[1:])]
+    return [(0, SPLIT), (SPLIT, total - SPLIT)]
 
 
 def body(
@@ -612,7 +607,7 @@
             moved = lax.all_to_all(stacked, "grp", split_axis=0, concat_axis=0, tiled=True)
             chunk_sums.append(jnp.sum(moved.astype(F32), axis=0))
     parts = [h1]
-    for k in (3, 2, 1, 0):
+    for k in (2, 3, 1, 0):
         if groups == 2:
             own, away = chunk_sums[k]
             away = to_y(away)

time: 119 us -> 119 us (level)
  transfers between devices with their start and end apart: 34 -> 34, of which waited for: 20 -> 19; matrix products, arithmetic and copies ran while one was open for 0% -> 0% of each run, Pallas kernels for 22% -> 22%
where the time goes in v6:
time: 119 us
  Pallas kernels  50 us (42%)
  waiting for transfers between devices  37 us (31%)
  starting transfers between devices  29.3 us (25%)
  between operations  1.51 us (1%)
    pallas_call x4, Pallas kernels, fetch(): pl.pallas_call(functools.partial(fetch_kernel, pieces), in_specs=[pl.Bloc...  19.4 us
    ppermute x6, waiting for transfers between devices, to_x(): return lax.ppermute(x, 'ffn', [(i, i ^ 2) for i in range(4)])  13.3 us
    ppermute x9, waiting for transfers between devices, to_z(): return lax.ppermute(x, 'tp', [(i, i ^ k) for i in range(4)])  12.5 us
    ppermute x9, starting transfers between devices, to_z(): return lax.ppermute(x, 'tp', [(i, i ^ k) for i in range(4)])  11.3 us
    pallas_call x1, Pallas kernels, attention(): return call(scalars, queries, kv_cache, kv_cache, new_kv, new_kv)  11.3 us
    pallas_call x2, Pallas kernels, gate_up(): pl.pallas_call(gate_up_kernel, out_shape=[jax.ShapeDtypeStruct((2, high,...  8.91 us
    ppermute x8, starting transfers between devices, to_y(): return lax.ppermute(x, 'grp', [(0, 1), (1, 0)])  8.23 us
    ppermute x6, starting transfers between devices, to_x(): return lax.ppermute(x, 'ffn', [(i, i ^ 2) for i in range(4)])  8.1 us
  transfers between devices with their start and end apart: 34, of which 19 were waited for; matrix products, arithmetic and copies ran while one was open for 0% of the time, Pallas kernels for 22%

profile of v6, /device:TPU:0, one launch (start us, length us, event | category | flops | bytes accessed | tf_op | source)
XLA Modules:
  0.0 118.9 jit_solution(14126990149203355854)
XLA Ops:
  1.4 11.3 %shard_map.109 = (bf16[96,1024]{1,0:T(8,128)(2,1)S(1)}, bf16[96,1024]{1,0:T(8,128)(2,1)S(1)}, f32[8,128]{1,0:T(8,128)S(1)}, f32[8,128]{1,0:T(8,128)S(1)}) custom-call(s32[6]{0:T(128)S(1)} %stack.27.scalars, bf16[96,2048]{1,0:T(8,128)(2,1)} %q_ref.1, bf16[2,1,2048,256]{3,2,1,0:T(8,128)(2,1)} %value_ref.1, bf16[2,1,2048,256]{3,2,1,0:T(8,128)(2,1)} %value_ref.1, ...), custom_call_target="tpu_custom_call" | custom-call | flops 1610612736 | bytes 2097152 | tf_op jit(solution)/shard_map/pallas_call | solution.py:166
  13.3 1.1 collective-permute-done.1.lse_b_ref
  14.8 2.8 %collective-permute-start.2 = (bf16[96,1024]{1,0:T(8,128)(2,1)S(1)}, bf16[96,1024]{1,0:T(8,128)(2,1)S(1)}, u32[]{:S(2)}, u32[]{:S(2)}) collective-permute-start(bf16[96,1024]{1,0:T(8,128)(2,1)S(1)} %get-tuple-element.72.a_ref), channel_id=1, source_target_pairs={{0,2},{1,3},{2,0},{3,1},{4,6},{5,7},{6,4},{7,5},{8,10},{9,11},{10,... | collective-permute-start | bytes 589832 | tf_op jit(solution)/shard_map/ppermute | solution.py:499
  17.7 3.4 %shard_map.111 = (bf16[2048,2048]{1,0:T(8,128)(2,1)S(1)}, f32[8,128]{1,0:T(8,128)S(1)}) custom-call(bf16[2048,2048]{1,0:T(8,128)(2,1)} %refs_0_), custom_call_target="tpu_custom_call" | custom-call | bytes 16777216 | tf_op jit(solution)/shard_map/pallas_call | solution.py:61
  21.1 1.9 %collective-permute-done.3.lse_b_ref = f32[8,128]{1,0:T(8,128)S(1)} collective-permute-done((f32[8,128]{1,0:T(8,128)S(1)}, f32[8,128]{1,0:T(8,128)S(1)}, u32[]{:S(2)}, u32[]{:S(2)}) %collective-permute-start.3) | collective-permute-done | bytes 4128 | tf_op jit(solution)/shard_map/ppermute | solution.py:499
  23.5 1.4 %collective-permute-done.4.other_ref = bf16[96,1024]{1,0:T(8,128)(2,1)S(1)} collective-permute-done((bf16[96,1024]{1,0:T(8,128)(2,1)S(1)}, bf16[96,1024]{1,0:T(8,128)(2,1)S(1)}, u32[]{:S(2)}, u32[]{:S(2)}) %collective-permute-start.4) | collective-permute-done | bytes 196640 | tf_op jit(solution)/shard_map/ppermute | solution.py:495
  25.0 2.5 %shard_map.113 = (f32[24,2048]{1,0:T(8,128)S(1)}, bf16[24,2048]{1,0:T(8,128)(2,1)S(1)}, bf16[24,2048]{1,0:T(8,128)(2,1)S(1)}, bf16[24,2048]{1,0:T(8,128)(2,1)S(1)}) custom-call(s32[6]{0:T(128)S(1)} %stack.27.scalars, bf16[96,1024]{1,0:T(8,128)(2,1)S(1)} %shard_map.112.keep_ref, bf16[96,1024]{1,0:T(8,128)(2,1)S(1)} %collective-permute-done.4.other_ref, ...), custom_call_target="tpu_custom_call" | custom-call | flops 805306368 | bytes 8388608 | tf_op jit(solution)/shard_map/pallas_call | solution.py:240
  27.4 1.9 %collective-permute-start.5 = (bf16[24,2048]{1,0:T(8,128)(2,1)S(1)}, bf16[24,2048]{1,0:T(8,128)(2,1)S(1)}, u32[]{:S(2)}, u32[]{:S(2)}) collective-permute-start(bf16[24,2048]{1,0:T(8,128)(2,1)S(1)} %get-tuple-element.79), channel_id=1, source_target_pairs={{0,4},{4,0},{8,12},{12,8},{1,5},{5,1},{9,13},{13,9},{2,6},{6,2},{1... | collective-permute-start | bytes 294920 | tf_op jit(solution)/shard_map/ppermute | solution.py:503
  29.3 2.5 %collective-permute-start.6 = (bf16[24,2048]{1,0:T(8,128)(2,1)S(1)}, bf16[24,2048]{1,0:T(8,128)(2,1)S(1)}, u32[]{:S(2)}, u32[]{:S(2)}) collective-permute-start(bf16[24,2048]{1,0:T(8,128)(2,1)S(1)} %get-tuple-element.80), channel_id=1, source_target_pairs={{0,12},{4,8},{8,4},{12,0},{1,13},{5,9},{9,5},{13,1},{2,14},{6,10},... | collective-permute-start | bytes 294920 | tf_op jit(solution)/shard_map/ppermute | solution.py:503
  31.9 7.4 %shard_map.114 = (bf16[1792,2048]{1,0:T(8,128)(2,1)S(1)}, bf16[1792,2048]{1,0:T(8,128)(2,1)S(1)}, bf16[1904,2048]{1,0:T(8,128)(2,1)S(1)}, f32[8,128]{1,0:T(8,128)S(1)}) custom-call(bf16[3696,2048]{1,0:T(8,128)(2,1)} %bitcast.11, bf16[3696,2048]{1,0:T(8,128)(2,1)} %bitcast.13, bf16[3696,2048]{1,0:T(8,128)(2,1)} %bitcast.12), custom_call_target="tpu_custom_call" | custom-call | bytes 44957696 | tf_op jit(solution)/shard_map/pallas_call | solution.py:61
  39.4 1.7 %collective-permute-done.7.rest_2_ = bf16[24,2048]{1,0:T(8,128)(2,1)S(1)} collective-permute-done((bf16[24,2048]{1,0:T(8,128)(2,1)S(1)}, bf16[24,2048]{1,0:T(8,128)(2,1)S(1)}, u32[]{:S(2)}, u32[]{:S(2)}) %collective-permute-start.7) | collective-permute-done | bytes 98336 | tf_op jit(solution)/shard_map/ppermute | solution.py:503
  41.1 0.7 shard_map.115.refs_0_
  41.7 1.6 %collective-permute-start.9 = (bf16[24,2048]{1,0:T(8,128)(2,1)S(1)}, bf16[24,2048]{1,0:T(8,128)(2,1)S(1)}, u32[]{:S(2)}, u32[]{:S(2)}) collective-permute-start(bf16[24,2048]{1,0:T(8,128)(2,1)S(1)} %shard_map.115.refs_0_), channel_id=1, source_target_pairs={{0,16},{16,0},{1,17},{17,1},{2,18},{18,2},{3,19},{19,3},{4,20},{20... | collective-permute-start | bytes 294920 | tf_op jit(solution)/shard_map/ppermute | solution.py:507
  43.3 1.2 collective-permute-start.8
  44.5 2.1 %collective-permute-start.10 = (bf16[24,2048]{1,0:T(8,128)(2,1)S(1)}, bf16[24,2048]{1,0:T(8,128)(2,1)S(1)}, u32[]{:S(2)}, u32[]{:S(2)}) collective-permute-start(bf16[24,2048]{1,0:T(8,128)(2,1)S(1)} %shard_map.115.refs_0_), channel_id=1, source_target_pairs={{0,4},{4,0},{8,12},{12,8},{1,5},{5,1},{9,13},{13,9},{2,6},{6,2},{1... | collective-permute-start | bytes 294920 | tf_op jit(solution)/shard_map/ppermute | solution.py:503
  46.5 3.5 %collective-permute-done.8.refs_4_ = bf16[24,2048]{1,0:T(8,128)(2,1)S(1)} collective-permute-done((bf16[24,2048]{1,0:T(8,128)(2,1)S(1)}, bf16[24,2048]{1,0:T(8,128)(2,1)S(1)}, u32[]{:S(2)}, u32[]{:S(2)}) %collective-permute-start.8) | collective-permute-done | bytes 98336 | tf_op jit(solution)/shard_map/ppermute | solution.py:503
  50.8 1.5 %collective-permute-start.11 = (bf16[24,2048]{1,0:T(8,128)(2,1)S(1)}, bf16[24,2048]{1,0:T(8,128)(2,1)S(1)}, u32[]{:S(2)}, u32[]{:S(2)}) collective-permute-start(bf16[24,2048]{1,0:T(8,128)(2,1)S(1)} %collective-permute-done.10.refs_2_), channel_id=1, source_target_pairs={{0,16},{16,0},{1,17},{17,1},{2,18},{18,2},{3,19},{19,3},{4,20},{20... | collective-permute-start | bytes 294920 | tf_op jit(solution)/shard_map/ppermute | solution.py:507
  52.3 2.3 %collective-permute-done.13.refs_6_ = bf16[24,2048]{1,0:T(8,128)(2,1)S(1)} collective-permute-done((bf16[24,2048]{1,0:T(8,128)(2,1)S(1)}, bf16[24,2048]{1,0:T(8,128)(2,1)S(1)}, u32[]{:S(2)}, u32[]{:S(2)}) %collective-permute-start.13) | collective-permute-done | bytes 98336 | tf_op jit(solution)/shard_map/ppermute | solution.py:503
  55.1 3.2 %shard_map.116 = (bf16[1904,2048]{1,0:T(8,128)(2,1)S(1)}, f32[8,128]{1,0:T(8,128)S(1)}) custom-call(bf16[3696,2048]{1,0:T(8,128)(2,1)} %bitcast.14), custom_call_target="tpu_custom_call" | custom-call | bytes 15597568 | tf_op jit(solution)/shard_map/pallas_call | solution.py:61
  58.4 0.8 collective-permute-done.14.refs_7_
  59.2 1.2 shard_map.117
  60.4 4.3 %shard_map.118 = (bf16[2,48,1920]{2,1,0:T(8,128)(2,1)S(1)}, bf16[2,48,1920]{2,1,0:T(8,128)(2,1)S(1)}, bf16[2,48,1920]{2,1,0:T(8,128)(2,1)S(1)}, bf16[2,48,1920]{2,1,0:T(8,128)(2,1)S(1)}) custom-call(bf16[2048,192]{1,0:T(8,128)(2,1)S(1)} %get-tuple-element.99.scaled_ref, bf16[1792,2048]{1,0:T(8,128)(2,1)S(1)} %get-tuple-element.92.gate_ref, ...), custom_call_target="tpu_custom_call" | custom-call | flops 2818572288 | bytes 14680064 | tf_op jit(solution)/shard_map/pallas_call | solution.py:358
  64.8 1.7 %collective-permute-done.16 = bf16[2,48,1920]{2,1,0:T(8,128)(2,1)S(1)} collective-permute-done((bf16[2,48,1920]{2,1,0:T(8,128)(2,1)S(1)}, bf16[2,48,1920]{2,1,0:T(8,128)(2,1)S(1)}, u32[]{:S(2)}, u32[]{:S(2)}) %collective-permute-start.16) | collective-permute-done | bytes 368672 | tf_op jit(solution)/shard_map/ppermute | solution.py:495
  66.6 1.6 %collective-permute-start.18 = (bf16[2,48,1920]{2,1,0:T(8,128)(2,1)S(1)}, bf16[2,48,1920]{2,1,0:T(8,128)(2,1)S(1)}, u32[]{:S(2)}, u32[]{:S(2)}) collective-permute-start(bf16[2,48,1920]{2,1,0:T(8,128)(2,1)S(1)} %add_convert_fusion.1), channel_id=1, source_target_pairs={{0,2},{1,3},{2,0},{3,1},{4,6},{5,7},{6,4},{7,5},{8,10},{9,11},{10,... | collective-permute-start | bytes 1105928 | tf_op jit(solution)/shard_map/ppermute | solution.py:499
  68.1 4.6 %shard_map.119 = (bf16[2,48,1904]{2,1,0:T(8,128)(2,1)S(1)}, bf16[2,48,1904]{2,1,0:T(8,128)(2,1)S(1)}, bf16[2,48,1904]{2,1,0:T(8,128)(2,1)S(1)}, bf16[2,48,1904]{2,1,0:T(8,128)(2,1)S(1)}) custom-call(bf16[2048,192]{1,0:T(8,128)(2,1)S(1)} %get-tuple-element.99.scaled_ref, bf16[1904,2048]{1,0:T(8,128)(2,1)S(1)} %get-tuple-element.100.gate_ref, ...), custom_call_target="tpu_custom_call" | custom-call | flops 2994733056 | bytes 15597568 | tf_op jit(solution)/shard_map/pallas_call | solution.py:358
  73.4 1.1 collective-permute-done.17
  74.5 2.8 %collective-permute-done.18.crossed_ref = bf16[2,48,1920]{2,1,0:T(8,128)(2,1)S(1)} collective-permute-done((bf16[2,48,1920]{2,1,0:T(8,128)(2,1)S(1)}, bf16[2,48,1920]{2,1,0:T(8,128)(2,1)S(1)}, u32[]{:S(2)}, u32[]{:S(2)}) %collective-permute-start.18) | collective-permute-done | bytes 368672 | tf_op jit(solution)/shard_map/ppermute | solution.py:499
  77.4 1.6 %collective-permute-start.21 = (bf16[2,48,1904]{2,1,0:T(8,128)(2,1)S(1)}, bf16[2,48,1904]{2,1,0:T(8,128)(2,1)S(1)}, u32[]{:S(2)}, u32[]{:S(2)}) collective-permute-start(bf16[2,48,1904]{2,1,0:T(8,128)(2,1)S(1)} %add_convert_fusion), channel_id=1, source_target_pairs={{0,2},{1,3},{2,0},{3,1},{4,6},{5,7},{6,4},{7,5},{8,10},{9,11},{10,... | collective-permute-start | bytes 1096712 | tf_op jit(solution)/shard_map/ppermute | solution.py:499
  78.9 5.3 %shard_map.120 = (bf16[1792,2048]{1,0:T(8,128)(2,1)S(1)}, bf16[1904,2048]{1,0:T(8,128)(2,1)S(1)}, f32[8,128]{1,0:T(8,128)S(1)}) custom-call(bf16[3696,2048]{1,0:T(8,128)(2,1)} %refs_1_, bf16[3696,2048]{1,0:T(8,128)(2,1)} %refs_1_), custom_call_target="tpu_custom_call" | custom-call | bytes 30277632 | tf_op jit(solution)/shard_map/pallas_call | solution.py:61
  85.2 2.9 %collective-permute-done.21.crossed_ref = bf16[2,48,1904]{2,1,0:T(8,128)(2,1)S(1)} collective-permute-done((bf16[2,48,1904]{2,1,0:T(8,128)(2,1)S(1)}, bf16[2,48,1904]{2,1,0:T(8,128)(2,1)S(1)}, u32[]{:S(2)}, u32[]{:S(2)}) %collective-permute-start.21) | collective-permute-done | bytes 365600 | tf_op jit(solution)/shard_map/ppermute | solution.py:499
  88.4 2.5 %collective-permute-done.19.refs_1_ = bf16[48,1792]{1,0:T(8,128)(2,1)S(1)} collective-permute-done((bf16[48,1792]{1,0:T(8,128)(2,1)S(1)}, bf16[48,1792]{1,0:T(8,128)(2,1)S(1)}, u32[]{:S(2)}, u32[]{:S(2)}) %collective-permute-start.19) | collective-permute-done | bytes 172064 | tf_op jit(solution)/shard_map/ppermute | solution.py:499
  90.9 1.5 %collective-permute-start.22 = (bf16[48,1904]{1,0:T(8,128)(2,1)S(1)}, bf16[48,1904]{1,0:T(8,128)(2,1)S(1)}, u32[]{:S(2)}, u32[]{:S(2)}) collective-permute-start(bf16[48,1904]{1,0:T(8,128)(2,1)S(1)} %shard_map.122.refs_0_), channel_id=1, source_target_pairs={{0,2},{1,3},{2,0},{3,1},{4,6},{5,7},{6,4},{7,5},{8,10},{9,11},{10,... | collective-permute-start | bytes 548360 | tf_op jit(solution)/shard_map/ppermute | solution.py:499
  92.7 2.2 %shard_map.123.refs_5_ = f32[4,48,2048]{2,1,0:T(8,128)S(1)} custom-call(s32[6]{0:T(128)S(1)} %stack.27.scalars, bf16[48,1792]{1,0:T(8,128)(2,1)S(1)} %get-tuple-element.110.rest_1_.refs_0_, bf16[48,1792]{1,0:T(8,128)(2,1)S(1)} %collective-permute-done.19.refs_1_, bf16[48,1792]{1,0:T(8,128)(2,1)S(1)} %collective-permute-done.23.refs_2_, ...), custom_call_target="tpu_custom_call" | custom-call | flops 1409286144 | bytes 7340032 | tf_op jit(solution)/shard_map/pallas_call | solution.py:476
  94.9 3.1 %collective-permute-done.22.refs_1_ = bf16[48,1904]{1,0:T(8,128)(2,1)S(1)} collective-permute-done((bf16[48,1904]{1,0:T(8,128)(2,1)S(1)}, bf16[48,1904]{1,0:T(8,128)(2,1)S(1)}, u32[]{:S(2)}, u32[]{:S(2)}) %collective-permute-start.22) | collective-permute-done | bytes 182816 | tf_op jit(solution)/shard_map/ppermute | solution.py:499
  98.0 1.4 %collective-permute-done.26.refs_3_ = bf16[48,1904]{1,0:T(8,128)(2,1)S(1)} collective-permute-done((bf16[48,1904]{1,0:T(8,128)(2,1)S(1)}, bf16[48,1904]{1,0:T(8,128)(2,1)S(1)}, u32[]{:S(2)}, u32[]{:S(2)}) %collective-permute-start.26) | collective-permute-done | bytes 182816 | tf_op jit(solution)/shard_map/ppermute | solution.py:495
  99.4 2.5 %shard_map.124 = (f32[24,2048]{1,0:T(8,128)S(1)}, bf16[24,2048]{1,0:T(8,128)(2,1)S(1)}, f32[24,2048]{1,0:T(8,128)S(1)}, bf16[24,2048]{1,0:T(8,128)(2,1)S(1)}, f3...) custom-call(s32[6]{0:T(128)S(1)} %stack.27.scalars, ...), custom_call_target="tpu_custom_call" | custom-call | flops 1497366528 | bytes 7798784 | tf_op jit(solution)/shard_map/pallas_call | solution.py:476
  101.9 0.8 collective-permute-start.27
  102.6 1.3 %collective-permute-start.29 = (bf16[24,2048]{1,0:T(8,128)(2,1)S(1)}, bf16[24,2048]{1,0:T(8,128)(2,1)S(1)}, u32[]{:S(2)}, u32[]{:S(2)}) collective-permute-start(bf16[24,2048]{1,0:T(8,128)(2,1)S(1)} %get-tuple-element.124), channel_id=1, source_target_pairs={{0,16},{16,0},{1,17},{17,1},{2,18},{18,2},{3,19},{19,3},{4,20},{20... | collective-permute-start | bytes 294920 | tf_op jit(solution)/shard_map/ppermute | solution.py:507
  104.0 0.7 collective-permute-start.31
  104.7 1.3 %collective-permute-start.33 = (bf16[24,2048]{1,0:T(8,128)(2,1)S(1)}, bf16[24,2048]{1,0:T(8,128)(2,1)S(1)}, u32[]{:S(2)}, u32[]{:S(2)}) collective-permute-start(bf16[24,2048]{1,0:T(8,128)(2,1)S(1)} %get-tuple-element.128), channel_id=1, source_target_pairs={{0,16},{16,0},{1,17},{17,1},{2,18},{18,2},{3,19},{19,3},{4,20},{20... | collective-permute-start | bytes 294920 | tf_op jit(solution)/shard_map/ppermute | solution.py:507
  106.0 1.6 %collective-permute-done.27 = bf16[24,2048]{1,0:T(8,128)(2,1)S(1)} collective-permute-done((bf16[24,2048]{1,0:T(8,128)(2,1)S(1)}, bf16[24,2048]{1,0:T(8,128)(2,1)S(1)}, u32[]{:S(2)}, u32[]{:S(2)}) %collective-permute-start.27) | collective-permute-done | bytes 98336 | tf_op jit(solution)/shard_map/ppermute | solution.py:507
  107.6 1.0 collective-permute-start.28
  108.6 1.1 collective-permute-done.29
  109.7 2.3 %collective-permute-start.30 = (bf16[24,2048]{1,0:T(8,128)(2,1)S(1)}, bf16[24,2048]{1,0:T(8,128)(2,1)S(1)}, u32[]{:S(2)}, u32[]{:S(2)}) collective-permute-start(bf16[24,2048]{1,0:T(8,128)(2,1)S(1)} %add_convert_fusion.3), channel_id=1, source_target_pairs={{0,12},{4,8},{8,4},{12,0},{1,13},{5,9},{9,5},{13,1},{2,14},{6,10},... | collective-permute-start | bytes 294920 | tf_op jit(solution)/shard_map/ppermute | solution.py:503
  112.1 1.0 collective-permute-done.33
  113.1 3.7 %collective-permute-done.28 = bf16[24,2048]{1,0:T(8,128)(2,1)S(1)} collective-permute-done((bf16[24,2048]{1,0:T(8,128)(2,1)S(1)}, bf16[24,2048]{1,0:T(8,128)(2,1)S(1)}, u32[]{:S(2)}, u32[]{:S(2)}) %collective-permute-start.28) | collective-permute-done | bytes 98336 | tf_op jit(solution)/shard_map/ppermute | solution.py:503
  116.8 1.3 %collective-permute-done.32 = bf16[24,2048]{1,0:T(8,128)(2,1)S(1)} collective-permute-done((bf16[24,2048]{1,0:T(8,128)(2,1)S(1)}, bf16[24,2048]{1,0:T(8,128)(2,1)S(1)}, u32[]{:S(2)}, u32[]{:S(2)}) %collective-permute-start.32) | collective-permute-done | bytes 98336 | tf_op jit(solution)/shard_map/ppermute | solution.py:503
  118.2 0.7 select_convert_fusion
  (49 shorter events, 5.7 us)
Async XLA Ops:
  12.7 1.7 %collective-permute-start = (bf16[96,1024]{1,0:T(8,128)(2,1)S(1)}, bf16[96,1024]{1,0:T(8,128)(2,1)S(1)}, u32[]{:S(2)}, u32[]{:S(2)}) collective-permute-start(bf16[96,1024]{1,0:T(8,128)(2,1)S(1)} %get-tuple-element.68), channel_id=1, source_target_pairs={{0,1},{1,0},{2,3},{3,2},{4,5},{5,4},{6,7},{7,6},{8,9},{9,8},{10,11... | collective-permute-start | bytes 589832 | tf_op jit(solution)/shard_map/ppermute | solution.py:495
  13.2 1.2 collective-permute-start.1
  14.8 8.2 %collective-permute-start.2 = (bf16[96,1024]{1,0:T(8,128)(2,1)S(1)}, bf16[96,1024]{1,0:T(8,128)(2,1)S(1)}, u32[]{:S(2)}, u32[]{:S(2)}) collective-permute-start(bf16[96,1024]{1,0:T(8,128)(2,1)S(1)} %get-tuple-element.72.a_ref), channel_id=1, source_target_pairs={{0,2},{1,3},{2,0},{3,1},{4,6},{5,7},{6,4},{7,5},{8,10},{9,11},{10,... | collective-permute-start | bytes 589832 | tf_op jit(solution)/shard_map/ppermute | solution.py:499
  17.6 5.4 %collective-permute-start.3 = (f32[8,128]{1,0:T(8,128)S(1)}, f32[8,128]{1,0:T(8,128)S(1)}, u32[]{:S(2)}, u32[]{:S(2)}) collective-permute-start(f32[8,128]{1,0:T(8,128)S(1)} %get-tuple-element.73.lse_a_ref), channel_id=1, source_target_pairs={{0,2},{1,3},{2,0},{3,1},{4,6},{5,7},{6,4},{7,5},{8,10},{9,11},{10,... | collective-permute-start | bytes 12296 | tf_op jit(solution)/shard_map/ppermute | solution.py:499
  23.4 1.5 %collective-permute-start.4 = (bf16[96,1024]{1,0:T(8,128)(2,1)S(1)}, bf16[96,1024]{1,0:T(8,128)(2,1)S(1)}, u32[]{:S(2)}, u32[]{:S(2)}) collective-permute-start(bf16[96,1024]{1,0:T(8,128)(2,1)S(1)} %shard_map.112.keep_ref), channel_id=1, source_target_pairs={{0,1},{1,0},{2,3},{3,2},{4,5},{5,4},{6,7},{7,6},{8,9},{9,8},{10,11... | collective-permute-start | bytes 589832 | tf_op jit(solution)/shard_map/ppermute | solution.py:495
  27.4 11.9 %collective-permute-start.5 = (bf16[24,2048]{1,0:T(8,128)(2,1)S(1)}, bf16[24,2048]{1,0:T(8,128)(2,1)S(1)}, u32[]{:S(2)}, u32[]{:S(2)}) collective-permute-start(bf16[24,2048]{1,0:T(8,128)(2,1)S(1)} %get-tuple-element.79), channel_id=1, source_target_pairs={{0,4},{4,0},{8,12},{12,8},{1,5},{5,1},{9,13},{13,9},{2,6},{6,2},{1... | collective-permute-start | bytes 294920 | tf_op jit(solution)/shard_map/ppermute | solution.py:503
  29.3 10.0 %collective-permute-start.6 = (bf16[24,2048]{1,0:T(8,128)(2,1)S(1)}, bf16[24,2048]{1,0:T(8,128)(2,1)S(1)}, u32[]{:S(2)}, u32[]{:S(2)}) collective-permute-start(bf16[24,2048]{1,0:T(8,128)(2,1)S(1)} %get-tuple-element.80), channel_id=1, source_target_pairs={{0,12},{4,8},{8,4},{12,0},{1,13},{5,9},{9,5},{13,1},{2,14},{6,10},... | collective-permute-start | bytes 294920 | tf_op jit(solution)/shard_map/ppermute | solution.py:503
  31.8 9.2 %copy-start = (bf16[96,2048]{1,0:T(8,128)(2,1)S(1)}, bf16[96,2048]{1,0:T(8,128)(2,1)}, u32[]{:S(2)}) copy-start(bf16[96,2048]{1,0:T(8,128)(2,1)} %resid_ref.1) | copy-start | bytes 1179652
  31.8 23.3 %copy-start.1 = (bf16[2048]{0:T(1024)(128)(2,1)S(1)}, bf16[2048]{0:T(1024)(128)(2,1)}, u32[]{:S(2)}) copy-start(bf16[2048]{0:T(1024)(128)(2,1)} %param.18) | copy-start | bytes 12292
  31.8 9.2 %collective-permute-start.7 = (bf16[24,2048]{1,0:T(8,128)(2,1)S(1)}, bf16[24,2048]{1,0:T(8,128)(2,1)S(1)}, u32[]{:S(2)}, u32[]{:S(2)}) collective-permute-start(bf16[24,2048]{1,0:T(8,128)(2,1)S(1)} %get-tuple-element.81), channel_id=1, source_target_pairs={{0,8},{4,12},{8,0},{12,4},{1,9},{5,13},{9,1},{13,5},{2,10},{6,14},... | collective-permute-start | bytes 294920 | tf_op jit(solution)/shard_map/ppermute | solution.py:503
  41.7 4.8 %collective-permute-start.9 = (bf16[24,2048]{1,0:T(8,128)(2,1)S(1)}, bf16[24,2048]{1,0:T(8,128)(2,1)S(1)}, u32[]{:S(2)}, u32[]{:S(2)}) collective-permute-start(bf16[24,2048]{1,0:T(8,128)(2,1)S(1)} %shard_map.115.refs_0_), channel_id=1, source_target_pairs={{0,16},{16,0},{1,17},{17,1},{2,18},{18,2},{3,19},{19,3},{4,20},{20... | collective-permute-start | bytes 294920 | tf_op jit(solution)/shard_map/ppermute | solution.py:507
  43.3 6.7 %collective-permute-start.8 = (bf16[24,2048]{1,0:T(8,128)(2,1)S(1)}, bf16[24,2048]{1,0:T(8,128)(2,1)S(1)}, u32[]{:S(2)}, u32[]{:S(2)}) collective-permute-start(bf16[24,2048]{1,0:T(8,128)(2,1)S(1)} %shard_map.115.refs_0_), channel_id=1, source_target_pairs={{0,8},{4,12},{8,0},{12,4},{1,9},{5,13},{9,1},{13,5},{2,10},{6,14},... | collective-permute-start | bytes 294920 | tf_op jit(solution)/shard_map/ppermute | solution.py:503
  44.5 6.3 %collective-permute-start.10 = (bf16[24,2048]{1,0:T(8,128)(2,1)S(1)}, bf16[24,2048]{1,0:T(8,128)(2,1)S(1)}, u32[]{:S(2)}, u32[]{:S(2)}) collective-permute-start(bf16[24,2048]{1,0:T(8,128)(2,1)S(1)} %shard_map.115.refs_0_), channel_id=1, source_target_pairs={{0,4},{4,0},{8,12},{12,8},{1,5},{5,1},{9,13},{13,9},{2,6},{6,2},{1... | collective-permute-start | bytes 294920 | tf_op jit(solution)/shard_map/ppermute | solution.py:503
  50.0 4.6 %collective-permute-start.13 = (bf16[24,2048]{1,0:T(8,128)(2,1)S(1)}, bf16[24,2048]{1,0:T(8,128)(2,1)S(1)}, u32[]{:S(2)}, u32[]{:S(2)}) collective-permute-start(bf16[24,2048]{1,0:T(8,128)(2,1)S(1)} %collective-permute-done.8.refs_4_), channel_id=1, source_target_pairs={{0,4},{4,0},{8,12},{12,8},{1,5},{5,1},{9,13},{13,9},{2,6},{6,2},{1... | collective-permute-start | bytes 294920 | tf_op jit(solution)/shard_map/ppermute | solution.py:503
  50.3 8.1 %collective-permute-start.12 = (bf16[24,2048]{1,0:T(8,128)(2,1)S(1)}, bf16[24,2048]{1,0:T(8,128)(2,1)S(1)}, u32[]{:S(2)}, u32[]{:S(2)}) collective-permute-start(bf16[24,2048]{1,0:T(8,128)(2,1)S(1)} %collective-permute-done.8.refs_4_), channel_id=1, source_target_pairs={{0,16},{16,0},{1,17},{17,1},{2,18},{18,2},{3,19},{19,3},{4,20},{20... | collective-permute-start | bytes 294920 | tf_op jit(solution)/shard_map/ppermute | solution.py:507
  50.8 7.6 %collective-permute-start.11 = (bf16[24,2048]{1,0:T(8,128)(2,1)S(1)}, bf16[24,2048]{1,0:T(8,128)(2,1)S(1)}, u32[]{:S(2)}, u32[]{:S(2)}) collective-permute-start(bf16[24,2048]{1,0:T(8,128)(2,1)S(1)} %collective-permute-done.10.refs_2_), channel_id=1, source_target_pairs={{0,16},{16,0},{1,17},{17,1},{2,18},{18,2},{3,19},{19,3},{4,20},{20... | collective-permute-start | bytes 294920 | tf_op jit(solution)/shard_map/ppermute | solution.py:507
  54.6 4.6 %collective-permute-start.14 = (bf16[24,2048]{1,0:T(8,128)(2,1)S(1)}, bf16[24,2048]{1,0:T(8,128)(2,1)S(1)}, u32[]{:S(2)}, u32[]{:S(2)}) collective-permute-start(bf16[24,2048]{1,0:T(8,128)(2,1)S(1)} %collective-permute-done.13.refs_6_), channel_id=1, source_target_pairs={{0,16},{16,0},{1,17},{17,1},{2,18},{18,2},{3,19},{19,3},{4,20},{20... | collective-permute-start | bytes 294920 | tf_op jit(solution)/shard_map/ppermute | solution.py:507
  64.7 1.8 %collective-permute-start.16 = (bf16[2,48,1920]{2,1,0:T(8,128)(2,1)S(1)}, bf16[2,48,1920]{2,1,0:T(8,128)(2,1)S(1)}, u32[]{:S(2)}, u32[]{:S(2)}) collective-permute-start(bf16[2,48,1920]{2,1,0:T(8,128)(2,1)S(1)} %get-tuple-element.98), channel_id=1, source_target_pairs={{0,1},{1,0},{2,3},{3,2},{4,5},{5,4},{6,7},{7,6},{8,9},{9,8},{10,11... | collective-permute-start | bytes 1105928 | tf_op jit(solution)/shard_map/ppermute | solution.py:495
  66.6 10.7 %collective-permute-start.18 = (bf16[2,48,1920]{2,1,0:T(8,128)(2,1)S(1)}, bf16[2,48,1920]{2,1,0:T(8,128)(2,1)S(1)}, u32[]{:S(2)}, u32[]{:S(2)}) collective-permute-start(bf16[2,48,1920]{2,1,0:T(8,128)(2,1)S(1)} %add_convert_fusion.1), channel_id=1, source_target_pairs={{0,2},{1,3},{2,0},{3,1},{4,6},{5,7},{6,4},{7,5},{8,10},{9,11},{10,... | collective-permute-start | bytes 1105928 | tf_op jit(solution)/shard_map/ppermute | solution.py:499
  72.7 1.8 %collective-permute-start.17 = (bf16[2,48,1904]{2,1,0:T(8,128)(2,1)S(1)}, bf16[2,48,1904]{2,1,0:T(8,128)(2,1)S(1)}, u32[]{:S(2)}, u32[]{:S(2)}) collective-permute-start(bf16[2,48,1904]{2,1,0:T(8,128)(2,1)S(1)} %get-tuple-element.102), channel_id=1, source_target_pairs={{0,1},{1,0},{2,3},{3,2},{4,5},{5,4},{6,7},{7,6},{8,9},{9,8},{10,11... | collective-permute-start | bytes 1096712 | tf_op jit(solution)/shard_map/ppermute | solution.py:495
  72.8 11.5 %collective-permute-start.15 = (bf16[2,48,1920]{2,1,0:T(8,128)(2,1)S(1)}, bf16[2,48,1920]{2,1,0:T(8,128)(2,1)S(1)}, u32[]{:S(2)}, u32[]{:S(2)}) collective-permute-start(bf16[2,48,1920]{2,1,0:T(8,128)(2,1)S(1)} %get-tuple-element.96), channel_id=1, source_target_pairs={{0,1},{1,0},{2,3},{3,2},{4,5},{5,4},{6,7},{7,6},{8,9},{9,8},{10,11... | collective-permute-start | bytes 1105928 | tf_op jit(solution)/shard_map/ppermute | solution.py:495
  73.3 11.9 %collective-permute-start.20 = (bf16[2,48,1904]{2,1,0:T(8,128)(2,1)S(1)}, bf16[2,48,1904]{2,1,0:T(8,128)(2,1)S(1)}, u32[]{:S(2)}, u32[]{:S(2)}) collective-permute-start(bf16[2,48,1904]{2,1,0:T(8,128)(2,1)S(1)} %get-tuple-element.112), channel_id=1, source_target_pairs={{0,1},{1,0},{2,3},{3,2},{4,5},{5,4},{6,7},{7,6},{8,9},{9,8},{10,11... | collective-permute-start | bytes 1096712 | tf_op jit(solution)/shard_map/ppermute | solution.py:495
  77.4 10.8 %collective-permute-start.21 = (bf16[2,48,1904]{2,1,0:T(8,128)(2,1)S(1)}, bf16[2,48,1904]{2,1,0:T(8,128)(2,1)S(1)}, u32[]{:S(2)}, u32[]{:S(2)}) collective-permute-start(bf16[2,48,1904]{2,1,0:T(8,128)(2,1)S(1)} %add_convert_fusion), channel_id=1, source_target_pairs={{0,2},{1,3},{2,0},{3,1},{4,6},{5,7},{6,4},{7,5},{8,10},{9,11},{10,... | collective-permute-start | bytes 1096712 | tf_op jit(solution)/shard_map/ppermute | solution.py:499
  84.6 6.3 %collective-permute-start.19 = (bf16[48,1792]{1,0:T(8,128)(2,1)S(1)}, bf16[48,1792]{1,0:T(8,128)(2,1)S(1)}, u32[]{:S(2)}, u32[]{:S(2)}) collective-permute-start(bf16[48,1792]{1,0:T(8,128)(2,1)S(1)} %get-tuple-element.110.rest_1_.refs_0_), channel_id=1, source_target_pairs={{0,2},{1,3},{2,0},{3,1},{4,6},{5,7},{6,4},{7,5},{8,10},{9,11},{10,... | collective-permute-start | bytes 516104 | tf_op jit(solution)/shard_map/ppermute | solution.py:499
  85.2 7.5 %collective-permute-start.23 = (bf16[48,1792]{1,0:T(8,128)(2,1)S(1)}, bf16[48,1792]{1,0:T(8,128)(2,1)S(1)}, u32[]{:S(2)}, u32[]{:S(2)}) collective-permute-start(bf16[48,1792]{1,0:T(8,128)(2,1)S(1)} %get-tuple-element.110.rest_1_.refs_0_), channel_id=1, source_target_pairs={{0,1},{1,0},{2,3},{3,2},{4,5},{5,4},{6,7},{7,6},{8,9},{9,8},{10,11... | collective-permute-start | bytes 516104 | tf_op jit(solution)/shard_map/ppermute | solution.py:495
  90.9 1.7 %collective-permute-start.24 = (bf16[48,1792]{1,0:T(8,128)(2,1)S(1)}, bf16[48,1792]{1,0:T(8,128)(2,1)S(1)}, u32[]{:S(2)}, u32[]{:S(2)}) collective-permute-start(bf16[48,1792]{1,0:T(8,128)(2,1)S(1)} %collective-permute-done.19.refs_1_), channel_id=1, source_target_pairs={{0,1},{1,0},{2,3},{3,2},{4,5},{5,4},{6,7},{7,6},{8,9},{9,8},{10,11... | collective-permute-start | bytes 516104 | tf_op jit(solution)/shard_map/ppermute | solution.py:495
  90.9 7.1 %collective-permute-start.22 = (bf16[48,1904]{1,0:T(8,128)(2,1)S(1)}, bf16[48,1904]{1,0:T(8,128)(2,1)S(1)}, u32[]{:S(2)}, u32[]{:S(2)}) collective-permute-start(bf16[48,1904]{1,0:T(8,128)(2,1)S(1)} %shard_map.122.refs_0_), channel_id=1, source_target_pairs={{0,2},{1,3},{2,0},{3,1},{4,6},{5,7},{6,4},{7,5},{8,10},{9,11},{10,... | collective-permute-start | bytes 548360 | tf_op jit(solution)/shard_map/ppermute | solution.py:499
  92.4 5.6 %collective-permute-start.25 = (bf16[48,1904]{1,0:T(8,128)(2,1)S(1)}, bf16[48,1904]{1,0:T(8,128)(2,1)S(1)}, u32[]{:S(2)}, u32[]{:S(2)}) collective-permute-start(bf16[48,1904]{1,0:T(8,128)(2,1)S(1)} %shard_map.122.refs_0_), channel_id=1, source_target_pairs={{0,1},{1,0},{2,3},{3,2},{4,5},{5,4},{6,7},{7,6},{8,9},{9,8},{10,11... | collective-permute-start | bytes 548360 | tf_op jit(solution)/shard_map/ppermute | solution.py:495
  98.0 1.4 %collective-permute-start.26 = (bf16[48,1904]{1,0:T(8,128)(2,1)S(1)}, bf16[48,1904]{1,0:T(8,128)(2,1)S(1)}, u32[]{:S(2)}, u32[]{:S(2)}) collective-permute-start(bf16[48,1904]{1,0:T(8,128)(2,1)S(1)} %collective-permute-done.22.refs_1_), channel_id=1, source_target_pairs={{0,1},{1,0},{2,3},{3,2},{4,5},{5,4},{6,7},{7,6},{8,9},{9,8},{10,11... | collective-permute-start | bytes 548360 | tf_op jit(solution)/shard_map/ppermute | solution.py:495
  101.9 5.7 %collective-permute-start.27 = (bf16[24,2048]{1,0:T(8,128)(2,1)S(1)}, bf16[24,2048]{1,0:T(8,128)(2,1)S(1)}, u32[]{:S(2)}, u32[]{:S(2)}) collective-permute-start(bf16[24,2048]{1,0:T(8,128)(2,1)S(1)} %get-tuple-element.122), channel_id=1, source_target_pairs={{0,16},{16,0},{1,17},{17,1},{2,18},{18,2},{3,19},{19,3},{4,20},{20... | collective-permute-start | bytes 294920 | tf_op jit(solution)/shard_map/ppermute | solution.py:507
  102.6 7.1 %collective-permute-start.29 = (bf16[24,2048]{1,0:T(8,128)(2,1)S(1)}, bf16[24,2048]{1,0:T(8,128)(2,1)S(1)}, u32[]{:S(2)}, u32[]{:S(2)}) collective-permute-start(bf16[24,2048]{1,0:T(8,128)(2,1)S(1)} %get-tuple-element.124), channel_id=1, source_target_pairs={{0,16},{16,0},{1,17},{17,1},{2,18},{18,2},{3,19},{19,3},{4,20},{20... | collective-permute-start | bytes 294920 | tf_op jit(solution)/shard_map/ppermute | solution.py:507
  104.0 8.0 %collective-permute-start.31 = (bf16[24,2048]{1,0:T(8,128)(2,1)S(1)}, bf16[24,2048]{1,0:T(8,128)(2,1)S(1)}, u32[]{:S(2)}, u32[]{:S(2)}) collective-permute-start(bf16[24,2048]{1,0:T(8,128)(2,1)S(1)} %get-tuple-element.126), channel_id=1, source_target_pairs={{0,16},{16,0},{1,17},{17,1},{2,18},{18,2},{3,19},{19,3},{4,20},{20... | collective-permute-start | bytes 294920 | tf_op jit(solution)/shard_map/ppermute | solution.py:507
  104.7 8.4 %collective-permute-start.33 = (bf16[24,2048]{1,0:T(8,128)(2,1)S(1)}, bf16[24,2048]{1,0:T(8,128)(2,1)S(1)}, u32[]{:S(2)}, u32[]{:S(2)}) collective-permute-start(bf16[24,2048]{1,0:T(8,128)(2,1)S(1)} %get-tuple-element.128), channel_id=1, source_target_pairs={{0,16},{16,0},{1,17},{17,1},{2,18},{18,2},{3,19},{19,3},{4,20},{20... | collective-permute-start | bytes 294920 | tf_op jit(solution)/shard_map/ppermute | solution.py:507
  107.6 9.2 %collective-permute-start.28 = (bf16[24,2048]{1,0:T(8,128)(2,1)S(1)}, bf16[24,2048]{1,0:T(8,128)(2,1)S(1)}, u32[]{:S(2)}, u32[]{:S(2)}) collective-permute-start(bf16[24,2048]{1,0:T(8,128)(2,1)S(1)} %add_convert_fusion.4), channel_id=1, source_target_pairs={{0,8},{4,12},{8,0},{12,4},{1,9},{5,13},{9,1},{13,5},{2,10},{6,14},... | collective-permute-start | bytes 294920 | tf_op jit(solution)/shard_map/ppermute | solution.py:503
  109.7 7.1 %collective-permute-start.30 = (bf16[24,2048]{1,0:T(8,128)(2,1)S(1)}, bf16[24,2048]{1,0:T(8,128)(2,1)S(1)}, u32[]{:S(2)}, u32[]{:S(2)}) collective-permute-start(bf16[24,2048]{1,0:T(8,128)(2,1)S(1)} %add_convert_fusion.3), channel_id=1, source_target_pairs={{0,12},{4,8},{8,4},{12,0},{1,13},{5,9},{9,5},{13,1},{2,14},{6,10},... | collective-permute-start | bytes 294920 | tf_op jit(solution)/shard_map/ppermute | solution.py:503
  112.0 6.1 %collective-permute-start.32 = (bf16[24,2048]{1,0:T(8,128)(2,1)S(1)}, bf16[24,2048]{1,0:T(8,128)(2,1)S(1)}, u32[]{:S(2)}, u32[]{:S(2)}) collective-permute-start(bf16[24,2048]{1,0:T(8,128)(2,1)S(1)} %add_convert_fusion.2), channel_id=1, source_target_pairs={{0,4},{4,0},{8,12},{12,8},{1,5},{5,1},{9,13},{13,9},{2,6},{6,2},{1... | collective-permute-start | bytes 294920 | tf_op jit(solution)/shard_map/ppermute | solution.py:503
